TPU v7x, 128 devices: a whole 4x4x4 slice. The times are simulated.
128 devices in a mesh: gy: 8 (over x, core), gz: 16 (over z, y).
Axes of the slice: x: 4, y: 4, z: 4, core: 2. Of those that a mesh axis runs over, the one named last changes fastest.
Arguments:
- features: bfloat16 [64, 64, 32, 512], P('gy', 'gz'), may hold values from -6 to 6
- cotangent: bfloat16 [64, 64, 32, 512], P('gy', 'gz'), may hold values from -6 to 6
- spectral_weight: bfloat16 [32, 32, 65536], P('gz', None, 'gy'), may hold values from -6 to 6
- kernel_weight: bfloat16 [3, 3, 32, 96], replicated, may hold values from -0.21875 to 0.21875
- channel_bias: float32 [32], replicated, may hold values from -4 to 4
Outputs:
- grad_field: bfloat16 [64, 64, 32, 512], P('gy', 'gz')
- grad_spectral: float32 [32, 32, 65536], P('gz', None, 'gy')
- grad_kernel: float32 [3, 3, 32, 96], replicated
- grad_bias: float32 [32], replicated
All inputs are finite; a program needn't handle non-finite values.
Results may differ from a plain program's by a relative error of at most 0.0075.
Values may be sent and summed in bfloat16 or wider, within the bound.
No kernel may reach another device: no remote copies, remote signals or barrier semaphores. Data moves between devices by JAX's collectives and lax.ppermute only.
A program may use at most 192 MiB of HBM per device.

v0:
```python
import math

import jax
import jax.numpy as jnp
from jax import lax
from jax.sharding import PartitionSpec as P

MX = 32
MY = 32
MZ = 32


def with_halo(cells, sides, width):
    for axis, dim in sides:
        count = lax.axis_size(axis)
        ends = count - 1
        head = lax.slice_in_dim(cells, 0, width, axis=dim)
        tail = lax.slice_in_dim(cells, cells.shape[dim] - width, cells.shape[dim], axis=dim)
        cells = jnp.concatenate(
            [
                lax.ppermute(tail, axis, [(i, (i + 1) % count) for i in range(ends)]),
                cells,
                lax.ppermute(head, axis, [((i + 1) % count, i) for i in range(ends)]),
            ],
            axis=dim,
        )
    return cells


def mode_freqs(positions, modes_kept, length):
    return jnp.where(positions < modes_kept // 2, positions, length - modes_kept + positions)


def phase_table(out_places, sum_places, length, rotation):
    products = out_places[:, None] * sum_places[None, :] % length
    angles = 2.0 * math.pi / length * products.astype(jnp.float32)
    cosine = jnp.cos(angles)
    sine_part = rotation * jnp.sin(angles)
    row_real = jnp.stack([cosine, -sine_part], axis=-1)
    row_imag = jnp.stack([sine_part, cosine], axis=-1)
    return jnp.stack([row_real, row_imag], axis=1)


def grid_table(length, modes_kept):
    places = jnp.arange(length, dtype=jnp.int32)
    frequency = jnp.arange(modes_kept, dtype=jnp.int32)
    products = places[:, None] * frequency[None, :] % length
    angles = 2.0 * math.pi / length * products.astype(jnp.float32)
    return jnp.stack([jnp.cos(angles), -jnp.sin(angles)], axis=-1)


def line_forward(block, modes_kept, norm_scale):
    rows_here, depth_here, channels, length = block.shape
    lookup = grid_table(length, modes_kept).reshape(length, 2 * modes_kept).astype(jnp.bfloat16)
    projected = jnp.dot(block.reshape(-1, length), lookup, preferred_element_type=jnp.float32)
    projected = projected.reshape(rows_here, depth_here, channels, modes_kept, 2).transpose(
        0, 1, 3, 4, 2
    )
    return (norm_scale * projected).reshape(rows_here, depth_here, modes_kept * 2 * channels)


def line_inverse(spectrum, channels, length, norm_scale):
    rows_here, depth_here, merged = spectrum.shape
    modes_kept = merged // (2 * channels)
    lookup = grid_table(length, modes_kept).transpose(1, 2, 0)
    pieces = spectrum.reshape(rows_here, depth_here, modes_kept, 2, channels)
    return norm_scale * jnp.einsum(
        "yzmpc,mpx->yzcx", pieces, lookup, precision=lax.Precision.HIGHEST
    )


def along_first(lookup, values, channels):
    first_len, second_len, merged = values.shape
    pieces = values.reshape(first_len, second_len, merged // (2 * channels), 2, channels)
    result = jnp.einsum("kqap,abmpc->kbmqc", lookup, pieces, precision=lax.Precision.HIGHEST)
    return result.reshape(lookup.shape[0], second_len, merged)


def along_second(lookup, values, channels):
    first_len, second_len, merged = values.shape
    pieces = values.reshape(first_len, second_len, merged // (2 * channels), 2, channels)
    result = jnp.einsum("kqbp,abmpc->akmqc", lookup, pieces, precision=lax.Precision.HIGHEST)
    return result.reshape(first_len, lookup.shape[0], merged)


def split_parts(spectrum, channels):
    first_len, second_len, merged = spectrum.shape
    pieces = spectrum.reshape(first_len, second_len, merged // (2 * channels), 2, channels)
    return (pieces[:, :, :, 0], pieces[:, :, :, 1])


def split_weight(weight, channels):
    first_len, second_len, merged = weight.shape
    pieces = weight.astype(jnp.float32).reshape(
        first_len, second_len, merged // (2 * channels * channels), 2, channels, channels
    )
    return (pieces[:, :, :, 0], pieces[:, :, :, 1])


def mix_modes(spectrum, weight, mode_gain, channels):
    real_in, imag_in = split_parts(spectrum, channels)
    real_w, imag_w = split_weight(weight, channels)
    contract = lambda left, right: jnp.einsum(
        "abmc,abmco->abmo", left, right, precision=lax.Precision.HIGHEST
    )
    real_out = contract(real_in, real_w) - contract(imag_in, imag_w)
    imag_out = contract(real_in, imag_w) + contract(imag_in, real_w)
    stacked = jnp.stack([real_out, imag_out], axis=3) * mode_gain[None, None, :, None, None]
    return stacked.reshape(spectrum.shape)


def mix_adjoint(spectrum, back_spectrum, weight, mode_gain, channels):
    real_in, imag_in = split_parts(spectrum, channels)
    real_back, imag_back = split_parts(back_spectrum, channels)
    real_w, imag_w = split_weight(weight, channels)
    to_input = lambda left, right: jnp.einsum(
        "abmo,abmco->abmc", left, right, precision=lax.Precision.HIGHEST
    )
    outer_prod = lambda left, right: jnp.einsum(
        "abmc,abmo->abmco", left, right, precision=lax.Precision.HIGHEST
    )
    gain_modes = mode_gain[None, None, :, None, None]
    real_mode = to_input(real_back, real_w) + to_input(imag_back, imag_w)
    imag_mode = to_input(imag_back, real_w) - to_input(real_back, imag_w)
    grad_modes = (jnp.stack([real_mode, imag_mode], axis=3) * gain_modes).reshape(spectrum.shape)
    real_grad = outer_prod(real_in, real_back) + outer_prod(imag_in, imag_back)
    imag_grad = outer_prod(real_in, imag_back) - outer_prod(imag_in, real_back)
    gain_weight = mode_gain[None, None, :, None, None, None]
    grad_weight = jnp.stack([real_grad, imag_grad], axis=3) * gain_weight
    return (grad_modes, grad_weight.reshape(weight.shape))


def widen(block):
    padded = with_halo(block, (("gy", 0), ("gz", 1)), 1)
    return jnp.pad(padded, ((0, 0), (0, 0), (0, 0), (1, 1)))


def on_device(features, cotangent, spectral_weight, kernel_weight, channel_bias):
    rows_here, depth_here, channels, length = features.shape
    full_y = rows_here * lax.axis_size("gy")
    full_z = depth_here * lax.axis_size("gz")
    norm_scale = 1.0 / math.sqrt(length * full_y * full_z)
    y_places = lax.axis_index("gy") * rows_here + jnp.arange(rows_here, dtype=jnp.int32)
    z_places = lax.axis_index("gz") * depth_here + jnp.arange(depth_here, dtype=jnp.int32)
    modes_own = MX // lax.axis_size("gy")
    kx_global = lax.axis_index("gy") * modes_own + jnp.arange(modes_own, dtype=jnp.int32)
    mode_gain = jnp.where(kx_global == 0, 1.0, 2.0).astype(jnp.float32)
    freq_y = mode_freqs(jnp.arange(MY, dtype=jnp.int32), MY, full_y)
    freq_z = mode_freqs(jnp.arange(MZ, dtype=jnp.int32), MZ, full_z)

    def analyse(block):
        spectrum = line_forward(block, MX, norm_scale)
        spectrum = along_first(phase_table(freq_y, y_places, full_y, -1.0), spectrum, channels)
        spectrum = lax.psum_scatter(spectrum, "gy", scatter_dimension=2, tiled=True)
        spectrum = along_second(phase_table(freq_z, z_places, full_z, -1.0), spectrum, channels)
        return lax.psum_scatter(spectrum, "gz", scatter_dimension=0, tiled=True)

    def synthesize(spectrum):
        spectrum = lax.all_gather(spectrum, "gz", axis=0, tiled=True)
        planes = along_second(phase_table(z_places, freq_z, full_z, 1.0), spectrum, channels)
        planes = planes.reshape(MY, depth_here, modes_own, 2 * channels)
        y_lookup = phase_table(y_places, freq_y, full_y, 1.0)
        piece = lax.all_gather(planes, "gy", axis=2, tiled=True)
        count = piece.shape[2]
        flat = piece.reshape(MY, depth_here, count * 2 * channels)
        rows = along_first(y_lookup, flat, channels)
        spectrum = rows.reshape(rows_here, depth_here, count, 2 * channels)
        spectrum = spectrum.reshape(rows_here, depth_here, MX * 2 * channels)
        return line_inverse(spectrum, channels, length, norm_scale)

    spectrum = analyse(features)
    spectral = synthesize(mix_modes(spectrum, spectral_weight, mode_gain, channels))
    padded = widen(features)
    stacked = jnp.concatenate(
        [padded[..., 0:length], padded[..., 1 : length + 1], padded[..., 2 : length + 2]], axis=2
    )
    local = jnp.zeros((rows_here, depth_here, channels, length), jnp.float32)
    for shift_row in range(3):
        for shift_depth in range(3):
            window = stacked[
                shift_row : shift_row + rows_here, shift_depth : shift_depth + depth_here
            ]
            local = local + jnp.einsum(
                "ok,yzkx->yzox",
                kernel_weight[shift_row, shift_depth],
                window,
                preferred_element_type=jnp.float32,
            )
    pre = spectral + local + channel_bias[None, None, :, None]
    _, gelu_pull = jax.vjp(jax.nn.gelu, pre)
    (slope,) = gelu_pull(cotangent.astype(jnp.float32))
    slope = slope.astype(jnp.bfloat16)
    back_spectrum = analyse(slope)
    grad_modes, grad_spectral = mix_adjoint(
        spectrum, back_spectrum, spectral_weight, mode_gain, channels
    )
    back_field = synthesize(grad_modes)
    widened = widen(slope)
    rolled = jnp.zeros((rows_here, depth_here, 3 * channels, length + 2), jnp.float32)
    kernel_terms = []
    for shift_row in range(3):
        for shift_depth in range(3):
            source = widened[
                2 - shift_row : 2 - shift_row + rows_here,
                2 - shift_depth : 2 - shift_depth + depth_here,
            ]
            rolled = rolled + jnp.einsum(
                "ok,yzox->yzkx",
                kernel_weight[shift_row, shift_depth],
                source,
                preferred_element_type=jnp.float32,
            )
            window = stacked[
                shift_row : shift_row + rows_here, shift_depth : shift_depth + depth_here
            ]
            kernel_terms.append(
                jnp.einsum("yzox,yzkx->ok", slope, window, preferred_element_type=jnp.float32)
            )
    conv_field = rolled[:, :, 0:channels, 2 : 2 + length]
    conv_field = conv_field + rolled[:, :, channels : 2 * channels, 1 : 1 + length]
    conv_field = conv_field + rolled[:, :, 2 * channels : 3 * channels, 0:length]
    kernel_local = jnp.stack(kernel_terms, axis=0).reshape(3, 3, channels, 3 * channels)
    bias_local = jnp.sum(slope, axis=(0, 1, 3), dtype=jnp.float32)
    kernel_total, bias_total = lax.psum((kernel_local, bias_local), ("gy", "gz"))
    grad_field = (back_field + conv_field).astype(jnp.bfloat16)
    return (grad_field, grad_spectral, norm_scale * kernel_total, norm_scale * bias_total)


def solution(mesh):
    return jax.shard_map(
        on_device,
        mesh=mesh,
        in_specs=(
            P("gy", "gz", None, None),
            P("gy", "gz", None, None),
            P("gz", None, "gy"),
            P(),
            P(),
        ),
        out_specs=(P("gy", "gz", None, None), P("gz", None, "gy"), P(), P()),
        check_vma=False,
    )
```

profile of v0, /device:TPU:1, one launch (start us, length us, event | category | flops | bytes accessed | tf_op | source)
XLA Modules:
  0.0 647.8 jit_solution(13038420485590383446)
XLA Ops:
  10.0 5.1 fusion.136
  15.1 3.6 copy.74
  19.0 32.2 %reduce-scatter.5.cloned.1.call-done = f32[32,4,256]{2,0,1:T(8,128)} async-done(((f32[32,4,2048]{2,0,1:T(8,128)}), f32[32,4,256]{2,0,1:T(8,128)}) %reduce-scatter.5.cloned.1.call-update) | async-done | bytes 131088 | tf_op jit(solution)/shard_map/reduce_scatter | solution.py:154
  52.6 5.1 fusion.144
  58.9 5.3 collective-permute-start.1
  64.3 1.9 collective-permute-start
  69.2 4.4 reshape.887
  73.8 3.1 collective-permute-start.2
  76.9 1.8 collective-permute-start.3
  78.7 58.7 %reduce-scatter.7.cloned.1.call-done = f32[2,32,256]{1,2,0:T(8,128)} async-done(((f32[32,32,256]{1,2,0:T(8,128)}), f32[2,32,256]{1,2,0:T(8,128)}) %reduce-scatter.7.cloned.1.call-update) | async-done | bytes 65552 | tf_op jit(solution)/shard_map/reduce_scatter | solution.py:156
  138.6 3.4 fusion.72
  141.9 3.4 fusion.69
  145.4 3.4 fusion.68
  148.8 3.4 fusion.73
  157.3 2.3 pad_maximum_fusion.1
  159.7 2.2 fusion.15
  162.8 1.9 fusion.19
  164.8 31.8 %all-gather.5.cloned.1.call-done = f32[32,32,256]{2,1,0:T(8,128)} async-done(((f32[2,32,256]{2,1,0:T(8,128)}), f32[32,32,256]{2,1,0:T(8,128)}) %all-gather.5.cloned.1.call-update) | async-done | bytes 1048592 | tf_op jit(solution)/shard_map/all_gather | solution.py:159
  196.5 5.9 reshape.888
  202.5 4.8 fusion.74
  208.7 3.9 fusion.23
  212.6 3.9 fusion.27
  216.5 3.8 fusion.31
  220.3 1.9 fusion.35
  222.2 2.0 fusion.39
  224.1 1.9 fusion.43
  226.3 8.7 %all-gather.7.cloned.1.call-done = f32[32,4,32,64]{3,0,2,1:T(8,128)} async-done(((f32[32,4,4,64]{3,0,2,1:T(8,128)}), f32[32,4,32,64]{3,0,2,1:T(8,128)}) %all-gather.7.cloned.1.call-update) | async-done | bytes 1048592 | tf_op jit(solution)/shard_map/all_gather | solution.py:163
  235.0 5.9 reshape.951
  240.9 4.6 fusion.59
  245.6 2.1 fusion.139
  247.7 6.5 %convert_reduce_fusion = (f32[32]{0:T(128)S(1)}, bf16[8,4,32,512]{3,2,1,0:T(8,128)(2,1)S(1)}) fusion(f32[32]{0:T(128)S(1)} %copy-done.23, bf16[10,6,96,512]{3,2,1,0:T(8,128)(2,1)S(1)} %bitcast.406, bf16[3,3,32,96]{3,2,1,0:T(8,128)(2,1)S(1)} %copy-done.8, f32[8,4,512,32]{2,3,1,0:T(8,128)S(1)} %copy-done.1, f32[8,4,512,32]{2,3,1,0:T(8,128)S(1)} %copy-done.2, ...), kind=kOutput, calls=%fused_computation.83 | convolution fusion | flops 118489056 | bytes 24126080 | tf_op jit(solution)/shard_map/ok,yzkx->yzox/dot_general | solution.py:183
  266.3 2.3 collective-permute-start.4
  268.6 2.0 collective-permute-start.5
  273.8 5.5 fusion.157
  279.3 66.0 %psum.15 = f32[32]{0:T(128)S(1)} all-reduce(f32[32]{0:T(128)S(1)} %get-tuple-element.44), channel_id=1, replica_groups=mesh['gy'=8,'gz'=16] {'gy','gz'}, use_global_device_ids=true, to_apply=%region_6.7 | all-reduce | flops 32 | bytes 256 | tf_op jit(solution)/shard_map/psum | solution.py:224
  345.4 2.0 collective-permute-start.6
  349.3 3.6 copy.84
  353.0 53.4 %all-reduce.4.cloned.1.call-done = f32[3,3,32,96]{3,2,1,0:T(8,128)} async-done(((f32[3,3,32,96]{3,2,1,0:T(8,128)}), f32[3,3,32,96]{3,2,1,0:T(8,128)}) %all-reduce.4.cloned.1.call-update) | async-done | bytes 110608 | tf_op jit(solution)/shard_map/psum | solution.py:224
  407.9 4.3 fusion.188
  412.2 4.4 fusion.185
  416.6 4.3 fusion.182
  420.9 4.4 fusion.179
  425.3 11.3 %reduce-scatter.9.cloned.1.call-done = f32[32,4,256]{2,0,1:T(8,128)} async-done(((f32[32,4,2048]{2,0,1:T(8,128)}), f32[32,4,256]{2,0,1:T(8,128)}) %reduce-scatter.9.cloned.1.call-update) | async-done | bytes 131088 | tf_op jit(solution)/shard_map/reduce_scatter | solution.py:154
  438.0 5.1 fusion.142
  443.3 4.4 fusion.176
  447.7 4.4 fusion.173
  452.1 4.3 fusion.170
  456.5 4.4 fusion.167
  460.9 60.2 %reduce-scatter.11.cloned.1.call-done = f32[2,32,256]{1,2,0:T(8,128)} async-done(((f32[32,32,256]{1,2,0:T(8,128)}), f32[2,32,256]{1,2,0:T(8,128)}) %reduce-scatter.11.cloned.1.call-update) | async-done | bytes 65552 | tf_op jit(solution)/shard_map/reduce_scatter | solution.py:156
  522.2 5.0 fusion.66
  527.2 5.0 fusion.71
  532.3 5.0 fusion.70
  537.3 5.2 fusion.67
  543.8 24.0 %add_bitcast_fusion = f32[8,4,96,514]{3,2,1,0:T(8,128)} fusion(f32[8,4,514,96]{2,3,1,0:T(8,128)} %fusion.167, f32[8,4,514,96]{2,3,1,0:T(8,128)} %fusion.170, f32[8,4,514,96]{2,3,1,0:T(8,128)} %fusion.173, f32[8,4,514,96]{2,3,1,0:T(8,128)} %fusion.176, f32[8,4,514,96]{2,3,1,0:T(8,128)} %fusion.179, f32[8,4,514,96]{2,3,1,0:T(8,128)} %fusion.182, ...), kind=kOutput, calls=%fused_computation.1 | convolution fusion | flops 131452416 | bytes 58818560 | tf_op jit(solution)/shard_map/ok,yzox->yzkx/dot_general | solution.py:207
  568.0 2.3 add_bitcast_fusion.1
  570.3 4.4 pad_maximum_fusion
  574.7 6.2 stack.221
  581.0 5.2 all-gather.9.cloned.1.call-done
  586.2 5.9 reshape.893
  592.1 4.8 fusion.77
  599.7 24.9 %all-gather.11.cloned.1.call-done = f32[32,4,32,64]{3,0,2,1:T(8,128)} async-done(((f32[32,4,4,64]{3,0,2,1:T(8,128)}), f32[32,4,32,64]{3,0,2,1:T(8,128)}) %all-gather.11.cloned.1.call-update) | async-done | bytes 1048592 | tf_op jit(solution)/shard_map/all_gather | solution.py:163
  624.6 5.6 reshape.952
  630.2 4.7 fusion.62
  634.9 5.9 fusion.57
  (158 shorter events, 43.6 us)
Async XLA Ops:
  7.2 44.1 %reduce-scatter.5.cloned.1.call-start = ((), (), s32[]{:S(2)}) async-start(), calls=%async_computation.4 | async-start | bytes 1179648 | tf_op jit(solution)/shard_map/reduce_scatter | solution.py:154
  10.0 8.7 %copy-start.12 = (f32[32,1,8,2]{0,2,3,1:T(8,128)}, f32[32,1,8,2]{0,2,3,1:T(8,128)S(1)}, u32[]{:S(2)}) copy-start(f32[32,1,8,2]{0,2,3,1:T(8,128)S(1)} %get-tuple-element.26) | copy-start | bytes 6148
  10.0 8.7 %copy-start.14 = (f32[32,1,8,2]{0,2,3,1:T(8,128)}, f32[32,1,8,2]{0,2,3,1:T(8,128)S(1)}, u32[]{:S(2)}) copy-start(f32[32,1,8,2]{0,2,3,1:T(8,128)S(1)} %get-tuple-element.27) | copy-start | bytes 6148
  18.7 118.7 %reduce-scatter.7.cloned.1.call-start = ((), (), s32[]{:S(2)}) async-start(), calls=%async_computation.5 | async-start | bytes 4456448 | tf_op jit(solution)/shard_map/reduce_scatter | solution.py:156
  19.0 38.7 %copy-start.21 = (f32[32,2,4,2,1,1]{0,2,3,1,5,4:T(4,128)}, f32[32,2,4,2,1,1]{0,2,3,1,5,4:T(4,128)S(1)}, u32[]{:S(2)}) copy-start(f32[32,2,4,2,1,1]{0,2,3,1,5,4:T(4,128)S(1)} %maximum_bitcast_fusion.8) | copy-start | bytes 6148
  57.7 1.2 copy-start.3
  57.7 11.5 %copy-start.4 = (bf16[2,32,8192]{2,1,0:T(8,128)(2,1)S(1)}, bf16[2,32,8192]{2,1,0:T(8,128)(2,1)}, u32[]{:S(2)}) copy-start(bf16[2,32,8192]{2,1,0:T(8,128)(2,1)} %param.7) | copy-start | bytes 3145732
  57.7 138.8 %all-gather.5.cloned.1.call-start = ((), (), s32[]{:S(2)}) async-start(), calls=%async_computation.6 | async-start | bytes 1114112 | tf_op jit(solution)/shard_map/all_gather | solution.py:159
  58.9 14.8 %collective-permute-start.1 = (bf16[1,4,32,512]{3,2,1,0:T(8,128)(2,1)S(1)}, bf16[1,4,32,512]{3,2,1,0:T(8,128)(2,1)S(1)}, u32[]{:S(2)}, u32[]{:S(2)}) collective-permute-start(bf16[1,4,32,512]{3,2,1,0:T(8,128)(2,1)S(1)} %get-tuple-element.12), channel_id=1, source_target_pairs={{16,0},{32,16},{48,32},{64,48},{80,64},{96,80},{112,96},{17,1},{33... | collective-permute-start | bytes 393224 | tf_op jit(solution)/shard_map/ppermute | solution.py:23
  64.3 9.4 %collective-permute-start = (bf16[1,4,32,512]{3,2,1,0:T(8,128)(2,1)S(1)}, bf16[1,4,32,512]{3,2,1,0:T(8,128)(2,1)S(1)}, u32[]{:S(2)}, u32[]{:S(2)}) collective-permute-start(bf16[1,4,32,512]{3,2,1,0:T(8,128)(2,1)S(1)} %get-tuple-element.13), channel_id=1, source_target_pairs={{0,16},{16,32},{32,48},{48,64},{64,80},{80,96},{96,112},{1,17},{17... | collective-permute-start | bytes 393224 | tf_op jit(solution)/shard_map/ppermute | solution.py:21
  73.6 167.3 %copy-start.10 = (f32[8,1,32,2]{2,0,3,1:T(8,128)}, f32[8,1,32,2]{2,0,3,1:T(8,128)S(1)}, u32[]{:S(2)}) copy-start(f32[8,1,32,2]{2,0,3,1:T(8,128)S(1)} %get-tuple-element.25) | copy-start | bytes 6148
  73.8 80.5 %collective-permute-start.2 = (bf16[10,1,32,512]{3,2,1,0:T(8,128)(2,1)S(1)}, bf16[10,1,32,512]{3,2,1,0:T(8,128)(2,1)S(1)}, u32[]{:S(2)}, u32[]{:S(2)}) collective-permute-start(bf16[10,1,32,512]{3,2,1,0:T(8,128)(2,1)S(1)} %get-tuple-element.8), channel_id=1, source_target_pairs={{0,1},{1,2},{2,3},{3,4},{4,5},{5,6},{6,7},{7,8},{8,9},{9,10},{10,1... | collective-permute-start | bytes 983048 | tf_op jit(solution)/shard_map/ppermute | solution.py:21
  76.9 77.5 %collective-permute-start.3 = (bf16[10,1,32,512]{3,2,1,0:T(8,128)(2,1)S(1)}, bf16[10,1,32,512]{3,2,1,0:T(8,128)(2,1)S(1)}, u32[]{:S(2)}, u32[]{:S(2)}) collective-permute-start(bf16[10,1,32,512]{3,2,1,0:T(8,128)(2,1)S(1)} %get-tuple-element.9), channel_id=1, source_target_pairs={{1,0},{2,1},{3,2},{4,3},{5,4},{6,5},{7,6},{8,7},{9,8},{10,9},{11,1... | collective-permute-start | bytes 983048 | tf_op jit(solution)/shard_map/ppermute | solution.py:23
  154.2 80.8 %all-gather.7.cloned.1.call-start = ((), (), s32[]{:S(2)}) async-start(), calls=%async_computation.7 | async-start | bytes 2359296 | tf_op jit(solution)/shard_map/all_gather | solution.py:163
  157.3 2.3 copy-start.8
  159.7 3.2 copy-start
  164.8 37.7 %copy-start.16 = (f32[4,1,32,2]{2,0,3,1:T(4,128)S(1)}, f32[4,1,32,2]{2,0,3,1:T(4,128)}, u32[]{:S(2)}) copy-start(f32[4,1,32,2]{2,0,3,1:T(4,128)} %get-tuple-element.28) | copy-start | bytes 3076
  164.8 37.7 %copy-start.18 = (f32[4,1,32,2]{2,0,3,1:T(4,128)S(1)}, f32[4,1,32,2]{2,0,3,1:T(4,128)}, u32[]{:S(2)}) copy-start(f32[4,1,32,2]{2,0,3,1:T(4,128)} %get-tuple-element.29) | copy-start | bytes 3076
  208.6 197.7 %all-reduce.4.cloned.1.call-start = ((), (), s32[]{:S(2)}) async-start(), calls=%async_computation.12 | async-start | bytes 294912 | tf_op jit(solution)/shard_map/psum | solution.py:224
  208.6 11.6 %slice-start = ((s8[5898240]{0:T(1024)(128)(4,1)}), s8[4194304]{0:T(1024)(128)(4,1)S(1)}, s32[]{:S(2)}) async-start(s8[5898240]{0:T(1024)(128)(4,1)} %bitcast.403), calls=%async_computation.13 | async-start | bytes 8388608
  212.6 7.7 %slice-start.1 = ((s8[5898240]{0:T(1024)(128)(4,1)}), s8[1703936]{0:T(1024)(128)(4,1)S(1)}, s32[]{:S(2)}) async-start(s8[5898240]{0:T(1024)(128)(4,1)} %bitcast.403), calls=%async_computation.14 | async-start | bytes 3407872
  235.0 12.6 %slice-start.2 = ((s8[5898240]{0:T(1024)(128)(4,1)}), s8[1703936]{0:T(1024)(128)(4,1)S(1)}, s32[]{:S(2)}) async-start(s8[5898240]{0:T(1024)(128)(4,1)} %bitcast.405), calls=%async_computation.15 | async-start | bytes 3407872
  240.9 6.7 %slice-start.3 = ((s8[5898240]{0:T(1024)(128)(4,1)}), s8[4194304]{0:T(1024)(128)(4,1)S(1)}, s32[]{:S(2)}) async-start(s8[5898240]{0:T(1024)(128)(4,1)} %bitcast.405), calls=%async_computation.16 | async-start | bytes 8388608
  240.9 6.7 %copy-start.1 = (f32[8,4,512,32]{2,3,1,0:T(8,128)S(1)}, f32[8,4,512,32]{2,3,1,0:T(8,128)}, u32[]{:S(2)}) copy-start(f32[8,4,512,32]{2,3,1,0:T(8,128)} %fusion.15) | copy-start | bytes 6291460
  240.9 6.7 %copy-start.2 = (f32[8,4,512,32]{2,3,1,0:T(8,128)S(1)}, f32[8,4,512,32]{2,3,1,0:T(8,128)}, u32[]{:S(2)}) copy-start(f32[8,4,512,32]{2,3,1,0:T(8,128)} %fusion.19) | copy-start | bytes 6291460
  240.9 6.7 %copy-start.23 = (f32[32]{0:T(128)S(1)}, f32[32]{0:T(128)}, u32[]{:S(2)}) copy-start(f32[32]{0:T(128)} %param.9) | copy-start | bytes 388
  264.4 6.3 copy-start.5
  265.5 0.7 copy-start.6
  265.5 8.3 %copy-start.13 = (f32[32,1,8,2]{0,2,3,1:T(8,128)S(1)}, f32[32,1,8,2]{0,2,3,1:T(8,128)}, u32[]{:S(2)}) copy-start(f32[32,1,8,2]{0,2,3,1:T(8,128)} %copy-done.12) | copy-start | bytes 6148
  265.6 8.2 %copy-start.15 = (f32[32,1,8,2]{0,2,3,1:T(8,128)S(1)}, f32[32,1,8,2]{0,2,3,1:T(8,128)}, u32[]{:S(2)}) copy-start(f32[32,1,8,2]{0,2,3,1:T(8,128)} %copy-done.14) | copy-start | bytes 6148
  266.3 170.4 %reduce-scatter.9.cloned.1.call-start = ((), (), s32[]{:S(2)}) async-start(), calls=%async_computation.8 | async-start | bytes 1179648 | tf_op jit(solution)/shard_map/reduce_scatter | solution.py:154
  266.3 79.0 %collective-permute-start.4 = (bf16[1,4,32,512]{3,2,1,0:T(8,128)(2,1)}, bf16[1,4,32,512]{3,2,1,0:T(8,128)(2,1)S(1)}, u32[]{:S(2)}, u32[]{:S(2)}) collective-permute-start(bf16[1,4,32,512]{3,2,1,0:T(8,128)(2,1)} %get-tuple-element.10), channel_id=1, source_target_pairs={{0,16},{16,32},{32,48},{48,64},{64,80},{80,96},{96,112},{1,17},{17... | collective-permute-start | bytes 393224 | tf_op jit(solution)/shard_map/ppermute | solution.py:21
  268.6 76.7 %collective-permute-start.5 = (bf16[1,4,32,512]{3,2,1,0:T(8,128)(2,1)S(1)}, bf16[1,4,32,512]{3,2,1,0:T(8,128)(2,1)S(1)}, u32[]{:S(2)}, u32[]{:S(2)}) collective-permute-start(bf16[1,4,32,512]{3,2,1,0:T(8,128)(2,1)S(1)} %get-tuple-element.11), channel_id=1, source_target_pairs={{16,0},{32,16},{48,32},{64,48},{80,64},{96,80},{112,96},{17,1},{33... | collective-permute-start | bytes 393224 | tf_op jit(solution)/shard_map/ppermute | solution.py:23
  345.4 62.5 %collective-permute-start.6 = (bf16[10,1,32,512]{3,2,1,0:T(8,128)(2,1)S(1)}, bf16[10,1,32,512]{3,2,1,0:T(8,128)(2,1)S(1)}, u32[]{:S(2)}, u32[]{:S(2)}) collective-permute-start(bf16[10,1,32,512]{3,2,1,0:T(8,128)(2,1)S(1)} %get-tuple-element.6), channel_id=1, source_target_pairs={{0,1},{1,2},{2,3},{3,4},{4,5},{5,6},{6,7},{7,8},{8,9},{9,10},{10,1... | collective-permute-start | bytes 983048 | tf_op jit(solution)/shard_map/ppermute | solution.py:21
  347.4 60.5 %collective-permute-start.7 = (bf16[10,1,32,512]{3,2,1,0:T(8,128)(2,1)S(1)}, bf16[10,1,32,512]{3,2,1,0:T(8,128)(2,1)S(1)}, u32[]{:S(2)}, u32[]{:S(2)}) collective-permute-start(bf16[10,1,32,512]{3,2,1,0:T(8,128)(2,1)S(1)} %get-tuple-element.7), channel_id=1, source_target_pairs={{1,0},{2,1},{3,2},{4,3},{5,4},{6,5},{7,6},{8,7},{9,8},{10,9},{11,1... | collective-permute-start | bytes 983048 | tf_op jit(solution)/shard_map/ppermute | solution.py:23
  349.3 58.7 %copy-start.9 = (bf16[3,3,32,96]{3,2,1,0:T(8,128)(2,1)S(1)}, bf16[3,3,32,96]{3,2,1,0:T(8,128)(2,1)}, u32[]{:S(2)}) copy-start(bf16[3,3,32,96]{3,2,1,0:T(8,128)(2,1)} %param.8) | copy-start | bytes 165892
  352.9 168.2 %reduce-scatter.11.cloned.1.call-start = ((), (), s32[]{:S(2)}) async-start(), calls=%async_computation.9 | async-start | bytes 4456448 | tf_op jit(solution)/shard_map/reduce_scatter | solution.py:156
  420.9 17.0 %copy-start.22 = (f32[32,2,4,2,1,1]{0,2,3,1,5,4:T(4,128)S(1)}, f32[32,2,4,2,1,1]{0,2,3,1,5,4:T(4,128)}, u32[]{:S(2)}) copy-start(f32[32,2,4,2,1,1]{0,2,3,1,5,4:T(4,128)} %copy-done.21) | copy-start | bytes 6148
  443.1 143.0 %all-gather.9.cloned.1.call-start = ((), (), s32[]{:S(2)}) async-start(), calls=%async_computation.10 | async-start | bytes 1114112 | tf_op jit(solution)/shard_map/all_gather | solution.py:159
  532.3 10.8 %copy-start.20 = (f32[256]{0:T(256)S(1)}, f32[256]{0:T(256)}, u32[]{:S(2)}) copy-start(f32[256]{0:T(256)} %mul.457) | copy-start | bytes 3076
  543.8 80.8 %all-gather.11.cloned.1.call-start = ((), (), s32[]{:S(2)}) async-start(), calls=%async_computation.11 | async-start | bytes 2359296 | tf_op jit(solution)/shard_map/all_gather | solution.py:163
  581.0 11.1 %copy-start.17 = (f32[4,1,32,2]{2,0,3,1:T(4,128)S(1)}, f32[4,1,32,2]{2,0,3,1:T(4,128)}, u32[]{:S(2)}) copy-start(f32[4,1,32,2]{2,0,3,1:T(4,128)} %get-tuple-element.28) | copy-start | bytes 3076
  581.0 11.1 %copy-start.19 = (f32[4,1,32,2]{2,0,3,1:T(4,128)S(1)}, f32[4,1,32,2]{2,0,3,1:T(4,128)}, u32[]{:S(2)}) copy-start(f32[4,1,32,2]{2,0,3,1:T(4,128)} %get-tuple-element.29) | copy-start | bytes 3076
  592.1 6.1 copy-start.7
  599.7 30.5 %copy-start.11 = (f32[8,1,32,2]{2,0,3,1:T(8,128)S(1)}, f32[8,1,32,2]{2,0,3,1:T(8,128)}, u32[]{:S(2)}) copy-start(f32[8,1,32,2]{2,0,3,1:T(8,128)} %copy-done.10) | copy-start | bytes 6148
Sparse Core Ops, SparseCore 0:
  18.9 32.2 reduce-scatter.4
  57.8 79.5 reduce-scatter.6
  154.3 42.2 all-gather.4
  208.7 26.2 all-gather.6
  266.4 139.8 all-reduce.3
  409.1 27.4 reduce-scatter.8
  443.2 77.7 reduce-scatter.10
  543.9 42.2 all-gather.8
  598.3 26.2 all-gather.10
where the time goes:
time: 655 us; the launch traced here: 648 us
  waiting for transfers between devices  287 us (44%)
  matrix products  182 us (28%)
  blocking collectives  66 us (10%)
  local copies, waits for them, and re-layouts  59.4 us (9%)
  starting transfers between devices  20.5 us (3%)
  other arithmetic  18.5 us (3%)
  between operations  15 us (2%)
    reduce_scatter x2, waiting for transfers between devices, analyse(): return lax.psum_scatter(spectrum, 'gz', scatter_dimension=0, tiled=True)  119 us
    psum x1, blocking collectives, on_device(): lax.psum((kernel_local, bias_local), ('gy', 'gz'))  66 us
    dot_general x9, matrix products, on_device(): jnp.einsum('ok,yzox->yzkx', kernel_weight[shift_row, shift_depth], source...  58.8 us
    psum x1, waiting for transfers between devices, on_device(): lax.psum((kernel_local, bias_local), ('gy', 'gz'))  53.4 us
    reduce_scatter x2, waiting for transfers between devices, analyse(): spectrum = lax.psum_scatter(spectrum, 'gy', scatter_dimension=2, tiled=True)  43.6 us
    all_gather x2, waiting for transfers between devices, synthesize(): spectrum = lax.all_gather(spectrum, 'gz', axis=0, tiled=True)  36.9 us
    all_gather x2, waiting for transfers between devices, synthesize(): piece = lax.all_gather(planes, 'gy', axis=2, tiled=True)  33.6 us
    dot_general x9, matrix products, on_device(): jnp.einsum('ok,yzkx->yzox', kernel_weight[shift_row, shift_depth], window...  28.1 us
  transfers between devices with their start and end apart: 17, of which 9 were waited for; matrix products, arithmetic and copies ran while one was open for 22% of the time, Pallas kernels for 0%

commit v1 on v0

v1 whole, which is shorter than its diff:
```python
import functools
import math

import jax
import jax.numpy as jnp
import ml_dtypes
import numpy as np
from jax import lax
from jax.experimental import pallas as pl
from jax.experimental.pallas import tpu as pltpu
from jax.sharding import PartitionSpec as P

NX, NY, NZ = 512, 64, 64
C = 32
GY, GZ = 8, 16
YL, ZL = 8, 4
KXL = 4
ROWS = 24
SCALE = 1.0 / math.sqrt(NX * NY * NZ)
F32, BF16 = jnp.float32, jnp.bfloat16
VMEM_BYTES = 32 * 1024 * 1024


def freqs(count, length):
    index = np.arange(count)
    return np.where(index < count // 2, index, length - count + index)


def angle(a, b, length):
    return 2.0 * math.pi / length * ((a[:, None] * b[None, :]) % length)


def split_np(table):
    high = table.astype(ml_dtypes.bfloat16)
    low = (table - high.astype(np.float64)).astype(ml_dtypes.bfloat16)
    return high, low


def x_forward_table():
    turn = angle(np.arange(32), np.arange(NX), NX)
    both = np.stack([np.cos(turn), -np.sin(turn)], 0).reshape(2, GY, KXL, NX)
    return both.transpose(1, 0, 2, 3).reshape(64, NX).astype(ml_dtypes.bfloat16)


def x_inverse_table():
    turn = angle(np.arange(32), np.arange(NX), NX)
    both = np.stack([np.cos(turn), -np.sin(turn)], 1).reshape(64, NX)
    high, low = split_np(both)
    return np.concatenate([high, low, high], 0)


def rotation(turn, sign):
    cos, sin = np.cos(turn), sign * np.sin(turn)
    return np.stack([np.stack([cos, -sin], -1), np.stack([sin, cos], -1)], 1)


def y_forward_tables():
    every = []
    for g in range(GY):
        turn = angle(freqs(32, NY), g * YL + np.arange(YL), NY)
        table = rotation(turn, -1.0).reshape(GZ, 2, 2, YL, 2)
        full = np.einsum("gkpyq,ab->gakpyqb", table, np.eye(KXL)).reshape(256, 64)
        high, low = split_np(full)
        every.append(np.concatenate([high, low, high], 1))
    return np.stack(every)


def z_forward_table():
    turn = angle(freqs(32, NZ), np.arange(NZ), NZ)
    table = SCALE * rotation(turn, -1.0).reshape(32, 2, GZ, ZL, 2)
    full = np.einsum("kpgzq,ab->pakzbqg", table, np.eye(2)).reshape(128, 256)
    return np.stack(split_np(full))


def z_inverse_table():
    turn = angle(np.arange(NZ), freqs(32, NZ), NZ)
    table = SCALE * rotation(turn, 1.0).reshape(GZ, ZL, 2, 32, 2)
    full = np.einsum("gzpkq,ab->gapzqbk", table, np.eye(2)).reshape(256, 128)
    return np.stack(split_np(full))


def y_inverse_tables():
    every = []
    for g in range(GY):
        turn = angle(g * YL + np.arange(YL), freqs(32, NY), NY)
        table = rotation(turn, 1.0).reshape(YL, 2, GZ, 2, 2)
        full = np.einsum("ypgkq,ab->apygkqb", table, np.eye(ZL)).reshape(64, 256)
        every.append(np.concatenate(split_np(full), 0))
    return np.stack(every)


def split(value):
    high = value.astype(BF16)
    return high, (value - high.astype(F32)).astype(BF16)


def dot(a, b):
    return jnp.dot(a, b, preferred_element_type=F32)


def dot_nt(a, b):
    return lax.dot_general(a, b, (((1,), (1,)), ((), ())), preferred_element_type=F32)


def dot_tn(a, b):
    return lax.dot_general(a, b, (((0,), (0,)), ((), ())), preferred_element_type=F32)


def lane_of(shape):
    return lax.broadcasted_iota(jnp.int32, shape, len(shape) - 1)


def swap_blocks(parts):
    lane = lane_of(parts[0].shape)
    half = lane < 64
    p0, p1, p2, p3 = parts
    q0 = jnp.where(half, p0, pltpu.roll(p2, 64, 1))
    q2 = jnp.where(half, pltpu.roll(p0, 64, 1), p2)
    q1 = jnp.where(half, p1, pltpu.roll(p3, 64, 1))
    q3 = jnp.where(half, pltpu.roll(p1, 64, 1), p3)
    even = (lane & 32) == 0
    out = []
    for lo, hi in ((q0, q1), (q2, q3)):
        out.append(jnp.where(even, lo, pltpu.roll(hi, 32, 1)))
        out.append(jnp.where(even, pltpu.roll(lo, 96, 1), hi))
    return out


def y_forward(lines, table):
    blocks = []
    for g in range(GY):
        blocks.append(jnp.concatenate([line[g * 8 : g * 8 + 8] for line in lines], 0))
    joined = jnp.concatenate(blocks, 1)
    high, low = split(joined)
    return dot(table, jnp.concatenate([high, high, low], 0))


def collect_spectrum(recv_ref, table_ref, sums_ref):
    total = recv_ref[0:GZ, 0:16, :].astype(F32)
    for g in range(1, GY):
        total = total + recv_ref[g * GZ : (g + 1) * GZ, 0:16, :].astype(F32)
    sums_ref[...] = total.reshape(256, 128)
    turned = []
    for j in range(4):
        turned.append(
            swap_blocks([sums_ref[pl.ds(k * 4 + j, GZ, stride=16), :] for k in range(KXL)])
        )
    joined = jnp.concatenate([turned[j][z] for z in range(ZL) for j in range(4)], 0)
    high, low = split(joined)
    return dot(table_ref[0], high) + dot(table_ref[1], high) + dot(table_ref[0], low)


def z_inverse(modes, table_ref):
    high, low = split(modes)
    return dot(table_ref[0], high) + dot(table_ref[1], high) + dot(table_ref[0], low)


def gain_lanes():
    lane = lane_of((128, 128))
    first = jnp.logical_and(lane < 32, lax.axis_index("gy") == 0)
    return jnp.where(first, 1.0, 2.0).astype(F32)


def repeat_matrix():
    row = lax.broadcasted_iota(jnp.int32, (64, 1024), 0) & 31
    return jnp.where(row == lane_of((64, 1024)) // 32, 1.0, 0.0).astype(BF16)


def spread(spectrum, k, matrix):
    high, low = split(spectrum[:, k * 32 : k * 32 + 32])
    return dot(jnp.concatenate([high, low], 1), matrix)


def fold_tiles(value):
    total = value[:, 0:128]
    for t in range(1, 8):
        total = total + value[:, t * 128 : t * 128 + 128]
    total = total + pltpu.roll(total, 64, 1)
    return total + pltpu.roll(total, 32, 1)


def synth_fields(recv_ref, table, field_ref):
    joined = jnp.concatenate(
        [recv_ref[g * GZ : (g + 1) * GZ, 0:16, :].reshape(256, 128) for g in range(GY)], 1
    )
    both = dot(table, joined)
    planes = both[0:64] + both[64:128]
    for g in range(GY):
        cols = planes[:, g * 128 : g * 128 + 128]
        turned = swap_blocks([cols[z * 16 : z * 16 + 16] for z in range(ZL)])
        for k in range(KXL):
            for part in range(2):
                field_ref[pl.ds((g * 4 + k) * 2 + part, YL, stride=64), :] = turned[k][
                    part * 8 : part * 8 + 8
                ]


def x_inverse(field, table):
    high, low = split(field)
    return dot_tn(jnp.concatenate([high, high, low], 0), table)


def shift_right(value):
    return jnp.where(lane_of(value.shape) == 0, 0.0, pltpu.roll(value, 1, 1))


def shift_left(value):
    return jnp.where(lane_of(value.shape) == NX - 1, 0.0, pltpu.roll(value, NX - 1, 1))


def analyse_kernel(idx_ref, field_ref, tx_ref, ty_ref, send_ref):
    lines = [dot_nt(tx_ref[...], field_ref[y]) for y in range(YL)]
    out = y_forward(lines, ty_ref[0])
    for g in range(GY):
        block = out[:, g * 128 : g * 128 + 128].astype(BF16)
        send_ref[g * GZ : (g + 1) * GZ] = block.reshape(GZ, 16, 128)


def mix_kernel(recv_ref, weight_ref, tzf_ref, tzi_ref, send_ref, spec_ref, sums_ref):
    spectrum = collect_spectrum(recv_ref, tzf_ref, sums_ref)
    spec_ref[...] = spectrum
    matrix = repeat_matrix()
    lane = lane_of((64, 128)) // 32
    real = jnp.zeros((64, 128), F32)
    imag = jnp.zeros((64, 128), F32)
    for k in range(KXL):
        wide = spread(spectrum, k, matrix)
        w_re = weight_ref[:, k * 2048 : k * 2048 + 1024].astype(F32)
        w_im = weight_ref[:, k * 2048 + 1024 : k * 2048 + 2048].astype(F32)
        s_re, s_im = wide[0:64], wide[64:128]
        real = jnp.where(lane == k, fold_tiles(s_re * w_re - s_im * w_im), real)
        imag = jnp.where(lane == k, fold_tiles(s_re * w_im + s_im * w_re), imag)
    modes = jnp.concatenate([real, imag], 0) * gain_lanes()
    block = z_inverse(modes, tzi_ref).astype(BF16).reshape(GZ, 16, 128)
    for g in range(GY):
        send_ref[g * GZ : (g + 1) * GZ] = block


def conv_rows(pad_ref, taps_ref, y):
    window = pad_ref[pl.ds(y, 3)].reshape(576, NX)
    wide = dot(taps_ref[...], window)
    return wide[128:256] + shift_right(wide[0:128]) + shift_left(wide[256:384])


def build_taps(kernel_ref, taps_ref):
    zero = jnp.zeros((C, C), F32)
    for dx in range(3):
        for z in range(ZL):
            parts = []
            for dy in range(3):
                for zin in range(ZL + 2):
                    dz = zin - z
                    if 0 <= dz < 3:
                        parts.append(
                            kernel_ref[dy, dz].astype(F32)[:, dx * C : dx * C + C]
                        )
                    else:
                        parts.append(zero)
            row = (dx * ZL + z) * C
            taps_ref[row : row + C, :] = jnp.concatenate(parts, 1).astype(BF16)


def fill_pad(pad_ref, own_ref, ylo_ref, yhi_ref, zlo_ref, zhi_ref):
    pad_ref[:, 0:32] = zlo_ref[...]
    pad_ref[:, 160:192] = zhi_ref[...]
    pad_ref[1:9, 32:160] = own_ref[...]
    pad_ref[0, 32:160] = ylo_ref[...]
    pad_ref[9, 32:160] = yhi_ref[...]


def conv_kernel(own_ref, ylo_ref, yhi_ref, zlo_ref, zhi_ref, kernel_ref, bias_ref, out_ref, pad_ref, taps_ref):
    fill_pad(pad_ref, own_ref, ylo_ref, yhi_ref, zlo_ref, zhi_ref)
    build_taps(kernel_ref, taps_ref)

    def step(y, carry):
        out_ref[y] = conv_rows(pad_ref, taps_ref, y) + bias_ref[...]
        return carry

    lax.fori_loop(0, YL, step, 0)


def slope_kernel(
    idx_ref, recv_ref, local_ref, cot_ref, pad_ref, tyi_ref, txi_ref, tx_ref, ty_ref,
    slope_ref, send_ref, field_ref, sums_ref, rows_ref,
):
    synth_fields(recv_ref, tyi_ref[0], field_ref)
    root = math.sqrt(2.0 / math.pi)
    sums_ref[...] = jnp.zeros_like(sums_ref)
    lines = []
    bias = jnp.zeros((128, 1), F32)
    for y in range(YL):
        pre = x_inverse(field_ref[y * 64 : y * 64 + 64], txi_ref[...]) + local_ref[y]
        square = pre * pre
        bent = jnp.tanh(root * pre * (1.0 + 0.044715 * square))
        rate = 0.5 * (1.0 + bent) + 0.5 * root * pre * (1.0 - bent * bent) * (
            1.0 + 3.0 * 0.044715 * square
        )
        slope = (cot_ref[y].astype(F32) * rate).astype(BF16)
        slope_ref[y] = slope
        lines.append(dot_nt(tx_ref[...], slope))
        wide = slope.astype(F32)
        bias = bias + jnp.sum(wide, axis=1, keepdims=True)
        three = jnp.concatenate(
            [shift_left(wide).astype(BF16), slope, shift_right(wide).astype(BF16)], 0
        )
        sums_ref[...] += dot_nt(three, pad_ref[y : y + 3].reshape(576, NX))
    out = y_forward(lines, ty_ref[0])
    for g in range(GY):
        block = out[:, g * 128 : g * 128 + 128].astype(BF16)
        send_ref[g * GZ : (g + 1) * GZ, 0:16] = block.reshape(GZ, 16, 128)
    bias32 = bias[0:32] + bias[32:64] + bias[64:96] + bias[96:128]
    lane = lane_of((C, 128))
    rows_ref[...] = jnp.zeros_like(rows_ref)
    for dx in range(3):
        for dy in range(3):
            total = jnp.zeros((C, 96), F32)
            for z in range(ZL):
                row = (dx * ZL + z) * C
                col = dy * 192 + z * C
                total = total + sums_ref[row : row + C, col : col + 96]
            total = jnp.concatenate([total, jnp.zeros((C, 32), F32)], 1)
            total = jnp.where(lane == 96, bias32, total)
            high = total.astype(BF16).astype(F32)
            rows_ref[pl.ds(dx * C * 8 + dy, C, stride=8), :] = high
            rows_ref[pl.ds(dx * C * 8 + dy + 3, C, stride=8), :] = total - high
    send_ref[:, 16:24] = rows_ref[...].reshape(128, 8, 128).astype(BF16)


def adjoint_kernel(recv_ref, weight_ref, tzf_ref, tzi_ref, send_ref, spec_ref, sums_ref):
    spectrum = collect_spectrum(recv_ref, tzf_ref, sums_ref)
    spec_ref[...] = spectrum
    row = lax.broadcasted_iota(jnp.int32, (1024, 128), 0) // 32
    lane = lane_of((1024, 128))
    gather = []
    for k in range(KXL):
        w_re = weight_ref[:, k * 2048 : k * 2048 + 1024].astype(F32)
        w_im = weight_ref[:, k * 2048 + 1024 : k * 2048 + 2048].astype(F32)
        own = spectrum[:, k * 32 : k * 32 + 32]
        four = jnp.concatenate([own] * 4, 1)
        wide = jnp.concatenate([four] * 8, 1)
        b_re, b_im = wide[0:64], wide[64:128]
        both = jnp.concatenate([b_re * w_re + b_im * w_im, b_im * w_re - b_re * w_im], 0)
        matrix = jnp.where(row + k * 32 == lane, 1.0, 0.0).astype(BF16)
        high, low = split(both)
        gather.append(dot(high, matrix) + dot(low, matrix))
    modes = (gather[0] + gather[1] + gather[2] + gather[3]) * gain_lanes()
    block = z_inverse(modes, tzi_ref).astype(BF16).reshape(GZ, 16, 128)
    total = jnp.sum(recv_ref[:, 16:24].astype(F32), axis=0)
    total = total + pltpu.roll(total, 5, 0)
    high = total.astype(BF16).astype(F32)
    low = total - high
    part = lax.broadcasted_iota(jnp.int32, (8, 128), 0)
    tail = jnp.where(part < 3, high, jnp.where(part < 6, pltpu.roll(low, 3, 0), 0.0)).astype(BF16)
    tail = jnp.broadcast_to(tail[None], (GZ, 8, 128))
    for g in range(GY):
        send_ref[g * GZ : (g + 1) * GZ, 0:16] = block
        send_ref[g * GZ : (g + 1) * GZ, 16:24] = tail


def outer_kernel(spec_ref, back_ref, out_ref):
    matrix = repeat_matrix()
    gain = gain_lanes()
    spectrum = spec_ref[...]
    back = back_ref[...] * gain
    for k in range(KXL):
        wide = spread(spectrum, k, matrix)
        s_re, s_im = wide[0:64], wide[64:128]
        own = back[:, k * 32 : k * 32 + 32]
        four = jnp.concatenate([own] * 4, 1)
        tiled = jnp.concatenate([four] * 8, 1)
        b_re, b_im = tiled[0:64], tiled[64:128]
        out_ref[:, k * 2048 : k * 2048 + 1024] = s_re * b_re + s_im * b_im
        out_ref[:, k * 2048 + 1024 : k * 2048 + 2048] = s_re * b_im - s_im * b_re


def final_kernel(
    idx_ref, recv_ref, conv_ref, tyi_ref, txi_ref, grad_ref, kernel_ref, bias_ref, field_ref, rows_ref
):
    synth_fields(recv_ref, tyi_ref[0], field_ref)
    for y in range(YL):
        back = x_inverse(field_ref[y * 64 : y * 64 + 64], txi_ref[...])
        grad_ref[y] = (back + conv_ref[y]).astype(BF16)
    rows_ref[...] = recv_ref[:, 16:24].astype(F32).reshape(1024, 128)
    for dy in range(3):
        three = []
        for dx in range(3):
            high = rows_ref[pl.ds(dx * C * 8 + dy, C, stride=8), :]
            low = rows_ref[pl.ds(dx * C * 8 + dy + 3, C, stride=8), :]
            three.append(SCALE * (high + low))
        for dz in range(3):
            kernel_ref[dy, dz] = jnp.concatenate([t[:, dz * C : dz * C + C] for t in three], 1)
        if dy == 0:
            bias_ref[...] = three[0][:, 96:97]


def call(body, out_shape, scratch=(), flops=0, nbytes=0, **extra):
    return pl.pallas_call(
        body,
        out_shape=out_shape,
        scratch_shapes=list(scratch),
        compiler_params=pltpu.CompilerParams(vmem_limit_bytes=VMEM_BYTES),
        cost_estimate=pl.CostEstimate(flops=flops, bytes_accessed=nbytes, transcendentals=0),
        **extra,
    )


def call_indexed(body, operands, out_shape, by_index, scratch=(), flops=0, nbytes=0):
    def whole(shape):
        return pl.BlockSpec(shape, lambda i, idx, n=len(shape): (0,) * n)

    def mine(shape):
        return pl.BlockSpec((1,) + shape[1:], lambda i, idx, n=len(shape): (idx[0],) + (0,) * (n - 1))

    in_specs = [
        mine(a.shape) if n in by_index else whole(a.shape) for n, a in enumerate(operands)
    ]
    shapes = out_shape if isinstance(out_shape, (tuple, list)) else (out_shape,)
    out_specs = [whole(s.shape) for s in shapes]
    if not isinstance(out_shape, (tuple, list)):
        out_specs = out_specs[0]
    index = lax.axis_index("gy").astype(jnp.int32).reshape(1)
    return pl.pallas_call(
        body,
        out_shape=out_shape,
        grid_spec=pltpu.PrefetchScalarGridSpec(
            num_scalar_prefetch=1,
            grid=(1,),
            in_specs=in_specs,
            out_specs=out_specs,
            scratch_shapes=list(scratch),
        ),
        compiler_params=pltpu.CompilerParams(vmem_limit_bytes=VMEM_BYTES),
        cost_estimate=pl.CostEstimate(flops=flops, bytes_accessed=nbytes, transcendentals=0),
    )(index, *operands)


def exchange(blocks):
    return lax.all_to_all(blocks, ("gy", "gz"), 0, 0, tiled=True)


def halos(own):
    up = [(i, i + 1) for i in range(GY - 1)]
    down = [(i + 1, i) for i in range(GY - 1)]
    ylo = lax.ppermute(own[YL - 1], "gy", up)
    yhi = lax.ppermute(own[0], "gy", down)
    ahead = [(i, i + 1) for i in range(GZ - 1)]
    behind = [(i + 1, i) for i in range(GZ - 1)]
    last = jnp.concatenate([ylo[None, 96:128], own[:, 96:128], yhi[None, 96:128]], 0)
    first = jnp.concatenate([ylo[None, 0:32], own[:, 0:32], yhi[None, 0:32]], 0)
    zlo = lax.ppermute(last, "gz", ahead)
    zhi = lax.ppermute(first, "gz", behind)
    return ylo, yhi, zlo, zhi


def shape(dims, kind):
    return jax.ShapeDtypeStruct(dims, kind)


def conv(own, halo, kernel, bias):
    return call(
        conv_kernel,
        (shape((YL, 128, NX), F32), shape((YL + 2, 192, NX), BF16)),
        [pltpu.VMEM((384, 576), BF16)],
        flops=2 * YL * 384 * 576 * NX,
        nbytes=6 << 20,
    )(own, *halo, kernel, bias)


def on_device(features, cotangent, spectral_weight, kernel_weight, channel_bias):
    own = features.reshape(YL, 128, NX)
    cot = cotangent.reshape(YL, 128, NX)
    weight = spectral_weight.reshape(64, 8192)
    tx = jnp.asarray(x_forward_table())
    txi = jnp.asarray(x_inverse_table())
    ty = jnp.asarray(y_forward_tables())
    tyi = jnp.asarray(y_inverse_tables())
    tzf = jnp.asarray(z_forward_table())
    tzi = jnp.asarray(z_inverse_table())
    bias_rows = jnp.tile(channel_bias, ZL).reshape(128, 1)
    flipped = kernel_weight.reshape(3, 3, C, 3, C)[::-1, ::-1, :, ::-1, :]
    flipped = flipped.transpose(0, 1, 4, 3, 2).reshape(3, 3, C, 3 * C)

    send = call_indexed(
        analyse_kernel, (own, tx, ty), shape((128, 16, 128), BF16), (2,), flops=1 << 27, nbytes=2 << 20
    )
    recv = exchange(send)
    halo = halos(own)
    local, padded = conv(own, halo, kernel_weight, bias_rows)
    send, spectrum = call(
        mix_kernel,
        (shape((128, 16, 128), BF16), shape((128, 128), F32)),
        [pltpu.VMEM((256, 128), F32)],
        flops=1 << 27,
        nbytes=2 << 20,
    )(recv, weight, tzf, tzi)
    recv = exchange(send)
    slope, send = call_indexed(
        slope_kernel,
        (recv, local, cot, padded, tyi, txi, tx, ty),
        (shape((YL, 128, NX), BF16), shape((128, ROWS, 128), BF16)),
        (4, 7),
        [
            pltpu.VMEM((512, 128), F32),
            pltpu.VMEM((384, 576), F32),
            pltpu.VMEM((1024, 128), F32),
        ],
        flops=1 << 31,
        nbytes=8 << 20,
    )
    recv = exchange(send)
    halo = halos(slope)
    conv_field, _ = conv(slope, halo, flipped, jnp.zeros((128, 1), F32))
    send, back = call(
        adjoint_kernel,
        (shape((128, ROWS, 128), BF16), shape((128, 128), F32)),
        [pltpu.VMEM((256, 128), F32)],
        flops=1 << 27,
        nbytes=2 << 20,
    )(recv, weight, tzf, tzi)
    recv = exchange(send)
    grad_spectral = call(
        outer_kernel, shape((64, 8192), F32), flops=1 << 27, nbytes=3 << 20
    )(spectrum, back)
    grad_field, grad_kernel, grad_bias = call_indexed(
        final_kernel,
        (recv, conv_field, tyi, txi),
        (shape((YL, 128, NX), BF16), shape((3, 3, C, 3 * C), F32), shape((C, 1), F32)),
        (2,),
        [pltpu.VMEM((512, 128), F32), pltpu.VMEM((1024, 128), F32)],
        flops=1 << 28,
        nbytes=4 << 20,
    )
    return (
        grad_field.reshape(features.shape),
        grad_spectral.reshape(spectral_weight.shape),
        grad_kernel,
        grad_bias.reshape(C),
    )


def solution(mesh):
    return jax.shard_map(
        on_device,
        mesh=mesh,
        in_specs=(
            P("gy", "gz", None, None),
            P("gy", "gz", None, None),
            P("gz", None, "gy"),
            P(),
            P(),
        ),
        out_specs=(P("gy", "gz", None, None), P("gz", None, "gy"), P(), P()),
        check_vma=False,
    )
```

time: 655 us -> 158 us (0.24)
  waiting for transfers between devices: 287 us -> 36.7 us
  matrix products: 182 us -> 0 us
  blocking collectives: 66 us -> 0 us
  starting transfers between devices: 20.5 us -> 53.6 us
  Pallas kernels: 0 us -> 29.6 us
  local copies, waits for them, and re-layouts: 59.4 us -> 31.5 us
  other arithmetic: 18.5 us -> 3.03 us
  between operations: 15 us -> 1.01 us
    dot_general x47 -> x0, matrix products: 182 us -> none  [the longest x9 58.8 us: on_device(): jnp.einsum('ok,yzox->yzkx', kernel_weight[shift_row, shift_depth], source...]
    reduce_scatter x4 -> x0, waiting for transfers between devices: 162 us -> none  [the longest x2 119 us: analyse(): return lax.psum_scatter(spectrum, 'gz', scatter_dimension=0, tiled=True)]
    all_gather x4 -> x0, waiting for transfers between devices: 70.5 us -> none  [the longest x2 36.9 us: synthesize(): spectrum = lax.all_gather(spectrum, 'gz', axis=0, tiled=True)]
    psum x1 -> x0, blocking collectives: 66 us -> none  [on_device(): lax.psum((kernel_local, bias_local), ('gy', 'gz'))]
    psum x1 -> x0, waiting for transfers between devices: 53.4 us -> none  [on_device(): lax.psum((kernel_local, bias_local), ('gy', 'gz'))]
    all_to_all x0 -> x4, starting transfers between devices: none -> 30.8 us  [exchange(): return lax.all_to_all(blocks, ('gy', 'gz'), 0, 0, tiled=True)]
    pallas_call x0 -> x8, Pallas kernels: none -> 29.6 us  [the longest x2 11.7 us: conv(): call(conv_kernel, (shape((YL, 128, NX), F32), shape((YL + 2, 192, NX), BF...]
    reshape x7 -> x2, local copies, waits for them, and re-layouts: 26.1 us -> 0.3 us  [the longest x1 0.16 us: on_device(): flipped = flipped.transpose(0, 1, 4, 3, 2).reshape(3, 3, C, 3 * C)]
  transfers between devices with their start and end apart: 17 -> 12, of which waited for: 9 -> 5; matrix products, arithmetic and copies ran while one was open for 22% -> 5% of each run, Pallas kernels for 0% -> 13%
where the time goes in v1:
time: 158 us; the launch traced here: 155 us
  starting transfers between devices  53.6 us (34%)
  waiting for transfers between devices  36.7 us (23%)
  local copies, waits for them, and re-layouts  31.5 us (20%)
  Pallas kernels  29.6 us (19%)
  other arithmetic  3.03 us (2%)
    all_to_all x4, starting transfers between devices, exchange(): return lax.all_to_all(blocks, ('gy', 'gz'), 0, 0, tiled=True)  30.8 us
    unnamed x82, local copies, waits for them, and re-layouts  23.7 us
    ppermute x2, waiting for transfers between devices, halos(): zhi = lax.ppermute(first, 'gz', behind)  20.6 us
    all_to_all x4, waiting for transfers between devices, exchange(): return lax.all_to_all(blocks, ('gy', 'gz'), 0, 0, tiled=True)  14.6 us
    pallas_call x2, Pallas kernels, conv(): call(conv_kernel, (shape((YL, 128, NX), F32), shape((YL + 2, 192, NX), BF...  11.7 us
    pallas_call x3, Pallas kernels, call_indexed(): pl.pallas_call(body, out_shape=out_shape, grid_spec=pltpu.PrefetchScalarG...  10.8 us
    ppermute x2, starting transfers between devices, halos(): zlo = lax.ppermute(last, 'gz', ahead)  8.16 us
    ppermute x2, starting transfers between devices, halos(): ylo = lax.ppermute(own[YL - 1], 'gy', up)  8.02 us
  transfers between devices with their start and end apart: 12, of which 5 were waited for; matrix products, arithmetic and copies ran while one was open for 5% of the time, Pallas kernels for 13%

profile of v1, /device:TPU:1, one launch (start us, length us, event | category | flops | bytes accessed | tf_op | source)
XLA Modules:
  0.0 155.4 jit_solution(9404561379623867313)
XLA Ops:
  0.6 1.6 %fusion.2 = (bf16[1,4,32,512]{3,2,1,0:T(8,128)(2,1)S(1)}, bf16[1,4,32,512]{3,2,1,0:T(8,128)(2,1)}) fusion(bf16[8,4,32,512]{3,2,1,0:T(8,128)(2,1)} %param.11), kind=kLoop, calls=%fused_computation.16 | loop fusion | bytes 524288 | tf_op jit(solution)/shard_map/slice | solution.py:445
  2.3 4.5 %collective-permute-start = (bf16[128,512]{1,0:T(8,128)(2,1)}, bf16[128,512]{1,0:T(8,128)(2,1)S(1)}, u32[]{:S(2)}, u32[]{:S(2)}) collective-permute-start(bf16[128,512]{1,0:T(8,128)(2,1)} %bitcast.3), channel_id=1, source_target_pairs={{0,16},{16,32},{32,48},{48,64},{64,80},{80,96},{96,112},{1,17},{17... | collective-permute-start | bytes 393224 | tf_op jit(solution)/shard_map/ppermute | solution.py:444
  6.8 1.9 %collective-permute-start.1 = (bf16[128,512]{1,0:T(8,128)(2,1)S(1)}, bf16[128,512]{1,0:T(8,128)(2,1)S(1)}, u32[]{:S(2)}, u32[]{:S(2)}) collective-permute-start(bf16[128,512]{1,0:T(8,128)(2,1)S(1)} %bitcast.39), channel_id=1, source_target_pairs={{16,0},{32,16},{48,32},{64,48},{80,64},{96,80},{112,96},{17,1},{33... | collective-permute-start | bytes 393224 | tf_op jit(solution)/shard_map/ppermute | solution.py:445
  8.7 0.0 copy-start.1
  8.7 1.2 copy-done.1
  9.9 1.2 copy-done.3
  11.2 0.8 copy-done.16
  12.0 1.5 shard_map.138
  13.6 10.6 %all-to-all-start = ((bf16[128,16,128]{2,1,0:T(8,128)(2,1)}), bf16[128,16,128]{2,1,0:T(8,128)(2,1)S(1)}, u32[]{:S(2)}, u32[]{:S(2)}) async-start(bf16[128,16,128]{2,1,0:T(8,128)(2,1)} %shard_map.138), calls=%async_computation | async-start | bytes 1048576 | tf_op jit(solution)/shard_map/all_to_all | solution.py:438
  24.3 0.6 slice_bitcast_fusion.7
  24.9 0.7 slice_bitcast_fusion.6
  25.6 0.8 pad_maximum_fusion
  26.3 4.0 %collective-permute-start.2 = (bf16[10,32,512]{2,1,0:T(8,128)(2,1)}, bf16[10,32,512]{2,1,0:T(8,128)(2,1)}, u32[]{:S(2)}, u32[]{:S(2)}) collective-permute-start(bf16[10,32,512]{2,1,0:T(8,128)(2,1)} %pad_maximum_fusion), channel_id=1, source_target_pairs={{0,1},{1,2},{2,3},{3,4},{4,5},{5,6},{6,7},{7,8},{8,9},{9,10},{10,1... | collective-permute-start | bytes 983048 | tf_op jit(solution)/shard_map/ppermute | solution.py:450
  30.4 7.9 %all-to-all-done.recv_ref = bf16[128,16,128]{2,1,0:T(8,128)(2,1)S(1)} async-done(((bf16[128,16,128]{2,1,0:T(8,128)(2,1)}), bf16[128,16,128]{2,1,0:T(8,128)(2,1)S(1)}, u32[]{:S(2)}, u32[]{:S(2)}) %all-to-all-start) | async-done | bytes 524320 | tf_op jit(solution)/shard_map/all_to_all | solution.py:438
  38.3 2.3 %shard_map.139 = (bf16[128,16,128]{2,1,0:T(8,128)(2,1)}, f32[128,128]{1,0:T(8,128)S(1)}) custom-call(bf16[128,16,128]{2,1,0:T(8,128)(2,1)S(1)} %all-to-all-done.recv_ref, bf16[64,8192]{1,0:T(8,128)(2,1)S(1)} %bitcast.31, bf16[2,128,256]{2,1,0:T(8,128)(2,1)S(1)} %copy-done.9, bf16[2,256,128]{2,1,0:T(8,128)(2,1)S(1)} %copy-done.10), custom_call_target="tpu_custom_call" | custom-call | flops 134217728 | bytes 2097152 | tf_op jit(solution)/shard_map/pallas_call | solution.py:489
  40.6 5.1 %all-to-all-start.1 = ((bf16[128,16,128]{2,1,0:T(8,128)(2,1)}), bf16[128,16,128]{2,1,0:T(8,128)(2,1)}, u32[]{:S(2)}, u32[]{:S(2)}) async-start(bf16[128,16,128]{2,1,0:T(8,128)(2,1)} %get-tuple-element.16), calls=%async_computation.1 | async-start | bytes 1048576 | tf_op jit(solution)/shard_map/all_to_all | solution.py:438
  45.7 1.6 pad_maximum_fusion.1
  47.2 1.3 collective-permute-start.3
  48.5 0.7 reshape_tile.4.bias_ref
  49.3 11.3 %collective-permute-done.3.zhi_ref = bf16[10,32,512]{2,1,0:T(8,128)(2,1)} collective-permute-done((bf16[10,32,512]{2,1,0:T(8,128)(2,1)}, bf16[10,32,512]{2,1,0:T(8,128)(2,1)}, u32[]{:S(2)}, u32[]{:S(2)}) %collective-permute-start.3) | collective-permute-done | bytes 327712 | tf_op jit(solution)/shard_map/ppermute | solution.py:451
  60.5 0.8 copy-done.20
  61.4 0.9 copy-done.22
  62.3 0.9 copy-done.24
  63.2 6.1 %shard_map.140 = (f32[8,128,512]{2,1,0:T(8,128)S(1)}, bf16[10,192,512]{2,1,0:T(8,128)(2,1)S(1)}) custom-call(bf16[8,128,512]{2,1,0:T(8,128)(2,1)S(1)} %bitcast.35, bf16[128,512]{1,0:T(8,128)(2,1)S(1)} %copy-done.22, bf16[128,512]{1,0:T(8,128)(2,1)S(1)} %copy-done.24, bf16[10,32,512]{2,1,0:T(8,128)(2,1)} %collective-permute-done.2.zlo_ref, ...), custom_call_target="tpu_custom_call" | custom-call | flops 1811939328 | bytes 6291456 | tf_op jit(solution)/shard_map/pallas_call | solution.py:460
  69.3 1.3 copy-done.34
  70.6 1.3 copy-done.36
  71.9 1.0 copy-done.11
  72.9 0.9 copy-done.13
  73.9 0.8 copy-done.17
  74.7 1.2 copy-done.29
  75.9 1.6 %copy-done.35 = f32[8,128,512]{2,1,0:T(8,128)S(1)} copy-done((f32[8,128,512]{2,1,0:T(8,128)S(1)}, f32[8,128,512]{2,1,0:T(8,128)}, u32[]{:S(2)}) %copy-start.35) | copy-done | bytes 2097176
  77.5 1.5 copy-done.37
  79.1 7.3 %shard_map.141 = (bf16[8,128,512]{2,1,0:T(8,128)(2,1)S(1)}, bf16[128,24,128]{2,1,0:T(8,128)(2,1)S(1)}) custom-call(s32[1]{0:T(128)} %bitcast.idx_ref, bf16[128,16,128]{2,1,0:T(8,128)(2,1)} %all-to-all-done.1.recv_ref, f32[8,128,512]{2,1,0:T(8,128)S(1)} %copy-done.35, bf16[8,128,512]{2,1,0:T(8,128)(2,1)S(1)} %bitcast.36, ...), custom_call_target="tpu_custom_call" | custom-call | flops 2147483648 | bytes 8388608 | tf_op jit(solution)/shard_map/pallas_call | solution.py:422
  86.3 0.0 copy-start.5
  86.3 0.9 copy-done.5
  87.2 1.0 copy-done.6
  88.2 10.4 %all-to-all-start.2 = ((bf16[128,24,128]{2,1,0:T(8,128)(2,1)}), bf16[128,24,128]{2,1,0:T(8,128)(2,1)S(1)}, u32[]{:S(2)}, u32[]{:S(2)}) async-start(bf16[128,24,128]{2,1,0:T(8,128)(2,1)} %copy-done.5), calls=%async_computation.2 | async-start | bytes 1572864 | tf_op jit(solution)/shard_map/all_to_all | solution.py:438
  98.6 1.6 %slice_bitcast_fusion = (bf16[128,512]{1,0:T(8,128)(2,1)}, bf16[128,512]{1,0:T(8,128)(2,1)S(1)}) fusion(bf16[8,128,512]{2,1,0:T(8,128)(2,1)} %copy-done.6), kind=kLoop, calls=%fused_computation.4 | loop fusion | bytes 524288 | tf_op jit(solution)/shard_map/squeeze | solution.py:445
  100.3 3.5 %collective-permute-start.4 = (bf16[128,512]{1,0:T(8,128)(2,1)S(1)}, bf16[128,512]{1,0:T(8,128)(2,1)S(1)}, u32[]{:S(2)}, u32[]{:S(2)}) collective-permute-start(bf16[128,512]{1,0:T(8,128)(2,1)S(1)} %get-tuple-element.31), channel_id=1, source_target_pairs={{0,16},{16,32},{32,48},{48,64},{64,80},{80,96},{96,112},{1,17},{17... | collective-permute-start | bytes 393224 | tf_op jit(solution)/shard_map/ppermute | solution.py:444
  103.8 2.1 %collective-permute-start.5 = (bf16[128,512]{1,0:T(8,128)(2,1)}, bf16[128,512]{1,0:T(8,128)(2,1)S(1)}, u32[]{:S(2)}, u32[]{:S(2)}) collective-permute-start(bf16[128,512]{1,0:T(8,128)(2,1)} %get-tuple-element.30), channel_id=1, source_target_pairs={{16,0},{32,16},{48,32},{64,48},{80,64},{96,80},{112,96},{17,1},{33... | collective-permute-start | bytes 393224 | tf_op jit(solution)/shard_map/ppermute | solution.py:445
  105.9 0.9 fusion
  106.8 1.5 collective-permute-done.4.ylo_ref
  108.3 6.7 %all-to-all-done.2.recv_ref = bf16[128,24,128]{2,1,0:T(8,128)(2,1)S(1)} async-done(((bf16[128,24,128]{2,1,0:T(8,128)(2,1)}), bf16[128,24,128]{2,1,0:T(8,128)(2,1)S(1)}, u32[]{:S(2)}, u32[]{:S(2)}) %all-to-all-start.2) | async-done | bytes 786464 | tf_op jit(solution)/shard_map/all_to_all | solution.py:438
  115.0 3.0 %shard_map.142 = (bf16[128,24,128]{2,1,0:T(8,128)(2,1)}, f32[128,128]{1,0:T(8,128)S(1)}) custom-call(bf16[128,24,128]{2,1,0:T(8,128)(2,1)S(1)} %all-to-all-done.2.recv_ref, bf16[64,8192]{1,0:T(8,128)(2,1)S(1)} %bitcast.32, bf16[2,128,256]{2,1,0:T(8,128)(2,1)S(1)} %copy-done.9, bf16[2,256,128]{2,1,0:T(8,128)(2,1)S(1)} %copy-done.10), custom_call_target="tpu_custom_call" | custom-call | flops 134217728 | bytes 2097152 | tf_op jit(solution)/shard_map/pallas_call | solution.py:513
  118.0 4.7 %all-to-all-start.3 = ((bf16[128,24,128]{2,1,0:T(8,128)(2,1)}), bf16[128,24,128]{2,1,0:T(8,128)(2,1)S(1)}, u32[]{:S(2)}, u32[]{:S(2)}) async-start(bf16[128,24,128]{2,1,0:T(8,128)(2,1)} %get-tuple-element.20), calls=%async_computation.3 | async-start | bytes 1572864 | tf_op jit(solution)/shard_map/all_to_all | solution.py:438
  122.7 0.6 copy-done.27
  123.3 1.3 collective-permute-start.7
  124.6 0.0 copy-start.28
  124.7 4.1 %collective-permute-start.6 = (bf16[10,32,512]{2,1,0:T(8,128)(2,1)S(1)}, bf16[10,32,512]{2,1,0:T(8,128)(2,1)S(1)}, u32[]{:S(2)}, u32[]{:S(2)}) collective-permute-start(bf16[10,32,512]{2,1,0:T(8,128)(2,1)S(1)} %pad_maximum_fusion.2), channel_id=1, source_target_pairs={{0,1},{1,2},{2,3},{3,4},{4,5},{5,6},{6,7},{7,8},{8,9},{9,10},{10,1... | collective-permute-start | bytes 983048 | tf_op jit(solution)/shard_map/ppermute | solution.py:450
  128.8 0.1 reshape.46
  129.0 1.0 rev.3
  129.9 0.2 copy.18
  130.2 0.2 reshape.47.kernel_ref
  130.4 9.3 %collective-permute-done.7.zhi_ref = bf16[10,32,512]{2,1,0:T(8,128)(2,1)S(1)} collective-permute-done((bf16[10,32,512]{2,1,0:T(8,128)(2,1)S(1)}, bf16[10,32,512]{2,1,0:T(8,128)(2,1)S(1)}, u32[]{:S(2)}, u32[]{:S(2)}) %collective-permute-start.7) | collective-permute-done | bytes 327712 | tf_op jit(solution)/shard_map/ppermute | solution.py:451
  139.7 0.7 copy-done.30
  140.4 0.7 copy-done.32
  141.2 1.2 copy-done.8
  142.4 1.0 copy-done.31
  143.4 1.0 copy-done.33
  144.3 5.6 %shard_map.143 = (f32[8,128,512]{2,1,0:T(8,128)S(1)}, bf16[10,192,512]{2,1,0:T(8,128)(2,1)}) custom-call(bf16[8,128,512]{2,1,0:T(8,128)(2,1)S(1)} %copy-done.8, bf16[128,512]{1,0:T(8,128)(2,1)S(1)} %copy-done.26, bf16[128,512]{1,0:T(8,128)(2,1)S(1)} %copy-done.28, bf16[10,32,512]{2,1,0:T(8,128)(2,1)S(1)} %copy-done.33, bf16[10,32,512]{2,1,0:T(8,128)(2,1)S(1)} %copy-done.31, ...), custom_call_target="tpu_custom_call" | custom-call | flops 1811939328 | bytes 6291456 | tf_op jit(solution)/shard_map/pallas_call | solution.py:460
  150.0 1.9 %shard_map.145 = f32[64,8192]{1,0:T(8,128)} custom-call(f32[128,128]{1,0:T(8,128)S(1)} %get-tuple-element.24.spec_ref, f32[128,128]{1,0:T(8,128)S(1)} %copy-done.19), custom_call_target="tpu_custom_call" | custom-call | flops 134217728 | bytes 3145728 | tf_op jit(solution)/shard_map/pallas_call | solution.py:521
  151.9 0.9 copy-done.14
  152.8 2.0 %shard_map.144 = (bf16[8,128,512]{2,1,0:T(8,128)(2,1)}, f32[3,3,32,96]{3,2,1,0:T(8,128)}, f32[32,1]{1,0:T(8,128)S(1)}) custom-call(s32[1]{0:T(128)} %bitcast.idx_ref, bf16[128,24,128]{2,1,0:T(8,128)(2,1)S(1)} %all-to-all-done.3.recv_ref, f32[8,128,512]{2,1,0:T(8,128)S(1)} %get-tuple-element.22.conv_ref, bf16[8,128,256]{2,1,0:T(8,128)(2,1)S(1)} %copy-done.12, ...), custom_call_target="tpu_custom_call" | custom-call | flops 268435456 | bytes 4194304 | tf_op jit(solution)/shard_map/pallas_call | solution.py:422
  154.8 0.6 reduce
  (70 shorter events, 0.3 us)
Async XLA Ops:
  2.3 22.0 %collective-permute-start = (bf16[128,512]{1,0:T(8,128)(2,1)}, bf16[128,512]{1,0:T(8,128)(2,1)S(1)}, u32[]{:S(2)}, u32[]{:S(2)}) collective-permute-start(bf16[128,512]{1,0:T(8,128)(2,1)} %bitcast.3), channel_id=1, source_target_pairs={{0,16},{16,32},{32,48},{48,64},{64,80},{80,96},{96,112},{1,17},{17... | collective-permute-start | bytes 393224 | tf_op jit(solution)/shard_map/ppermute | solution.py:444
  6.8 18.1 %collective-permute-start.1 = (bf16[128,512]{1,0:T(8,128)(2,1)S(1)}, bf16[128,512]{1,0:T(8,128)(2,1)S(1)}, u32[]{:S(2)}, u32[]{:S(2)}) collective-permute-start(bf16[128,512]{1,0:T(8,128)(2,1)S(1)} %bitcast.39), channel_id=1, source_target_pairs={{16,0},{32,16},{48,32},{64,48},{80,64},{96,80},{112,96},{17,1},{33... | collective-permute-start | bytes 393224 | tf_op jit(solution)/shard_map/ppermute | solution.py:445
  8.7 1.2 copy-start.1
  9.9 1.2 copy-start.3
  11.2 0.8 copy-start.16
  12.0 12.2 %copy-start.2 = (bf16[8,4,32,512]{3,2,1,0:T(8,128)(2,1)S(1)}, bf16[8,4,32,512]{3,2,1,0:T(8,128)(2,1)}, u32[]{:S(2)}) copy-start(bf16[8,4,32,512]{3,2,1,0:T(8,128)(2,1)} %param.11) | copy-start | bytes 3145732
  13.6 24.7 %copy-start = (bf16[2,32,8192]{2,1,0:T(8,128)(2,1)S(1)}, bf16[2,32,8192]{2,1,0:T(8,128)(2,1)}, u32[]{:S(2)}) copy-start(bf16[2,32,8192]{2,1,0:T(8,128)(2,1)} %param.13) | copy-start | bytes 3145732
  13.6 24.7 %copy-start.9 = (bf16[2,128,256]{2,1,0:T(8,128)(2,1)S(1)}, bf16[2,128,256]{2,1,0:T(8,128)(2,1)}, u32[]{:S(2)}) copy-start(bf16[2,128,256]{2,1,0:T(8,128)(2,1)} %constant.24.clone.tzf_ref) | copy-start | bytes 393220
  13.6 24.7 %copy-start.10 = (bf16[2,256,128]{2,1,0:T(8,128)(2,1)S(1)}, bf16[2,256,128]{2,1,0:T(8,128)(2,1)}, u32[]{:S(2)}) copy-start(bf16[2,256,128]{2,1,0:T(8,128)(2,1)} %constant.25.clone.tzi_ref) | copy-start | bytes 393220
  13.6 24.7 %all-to-all-start = ((bf16[128,16,128]{2,1,0:T(8,128)(2,1)}), bf16[128,16,128]{2,1,0:T(8,128)(2,1)S(1)}, u32[]{:S(2)}, u32[]{:S(2)}) async-start(bf16[128,16,128]{2,1,0:T(8,128)(2,1)} %shard_map.138), calls=%async_computation | async-start | bytes 1048576 | tf_op jit(solution)/shard_map/all_to_all | solution.py:438
  24.3 22.9 %copy-start.21 = (bf16[128,512]{1,0:T(8,128)(2,1)}, bf16[128,512]{1,0:T(8,128)(2,1)S(1)}, u32[]{:S(2)}) copy-start(bf16[128,512]{1,0:T(8,128)(2,1)S(1)} %collective-permute-done.ylo_ref) | copy-start | bytes 393220
  24.9 22.3 %copy-start.23 = (bf16[128,512]{1,0:T(8,128)(2,1)}, bf16[128,512]{1,0:T(8,128)(2,1)S(1)}, u32[]{:S(2)}) copy-start(bf16[128,512]{1,0:T(8,128)(2,1)S(1)} %collective-permute-done.1.yhi_ref) | copy-start | bytes 393220
  25.6 22.9 %copy-start.40 = (f32[32]{0:T(128)S(1)}, f32[32]{0:T(128)}, u32[]{:S(2)}) copy-start(f32[32]{0:T(128)} %param.15) | copy-start | bytes 388
  25.6 34.9 %copy-start.15 = (bf16[3,3,32,96]{3,2,1,0:T(8,128)(2,1)S(1)}, bf16[3,3,32,96]{3,2,1,0:T(8,128)(2,1)}, u32[]{:S(2)}) copy-start(bf16[3,3,32,96]{3,2,1,0:T(8,128)(2,1)} %kernel_ref.1) | copy-start | bytes 165892
  26.3 22.9 %collective-permute-start.2 = (bf16[10,32,512]{2,1,0:T(8,128)(2,1)}, bf16[10,32,512]{2,1,0:T(8,128)(2,1)}, u32[]{:S(2)}, u32[]{:S(2)}) collective-permute-start(bf16[10,32,512]{2,1,0:T(8,128)(2,1)} %pad_maximum_fusion), channel_id=1, source_target_pairs={{0,1},{1,2},{2,3},{3,4},{4,5},{5,6},{6,7},{7,8},{8,9},{9,10},{10,1... | collective-permute-start | bytes 983048 | tf_op jit(solution)/shard_map/ppermute | solution.py:450
  40.6 31.3 %all-to-all-start.1 = ((bf16[128,16,128]{2,1,0:T(8,128)(2,1)}), bf16[128,16,128]{2,1,0:T(8,128)(2,1)}, u32[]{:S(2)}, u32[]{:S(2)}) async-start(bf16[128,16,128]{2,1,0:T(8,128)(2,1)} %get-tuple-element.16), calls=%async_computation.1 | async-start | bytes 1048576 | tf_op jit(solution)/shard_map/all_to_all | solution.py:438
  47.2 13.3 %collective-permute-start.3 = (bf16[10,32,512]{2,1,0:T(8,128)(2,1)}, bf16[10,32,512]{2,1,0:T(8,128)(2,1)}, u32[]{:S(2)}, u32[]{:S(2)}) collective-permute-start(bf16[10,32,512]{2,1,0:T(8,128)(2,1)} %pad_maximum_fusion.1), channel_id=1, source_target_pairs={{1,0},{2,1},{3,2},{4,3},{5,4},{6,5},{7,6},{8,7},{9,8},{10,9},{11,1... | collective-permute-start | bytes 983048 | tf_op jit(solution)/shard_map/ppermute | solution.py:451
  49.3 22.6 %copy-start.4 = (bf16[8,256,192]{2,1,0:T(8,128)(2,1)S(1)}, bf16[8,256,192]{2,1,0:T(8,128)(2,1)}, u32[]{:S(2)}) copy-start(bf16[8,256,192]{2,1,0:T(8,128)(2,1)} %constant.22.clone.ty_ref) | copy-start | bytes 2359300
  60.5 0.8 copy-start.20
  61.4 0.9 copy-start.22
  62.3 0.9 copy-start.24
  69.2 1.3 copy-start.34
  70.6 1.3 copy-start.36
  71.9 1.0 copy-start.11
  72.9 0.9 copy-start.13
  73.9 0.8 copy-start.17
  74.7 1.2 copy-start.29
  75.9 1.6 %copy-start.35 = (f32[8,128,512]{2,1,0:T(8,128)S(1)}, f32[8,128,512]{2,1,0:T(8,128)}, u32[]{:S(2)}) copy-start(f32[8,128,512]{2,1,0:T(8,128)} %copy-done.34) | copy-start | bytes 6291460
  77.5 1.5 copy-start.37
  86.3 0.9 copy-start.5
  87.2 1.0 copy-start.6
  88.2 17.7 %copy-start.7 = (bf16[8,128,512]{2,1,0:T(8,128)(2,1)S(1)}, bf16[8,128,512]{2,1,0:T(8,128)(2,1)}, u32[]{:S(2)}) copy-start(bf16[8,128,512]{2,1,0:T(8,128)(2,1)} %copy-done.6) | copy-start | bytes 3145732
  88.2 26.8 %all-to-all-start.2 = ((bf16[128,24,128]{2,1,0:T(8,128)(2,1)}), bf16[128,24,128]{2,1,0:T(8,128)(2,1)S(1)}, u32[]{:S(2)}, u32[]{:S(2)}) async-start(bf16[128,24,128]{2,1,0:T(8,128)(2,1)} %copy-done.5), calls=%async_computation.2 | async-start | bytes 1572864 | tf_op jit(solution)/shard_map/all_to_all | solution.py:438
  100.3 8.0 %collective-permute-start.4 = (bf16[128,512]{1,0:T(8,128)(2,1)S(1)}, bf16[128,512]{1,0:T(8,128)(2,1)S(1)}, u32[]{:S(2)}, u32[]{:S(2)}) collective-permute-start(bf16[128,512]{1,0:T(8,128)(2,1)S(1)} %get-tuple-element.31), channel_id=1, source_target_pairs={{0,16},{16,32},{32,48},{48,64},{64,80},{80,96},{96,112},{1,17},{17... | collective-permute-start | bytes 393224 | tf_op jit(solution)/shard_map/ppermute | solution.py:444
  103.8 18.8 %collective-permute-start.5 = (bf16[128,512]{1,0:T(8,128)(2,1)}, bf16[128,512]{1,0:T(8,128)(2,1)S(1)}, u32[]{:S(2)}, u32[]{:S(2)}) collective-permute-start(bf16[128,512]{1,0:T(8,128)(2,1)} %get-tuple-element.30), channel_id=1, source_target_pairs={{16,0},{32,16},{48,32},{64,48},{80,64},{96,80},{112,96},{17,1},{33... | collective-permute-start | bytes 393224 | tf_op jit(solution)/shard_map/ppermute | solution.py:445
  106.8 15.9 %copy-start.39 = (bf16[8,32,512]{2,1,0:T(8,128)(2,1)S(1)}, bf16[8,32,512]{2,1,0:T(8,128)(2,1)}, u32[]{:S(2)}) copy-start(bf16[8,32,512]{2,1,0:T(8,128)(2,1)} %get-tuple-element.28) | copy-start | bytes 786436
  108.3 14.4 %copy-start.25 = (bf16[128,512]{1,0:T(8,128)(2,1)}, bf16[128,512]{1,0:T(8,128)(2,1)S(1)}, u32[]{:S(2)}) copy-start(bf16[128,512]{1,0:T(8,128)(2,1)S(1)} %collective-permute-done.4.ylo_ref) | copy-start | bytes 393220
  108.3 16.3 %copy-start.38 = (bf16[8,32,512]{2,1,0:T(8,128)(2,1)S(1)}, bf16[8,32,512]{2,1,0:T(8,128)(2,1)}, u32[]{:S(2)}) copy-start(bf16[8,32,512]{2,1,0:T(8,128)(2,1)} %get-tuple-element.29) | copy-start | bytes 786436
  118.0 12.2 %copy-start.18 = (f32[128,128]{1,0:T(8,128)}, f32[128,128]{1,0:T(8,128)S(1)}, u32[]{:S(2)}) copy-start(f32[128,128]{1,0:T(8,128)S(1)} %get-tuple-element.25.back_ref) | copy-start | bytes 196612
  118.0 33.9 %all-to-all-start.3 = ((bf16[128,24,128]{2,1,0:T(8,128)(2,1)}), bf16[128,24,128]{2,1,0:T(8,128)(2,1)S(1)}, u32[]{:S(2)}, u32[]{:S(2)}) async-start(bf16[128,24,128]{2,1,0:T(8,128)(2,1)} %get-tuple-element.20), calls=%async_computation.3 | async-start | bytes 1572864 | tf_op jit(solution)/shard_map/all_to_all | solution.py:438
  122.6 0.7 copy-start.27
  123.3 16.4 %collective-permute-start.7 = (bf16[10,32,512]{2,1,0:T(8,128)(2,1)S(1)}, bf16[10,32,512]{2,1,0:T(8,128)(2,1)S(1)}, u32[]{:S(2)}, u32[]{:S(2)}) collective-permute-start(bf16[10,32,512]{2,1,0:T(8,128)(2,1)S(1)} %pad_maximum_fusion.3), channel_id=1, source_target_pairs={{1,0},{2,1},{3,2},{4,3},{5,4},{6,5},{7,6},{8,7},{9,8},{10,9},{11,1... | collective-permute-start | bytes 983048 | tf_op jit(solution)/shard_map/ppermute | solution.py:451
  124.6 16.6 %copy-start.26 = (bf16[128,512]{1,0:T(8,128)(2,1)S(1)}, bf16[128,512]{1,0:T(8,128)(2,1)}, u32[]{:S(2)}) copy-start(bf16[128,512]{1,0:T(8,128)(2,1)} %copy-done.25) | copy-start | bytes 393220
  124.6 16.6 %copy-start.28 = (bf16[128,512]{1,0:T(8,128)(2,1)S(1)}, bf16[128,512]{1,0:T(8,128)(2,1)}, u32[]{:S(2)}) copy-start(bf16[128,512]{1,0:T(8,128)(2,1)} %copy-done.27) | copy-start | bytes 393220
  124.7 15.7 %collective-permute-start.6 = (bf16[10,32,512]{2,1,0:T(8,128)(2,1)S(1)}, bf16[10,32,512]{2,1,0:T(8,128)(2,1)S(1)}, u32[]{:S(2)}, u32[]{:S(2)}) collective-permute-start(bf16[10,32,512]{2,1,0:T(8,128)(2,1)S(1)} %pad_maximum_fusion.2), channel_id=1, source_target_pairs={{0,1},{1,2},{2,3},{3,4},{4,5},{5,6},{6,7},{7,8},{8,9},{9,10},{10,1... | collective-permute-start | bytes 983048 | tf_op jit(solution)/shard_map/ppermute | solution.py:450
  139.7 0.7 copy-start.30
  140.4 0.7 copy-start.32
  141.2 1.2 copy-start.8
  142.4 1.0 copy-start.31
  143.4 1.0 copy-start.33
  144.3 5.7 %copy-start.19 = (f32[128,128]{1,0:T(8,128)S(1)}, f32[128,128]{1,0:T(8,128)}, u32[]{:S(2)}) copy-start(f32[128,128]{1,0:T(8,128)} %copy-done.18) | copy-start | bytes 196612
  150.0 1.9 %copy-start.12 = (bf16[8,128,256]{2,1,0:T(8,128)(2,1)S(1)}, bf16[8,128,256]{2,1,0:T(8,128)(2,1)}, u32[]{:S(2)}) copy-start(bf16[8,128,256]{2,1,0:T(8,128)(2,1)} %constant.23.clone.tyi_ref) | copy-start | bytes 1572868
  151.9 0.9 copy-start.14

commit v2 on v1

v2 whole, which is shorter than its diff:
```python
import functools
import math

import jax
import jax.numpy as jnp
import ml_dtypes
import numpy as np
from jax import lax
from jax.experimental import pallas as pl
from jax.experimental.pallas import tpu as pltpu
from jax.sharding import PartitionSpec as P

NX, NY, NZ = 512, 64, 64
C = 32
GY, GZ = 8, 16
YL, ZL = 8, 4
KXL = 4
LINE_ROWS = 64
MODE_ROWS = 16
GRAD_ROWS = 32
TAIL_ROWS = 8
SCALE = 1.0 / math.sqrt(NX * NY * NZ)
F32, BF16 = jnp.float32, jnp.bfloat16
LARGE = 60 * 1024 * 1024
SMALL = 16 * 1024 * 1024


def freqs(count, length):
    index = np.arange(count)
    return np.where(index < count // 2, index, length - count + index)


def angle(a, b, length):
    return 2.0 * math.pi / length * ((a[:, None] * b[None, :]) % length)


def split_np(table):
    high = table.astype(ml_dtypes.bfloat16)
    low = (table - high.astype(np.float64)).astype(ml_dtypes.bfloat16)
    return high, low


def x_forward_table():
    turn = angle(np.arange(32), np.arange(NX), NX)
    both = np.stack([np.cos(turn), -np.sin(turn)], 0).reshape(2, GY, KXL, NX)
    return both.transpose(1, 0, 2, 3).reshape(64, NX).astype(ml_dtypes.bfloat16)


def x_inverse_table():
    turn = angle(np.arange(32), np.arange(NX), NX)
    both = np.stack([np.cos(turn), -np.sin(turn)], 1).reshape(64, NX)
    high, low = split_np(both)
    return np.concatenate([high, low, high], 0)


def rotation(turn, sign):
    cos, sin = np.cos(turn), sign * np.sin(turn)
    return np.stack([np.stack([cos, -sin], -1), np.stack([sin, cos], -1)], 1)


def y_forward_table():
    turn = angle(freqs(32, NY), np.arange(NY), NY)
    table = rotation(turn, -1.0).reshape(GZ, 2, 2, NY, 2)
    full = np.einsum("gkpyq,ab->gakpyqb", table, np.eye(KXL)).reshape(256, 512)
    return np.stack(split_np(full))


def z_forward_table():
    turn = angle(freqs(32, NZ), np.arange(NZ), NZ)
    table = SCALE * rotation(turn, -1.0).reshape(32, 2, GZ, ZL, 2)
    full = np.einsum("kpgzq,ab->pakzbqg", table, np.eye(2)).reshape(128, 256)
    return np.stack(split_np(full))


def z_inverse_table():
    turn = angle(np.arange(NZ), freqs(32, NZ), NZ)
    table = SCALE * rotation(turn, 1.0).reshape(GZ, ZL, 2, 32, 2)
    full = np.einsum("gzpkq,ab->gapzqbk", table, np.eye(2)).reshape(256, 128)
    return np.stack(split_np(full))


def y_inverse_table():
    turn = angle(np.arange(NY), freqs(32, NY), NY)
    table = rotation(turn, 1.0).reshape(GY, YL, 2, GZ, 2, 2)
    full = np.einsum("dypgkq,ab->dapygkqb", table, np.eye(ZL)).reshape(512, 256)
    return np.stack(split_np(full))


def split(value):
    high = value.astype(BF16)
    return high, (value - high.astype(F32)).astype(BF16)


def dot(a, b):
    return jnp.dot(a, b, preferred_element_type=F32)


def dot_nt(a, b):
    return lax.dot_general(a, b, (((1,), (1,)), ((), ())), preferred_element_type=F32)


def dot_tn(a, b):
    return lax.dot_general(a, b, (((0,), (0,)), ((), ())), preferred_element_type=F32)


def lane_of(shape):
    return lax.broadcasted_iota(jnp.int32, shape, len(shape) - 1)


def swap_blocks(parts):
    lane = lane_of(parts[0].shape)
    half = lane < 64
    p0, p1, p2, p3 = parts
    q0 = jnp.where(half, p0, pltpu.roll(p2, 64, 1))
    q2 = jnp.where(half, pltpu.roll(p0, 64, 1), p2)
    q1 = jnp.where(half, p1, pltpu.roll(p3, 64, 1))
    q3 = jnp.where(half, pltpu.roll(p1, 64, 1), p3)
    even = (lane & 32) == 0
    out = []
    for lo, hi in ((q0, q1), (q2, q3)):
        out.append(jnp.where(even, lo, pltpu.roll(hi, 32, 1)))
        out.append(jnp.where(even, pltpu.roll(lo, 96, 1), hi))
    return out


def pack_lines(lines, send_ref):
    for g in range(GY):
        block = jnp.concatenate([line[g * 8 : g * 8 + 8] for line in lines], 0)
        send_ref[g, 0:LINE_ROWS] = block.astype(BF16)


def collect_spectrum(recv_ref, table_ref, rows_ref):
    rows_ref[...] = recv_ref[:, 0:MODE_ROWS].astype(F32).reshape(256, 128)
    turned = []
    for j in range(4):
        turned.append(
            swap_blocks([rows_ref[pl.ds(k * 4 + j, GZ, stride=16), :] for k in range(KXL)])
        )
    joined = jnp.concatenate([turned[j][z] for z in range(ZL) for j in range(4)], 0).astype(BF16)
    return dot(table_ref[0], joined) + dot(table_ref[1], joined)


def z_inverse(modes, table_ref):
    high, low = split(modes)
    return dot(table_ref[0], high) + dot(table_ref[1], high) + dot(table_ref[0], low)


def gain_lanes():
    lane = lane_of((128, 128))
    first = jnp.logical_and(lane < 32, lax.axis_index("gy") == 0)
    return jnp.where(first, 1.0, 2.0).astype(F32)


def repeat_matrix():
    row = lax.broadcasted_iota(jnp.int32, (64, 1024), 0) & 31
    return jnp.where(row == lane_of((64, 1024)) // 32, 1.0, 0.0).astype(BF16)


def spread(spectrum, k, matrix):
    high, low = split(spectrum[:, k * 32 : k * 32 + 32])
    return dot(jnp.concatenate([high, low], 1), matrix)


def fold_tiles(value):
    total = value[:, 0:128]
    for t in range(1, 8):
        total = total + value[:, t * 128 : t * 128 + 128]
    total = total + pltpu.roll(total, 64, 1)
    return total + pltpu.roll(total, 32, 1)


def place_fields(recv_ref, field_ref):
    for g in range(GY):
        block = recv_ref[g, 0:LINE_ROWS].astype(F32)
        turned = swap_blocks([block[z * 16 : z * 16 + 16] for z in range(ZL)])
        for k in range(KXL):
            for part in range(2):
                field_ref[pl.ds((g * 4 + k) * 2 + part, YL, stride=64), :] = turned[k][
                    part * 8 : part * 8 + 8
                ]


def x_inverse(field, table):
    high, low = split(field)
    return dot_tn(jnp.concatenate([high, high, low], 0), table)


def shift_right(value):
    return jnp.where(lane_of(value.shape) == 0, 0.0, pltpu.roll(value, 1, 1))


def shift_left(value):
    return jnp.where(lane_of(value.shape) == NX - 1, 0.0, pltpu.roll(value, NX - 1, 1))


def begin(copies, sems):
    started = [pltpu.make_async_copy(src, dst, sems.at[n]) for n, (src, dst) in enumerate(copies)]
    for copy in started:
        copy.start()
    return started


def finish(copies):
    for copy in copies:
        copy.wait()


def face_copies(field, front_ref, back_ref, first_ref, last_ref):
    return [
        (field.at[:, 0:32], front_ref),
        (field.at[:, 96:128], back_ref),
        (field.at[0], first_ref),
        (field.at[YL - 1], last_ref),
    ]


def analyse_kernel(own_ref, tx_hbm, send_ref, front_ref, back_ref, first_ref, last_ref, field, tx, in_sems, out_sems):
    fetched = begin([(tx_hbm, tx)] + [(own_ref.at[y], field.at[y]) for y in range(YL)], in_sems)
    fetched[0].wait()
    lines = []
    for y in range(YL):
        fetched[1 + y].wait()
        lines.append(dot_nt(tx[...], field[y]))
    faces = begin(face_copies(field, front_ref, back_ref, first_ref, last_ref), out_sems)
    pack_lines(lines, send_ref)
    finish(faces)


def y_kernel(recv_ref, table_ref, send_ref):
    lines = recv_ref[:, 0:LINE_ROWS].reshape(512, 128)
    out = dot(table_ref[0], lines) + dot(table_ref[1], lines)
    send_ref[:, 0:MODE_ROWS] = out.astype(BF16).reshape(GZ, MODE_ROWS, 128)


def y_back_kernel(recv_ref, table_ref, send_ref, sums_ref, tail_ref):
    y_kernel(recv_ref, table_ref, send_ref)
    total = jnp.zeros((2 * GRAD_ROWS, 128), F32)
    for g in range(GY):
        total = total + recv_ref[g, LINE_ROWS : LINE_ROWS + 2 * GRAD_ROWS].astype(F32)
    sums_ref[...] = total[0:GRAD_ROWS] + total[GRAD_ROWS : 2 * GRAD_ROWS]
    tail_ref[...] = jnp.zeros_like(tail_ref)
    for r in range(2):
        rows = sums_ref[pl.ds(r, GZ, stride=2), :]
        high = rows.astype(BF16).astype(F32)
        tail_ref[pl.ds(r, GZ, stride=TAIL_ROWS), :] = high
        tail_ref[pl.ds(r + 2, GZ, stride=TAIL_ROWS), :] = rows - high
    tail = tail_ref[...].reshape(GZ, TAIL_ROWS, 128)
    send_ref[:, MODE_ROWS : MODE_ROWS + TAIL_ROWS] = tail.astype(BF16)


def spread_kernel(recv_ref, table_ref, send_ref):
    modes = recv_ref[:, 0:MODE_ROWS].reshape(256, 128)
    out = dot(table_ref[0], modes) + dot(table_ref[1], modes)
    send_ref[:, 0:LINE_ROWS] = out.astype(BF16).reshape(GY, LINE_ROWS, 128)


def spread_back_kernel(recv_ref, table_ref, send_ref, tail_ref, both_ref):
    spread_kernel(recv_ref, table_ref, send_ref)
    tail = recv_ref[:, MODE_ROWS : MODE_ROWS + TAIL_ROWS].astype(F32)
    tail_ref[...] = tail.reshape(GZ * TAIL_ROWS, 128)
    for r in range(2):
        both_ref[pl.ds(r, GZ, stride=2), :] = tail_ref[pl.ds(r, GZ, stride=TAIL_ROWS), :]
        both_ref[pl.ds(GRAD_ROWS + r, GZ, stride=2), :] = tail_ref[pl.ds(r + 2, GZ, stride=TAIL_ROWS), :]
    both = both_ref[...].astype(BF16)
    for g in range(GY):
        send_ref[g, LINE_ROWS : LINE_ROWS + 2 * GRAD_ROWS] = both


def edges_kernel(own_first_ref, own_last_ref, zlo_ref, zhi_ref, first_ref, last_ref):
    for y, own, row in ((0, own_first_ref, first_ref), (YL - 1, own_last_ref, last_ref)):
        row[0:32] = zlo_ref[y]
        row[32:160] = own[...]
        row[160:192] = zhi_ref[y]


def pad_copies(pad, own_ref, zlo_ref, zhi_ref, ylo_ref, yhi_ref):
    return [
        (own_ref, pad.at[1:9, 32:160]),
        (zlo_ref, pad.at[1:9, 0:32]),
        (zhi_ref, pad.at[1:9, 160:192]),
        (ylo_ref, pad.at[0]),
        (yhi_ref, pad.at[9]),
    ]


def mix_kernel(recv_ref, weight_ref, tzf_ref, tzi_ref, send_ref, spec_ref, rows_ref):
    spectrum = collect_spectrum(recv_ref, tzf_ref, rows_ref)
    spec_ref[...] = spectrum
    matrix = repeat_matrix()
    lane = lane_of((64, 128)) // 32
    real = jnp.zeros((64, 128), F32)
    imag = jnp.zeros((64, 128), F32)
    for k in range(KXL):
        wide = spread(spectrum, k, matrix)
        w_re = weight_ref[:, k * 2048 : k * 2048 + 1024].astype(F32)
        w_im = weight_ref[:, k * 2048 + 1024 : k * 2048 + 2048].astype(F32)
        s_re, s_im = wide[0:64], wide[64:128]
        real = jnp.where(lane == k, fold_tiles(s_re * w_re - s_im * w_im), real)
        imag = jnp.where(lane == k, fold_tiles(s_re * w_im + s_im * w_re), imag)
    modes = jnp.concatenate([real, imag], 0) * gain_lanes()
    send_ref[...] = z_inverse(modes, tzi_ref).astype(BF16).reshape(GZ, MODE_ROWS, 128)


def build_taps(kernel_ref, taps, flip):
    zero = jnp.zeros((C, C), F32)
    row = lax.broadcasted_iota(jnp.int32, (C, C), 0)
    eye = jnp.where(row == lane_of((C, C)), 1.0, 0.0).astype(BF16)
    tap = {}
    for dy in range(3):
        for dz in range(3):
            if flip:
                turned = dot_tn(kernel_ref[2 - dy, 2 - dz], eye)
                for dx in range(3):
                    tap[dx, dy, dz] = turned[(2 - dx) * C : (2 - dx) * C + C]
            else:
                whole = kernel_ref[dy, dz].astype(F32)
                for dx in range(3):
                    tap[dx, dy, dz] = whole[:, dx * C : dx * C + C]
    for dx in range(3):
        for z in range(ZL):
            parts = [
                tap[dx, dy, zin - z] if 0 <= zin - z < 3 else zero
                for dy in range(3)
                for zin in range(ZL + 2)
            ]
            row = (dx * ZL + z) * C
            taps[row : row + C, :] = jnp.concatenate(parts, 1).astype(BF16)


def conv_kernel(
    flip, own_ref, zlo_ref, zhi_ref, ylo_ref, yhi_ref, kernel_hbm, bias_hbm, out_ref,
    pad, taps, buffer, kernel_ref, bias_ref, in_sems, out_sems,
):
    fetched = begin(
        [(kernel_hbm, kernel_ref), (bias_hbm, bias_ref)]
        + pad_copies(pad, own_ref, zlo_ref, zhi_ref, ylo_ref, yhi_ref),
        in_sems,
    )
    finish(fetched[0:2])
    build_taps(kernel_ref, taps, flip)
    if not flip:
        row = lax.broadcasted_iota(jnp.int32, (128, C), 0) & 31
        picked = jnp.where(row == lane_of((128, C)), bias_ref[...], 0.0)
        bias = jnp.sum(picked, axis=1, keepdims=True)
    finish(fetched[2:])

    def step(y, carry):
        window = pad[pl.ds(y, 3)].reshape(576, NX)
        wide = dot(taps[...], window)
        total = wide[128:256] + shift_right(wide[0:128]) + shift_left(wide[256:384])
        buffer[y] = total if flip else total + bias
        pltpu.make_async_copy(buffer.at[y], out_ref.at[y], out_sems.at[y]).start()
        return carry

    lax.fori_loop(0, YL, step, 0)
    for y in range(YL):
        pltpu.make_async_copy(buffer.at[y], out_ref.at[y], out_sems.at[y]).wait()


def slope_kernel(
    recv_ref, local_ref, cot_ref, txi_hbm, slope_ref, front_ref, back_ref, first_ref, last_ref,
    recv, local, cot, txi, field_ref, slopes, in_sems, out_sems,
):
    fetched = begin(
        [(recv_ref, recv), (txi_hbm, txi)]
        + [(local_ref.at[y], local.at[y]) for y in range(YL)]
        + [(cot_ref.at[y], cot.at[y]) for y in range(YL)],
        in_sems,
    )
    fetched[0].wait()
    place_fields(recv, field_ref)
    fetched[1].wait()
    root = math.sqrt(2.0 / math.pi)
    copies = []
    for y in range(YL):
        fetched[2 + y].wait()
        fetched[2 + YL + y].wait()
        pre = x_inverse(field_ref[y * 64 : y * 64 + 64], txi[...]) + local[y]
        square = pre * pre
        bent = jnp.tanh(root * pre * (1.0 + 0.044715 * square))
        rate = 0.5 * (1.0 + bent) + 0.5 * root * pre * (1.0 - bent * bent) * (
            1.0 + 3.0 * 0.044715 * square
        )
        slopes[y] = (cot[y].astype(F32) * rate).astype(BF16)
        copies += begin([(slopes.at[y], slope_ref.at[y])], out_sems.at[y : y + 1])
    copies += begin(face_copies(slopes, front_ref, back_ref, first_ref, last_ref), out_sems.at[YL : YL + 4])
    finish(copies)


def back_kernel(
    slope_ref, own_ref, zlo_ref, zhi_ref, ylo_ref, yhi_ref, tx_hbm, send_ref,
    slopes, pad, tx, sums_ref, in_sems,
):
    fetched = begin(
        [(tx_hbm, tx)]
        + [(slope_ref.at[y], slopes.at[y]) for y in range(YL)]
        + pad_copies(pad, own_ref, zlo_ref, zhi_ref, ylo_ref, yhi_ref),
        in_sems,
    )
    sums_ref[...] = jnp.zeros_like(sums_ref)
    finish(fetched)
    lines = []
    bias = jnp.zeros((128, 1), F32)
    for y in range(YL):
        slope = slopes[y]
        lines.append(dot_nt(tx[...], slope))
        wide = slope.astype(F32)
        bias = bias + jnp.sum(wide, axis=1, keepdims=True)
        three = jnp.concatenate(
            [shift_left(wide).astype(BF16), slope, shift_right(wide).astype(BF16)], 0
        )
        sums_ref[...] += dot_nt(three, pad[y : y + 3].reshape(576, NX))
    pack_lines(lines, send_ref)
    bias32 = bias[0:32] + bias[32:64] + bias[64:96] + bias[96:128]
    pieces = []
    for dx in range(3):
        for dy in range(3):
            total = jnp.zeros((C, 96), F32)
            for z in range(ZL):
                row = (dx * ZL + z) * C
                col = dy * 192 + z * C
                total = total + sums_ref[row : row + C, col : col + 96]
            pieces += [total[:, dz * C : dz * C + C] for dz in range(3)]
    pieces.append(jnp.broadcast_to(bias32, (C, C)))
    for g in range(GY):
        if g < 7:
            rows = jnp.concatenate(pieces[4 * g : 4 * g + 4], 1)
        else:
            rows = jnp.zeros((C, 128), F32)
        high, low = split(rows)
        send_ref[g, LINE_ROWS : LINE_ROWS + GRAD_ROWS] = high
        send_ref[g, LINE_ROWS + GRAD_ROWS : LINE_ROWS + 2 * GRAD_ROWS] = low


def adjoint_kernel(recv_ref, weight_ref, tzf_ref, tzi_ref, send_ref, spec_ref, rows_ref):
    spectrum = collect_spectrum(recv_ref, tzf_ref, rows_ref)
    spec_ref[...] = spectrum
    row = lax.broadcasted_iota(jnp.int32, (1024, 128), 0) // 32
    lane = lane_of((1024, 128))
    gather = []
    for k in range(KXL):
        w_re = weight_ref[:, k * 2048 : k * 2048 + 1024].astype(F32)
        w_im = weight_ref[:, k * 2048 + 1024 : k * 2048 + 2048].astype(F32)
        own = spectrum[:, k * 32 : k * 32 + 32]
        four = jnp.concatenate([own] * 4, 1)
        wide = jnp.concatenate([four] * 8, 1)
        b_re, b_im = wide[0:64], wide[64:128]
        both = jnp.concatenate([b_re * w_re + b_im * w_im, b_im * w_re - b_re * w_im], 0)
        matrix = jnp.where(row + k * 32 == lane, 1.0, 0.0).astype(BF16)
        high, low = split(both)
        gather.append(dot(high, matrix) + dot(low, matrix))
    modes = (gather[0] + gather[1] + gather[2] + gather[3]) * gain_lanes()
    block = z_inverse(modes, tzi_ref).astype(BF16)
    send_ref[:, 0:MODE_ROWS] = block.reshape(GZ, MODE_ROWS, 128)
    total = jnp.sum(recv_ref[:, MODE_ROWS : MODE_ROWS + TAIL_ROWS].astype(F32), axis=0)
    total = total + pltpu.roll(total, TAIL_ROWS - 2, 0)
    high = total.astype(BF16).astype(F32)
    part = lax.broadcasted_iota(jnp.int32, (TAIL_ROWS, 128), 0)
    low = jnp.where(part < 4, pltpu.roll(total - high, 2, 0), 0.0)
    tail = jnp.where(part < 2, high, low).astype(BF16)
    send_ref[:, MODE_ROWS : MODE_ROWS + TAIL_ROWS] = jnp.broadcast_to(tail[None], (GZ, TAIL_ROWS, 128))


def outer_kernel(spec_ref, back_ref, out_hbm, out_ref, sems):
    copies = []
    matrix = repeat_matrix()
    gain = gain_lanes()
    spectrum = spec_ref[...]
    back = back_ref[...] * gain
    for k in range(KXL):
        wide = spread(spectrum, k, matrix)
        s_re, s_im = wide[0:64], wide[64:128]
        own = back[:, k * 32 : k * 32 + 32]
        four = jnp.concatenate([own] * 4, 1)
        tiled = jnp.concatenate([four] * 8, 1)
        b_re, b_im = tiled[0:64], tiled[64:128]
        out_ref[:, k * 2048 : k * 2048 + 1024] = s_re * b_re + s_im * b_im
        out_ref[:, k * 2048 + 1024 : k * 2048 + 2048] = s_re * b_im - s_im * b_re
        part = slice(k * 2048, k * 2048 + 2048)
        copies += begin([(out_ref.at[:, part], out_hbm.at[:, part])], sems.at[k : k + 1])
    finish(copies)


def final_kernel(
    recv_ref, conv_ref, txi_hbm, grad_ref, kernel_ref, bias_ref,
    recv, conv, txi, field_ref, grads, in_sems, out_sems,
):
    fetched = begin(
        [(recv_ref, recv), (txi_hbm, txi)] + [(conv_ref.at[y], conv.at[y]) for y in range(YL)], in_sems
    )
    fetched[0].wait()
    place_fields(recv, field_ref)
    fetched[1].wait()
    copies = []
    for y in range(YL):
        back = x_inverse(field_ref[y * 64 : y * 64 + 64], txi[...])
        fetched[2 + y].wait()
        grads[y] = (back + conv[y]).astype(BF16)
        copies += begin([(grads.at[y], grad_ref.at[y])], out_sems.at[y : y + 1])
    piece = []
    for g in range(7):
        high = recv[g, LINE_ROWS : LINE_ROWS + GRAD_ROWS].astype(F32)
        low = recv[g, LINE_ROWS + GRAD_ROWS : LINE_ROWS + 2 * GRAD_ROWS].astype(F32)
        rows = SCALE * (high + low)
        piece += [rows[:, j * C : j * C + C] for j in range(4)]
    for dy in range(3):
        for dz in range(3):
            kernel_ref[dy, dz] = jnp.concatenate([piece[dx * 9 + dy * 3 + dz] for dx in range(3)], 1)
    row = lax.broadcasted_iota(jnp.int32, (C, C), 0)
    bias_ref[...] = jnp.sum(jnp.where(row == lane_of((C, C)), piece[27], 0.0), axis=0, keepdims=True)
    finish(copies)


AUTO, HBM = pl.BlockSpec(), pl.BlockSpec(memory_space=pltpu.HBM)


def vmem(dims, kind):
    return pltpu.VMEM(dims, kind)


def sems(count):
    return pltpu.SemaphoreType.DMA((count,))


def shape(dims, kind):
    return jax.ShapeDtypeStruct(dims, kind)


def call(body, ins, outs, scratch, room, *operands):
    return pl.pallas_call(
        body,
        in_specs=ins,
        out_specs=[spec for spec, _ in outs],
        out_shape=[kind for _, kind in outs],
        scratch_shapes=scratch,
        compiler_params=pltpu.CompilerParams(vmem_limit_bytes=room),
    )(*operands)


def exchange(blocks, axis):
    return lax.all_to_all(blocks, axis, 0, 0, tiled=True)


FIELD = shape((YL, 128, NX), BF16)
SIDE = shape((YL, 32, NX), BF16)
FACE = shape((128, NX), BF16)
EDGE = shape((192, NX), BF16)
PAD = vmem((YL + 2, 192, NX), BF16)


def after(value, *others):
    return lax.optimization_barrier((value, *others))[0]


def z_halos(front, back):
    zlo = lax.ppermute(back, "gz", [(i, i + 1) for i in range(GZ - 1)])
    zhi = lax.ppermute(front, "gz", [(i + 1, i) for i in range(GZ - 1)])
    return zlo, zhi


def y_edges(first, last, zlo, zhi):
    return call(edges_kernel, [AUTO] * 4, [(AUTO, EDGE)] * 2, [], SMALL, first, last, zlo, zhi)


def y_halos(first, last):
    ylo = lax.ppermute(last, "gy", [(i, i + 1) for i in range(GY - 1)])
    yhi = lax.ppermute(first, "gy", [(i + 1, i) for i in range(GY - 1)])
    return ylo, yhi


def conv(flip, own, halo, kernel, bias):
    return call(
        functools.partial(conv_kernel, flip),
        [HBM] * 7,
        [(HBM, shape((YL, 128, NX), F32))],
        [
            PAD, vmem((384, 576), BF16), vmem((YL, 128, NX), F32),
            vmem((3, 3, C, 3 * C), BF16), vmem((1, C), F32), sems(7), sems(YL),
        ],
        LARGE,
        own, *halo, kernel, bias,
    )[0]


def on_device(features, cotangent, spectral_weight, kernel_weight, channel_bias):
    own = features.reshape(YL, 128, NX)
    cot = cotangent.reshape(YL, 128, NX)
    weight = spectral_weight.reshape(64, 8192)
    bias = channel_bias.reshape(1, C)
    tx = jnp.asarray(x_forward_table())
    txi = jnp.asarray(x_inverse_table())
    ty = jnp.asarray(y_forward_table())
    tyi = jnp.asarray(y_inverse_table())
    tzf = jnp.asarray(z_forward_table())
    tzi = jnp.asarray(z_inverse_table())
    faces_out = [(HBM, SIDE)] * 2 + [(HBM, FACE)] * 2
    spectrum_out = (AUTO, shape((128, 128), F32))

    def lines_out(rows):
        return AUTO, shape((GY, rows, 128), BF16)

    def modes_out(rows):
        return AUTO, shape((GZ, rows, 128), BF16)

    both_rows = LINE_ROWS + 2 * GRAD_ROWS
    tail_rows = MODE_ROWS + TAIL_ROWS
    send, front, back, first, last = call(
        analyse_kernel,
        [HBM] * 2,
        [lines_out(LINE_ROWS)] + faces_out,
        [vmem((YL, 128, NX), BF16), vmem((64, NX), BF16), sems(1 + YL), sems(4)],
        LARGE,
        own, tx,
    )
    recv = exchange(send, "gy")

    zlo, zhi = z_halos(front, back)
    (send,) = call(y_kernel, [AUTO] * 2, [modes_out(MODE_ROWS)], [], SMALL, recv, ty)
    recv = exchange(send, "gz")
    send, spectrum = call(
        mix_kernel,
        [AUTO] * 4,
        [modes_out(MODE_ROWS), spectrum_out],
        [vmem((256, 128), F32)],
        SMALL,
        recv, weight, tzf, tzi,
    )
    halo = (zlo, zhi, *y_halos(*y_edges(after(first, send), last, zlo, zhi)))
    recv = exchange(send, "gz")
    recv, *halo = lax.optimization_barrier((recv, *halo))
    (send,) = call(spread_kernel, [AUTO] * 2, [lines_out(LINE_ROWS)], [], SMALL, recv, tyi)
    local = conv(False, after(own, send), halo, kernel_weight, bias)
    recv = exchange(send, "gy")
    slope, front, back, first, last = call(
        slope_kernel,
        [HBM] * 4,
        [(HBM, FIELD)] + faces_out,
        [
            vmem((GY, LINE_ROWS, 128), BF16), vmem((YL, 128, NX), F32), vmem((YL, 128, NX), BF16),
            vmem((192, NX), BF16), vmem((512, 128), F32), vmem((YL, 128, NX), BF16),
            sems(2 + 2 * YL), sems(YL + 4),
        ],
        LARGE,
        recv, local, cot, txi,
    )
    (send,) = call(
        back_kernel,
        [HBM] * 7,
        [lines_out(both_rows)],
        [
            vmem((YL, 128, NX), BF16), PAD, vmem((64, NX), BF16), vmem((384, 576), F32), sems(6 + YL),
        ],
        LARGE,
        slope, own, *halo, tx,
    )
    recv = exchange(send, "gy")

    zlo, zhi = z_halos(front, back)
    (send,) = call(
        y_back_kernel,
        [AUTO] * 2,
        [modes_out(tail_rows)],
        [vmem((GRAD_ROWS, 128), F32), vmem((GZ * TAIL_ROWS, 128), F32)],
        SMALL,
        recv, ty,
    )
    recv = exchange(send, "gz")
    send, back = call(
        adjoint_kernel,
        [AUTO] * 4,
        [modes_out(tail_rows), spectrum_out],
        [vmem((256, 128), F32)],
        SMALL,
        recv, weight, tzf, tzi,
    )
    halo = (zlo, zhi, *y_halos(*y_edges(after(first, send), last, zlo, zhi)))
    recv = exchange(send, "gz")
    (grad_spectral,) = call(
        outer_kernel,
        [AUTO] * 2,
        [(HBM, shape((64, 8192), F32))],
        [vmem((64, 8192), F32), sems(KXL)],
        LARGE,
        after(spectrum, send), back,
    )
    recv, grad_spectral, *halo = lax.optimization_barrier((recv, grad_spectral, *halo))
    (send,) = call(
        spread_back_kernel,
        [AUTO] * 2,
        [lines_out(both_rows)],
        [vmem((GZ * TAIL_ROWS, 128), F32), vmem((2 * GRAD_ROWS, 128), F32)],
        SMALL,
        recv, tyi,
    )
    recv = exchange(send, "gy")
    conv_field = conv(True, after(slope, send), halo, kernel_weight, bias)
    grad_field, grad_kernel, grad_bias = call(
        final_kernel,
        [HBM] * 3,
        [(HBM, FIELD), (AUTO, shape((3, 3, C, 3 * C), F32)), (AUTO, shape((1, C), F32))],
        [
            vmem((GY, both_rows, 128), BF16), vmem((YL, 128, NX), F32), vmem((192, NX), BF16),
            vmem((512, 128), F32), vmem((YL, 128, NX), BF16), sems(2 + YL), sems(YL),
        ],
        LARGE,
        recv, conv_field, txi,
    )
    return (
        grad_field.reshape(features.shape),
        grad_spectral.reshape(spectral_weight.shape),
        grad_kernel,
        grad_bias.reshape(C),
    )


def solution(mesh):
    return jax.shard_map(
        on_device,
        mesh=mesh,
        in_specs=(
            P("gy", "gz", None, None),
            P("gy", "gz", None, None),
            P("gz", None, "gy"),
            P(),
            P(),
        ),
        out_specs=(P("gy", "gz", None, None), P("gz", None, "gy"), P(), P()),
        check_vma=False,
    )
```

time: 158 us -> 144 us (0.911)
  blocking collectives: 0 us -> 44.7 us
  waiting for transfers between devices: 36.7 us -> 6.89 us
  local copies, waits for them, and re-layouts: 31.5 us -> 4.29 us
  Pallas kernels: 29.6 us -> 43.2 us
  starting transfers between devices: 53.6 us -> 42.7 us
  other arithmetic: 3.03 us -> 0 us
    all_to_all x0 -> x4, blocking collectives: none -> 44.7 us  [exchange(): return lax.all_to_all(blocks, axis, 0, 0, tiled=True)]
    ppermute x8, waiting for transfers between devices: 22.1 us -> 0.02 us  [the longest x2 0.01 us: y_halos(): yhi = lax.ppermute(first, 'gy', [(i + 1, i) for i in range(GY - 1)])]
    unnamed x82 -> x48, local copies, waits for them, and re-layouts: 23.7 us -> 4.29 us
    pallas_call x8 -> x15, Pallas kernels: 29.6 us -> 43.2 us  [call(): pl.pallas_call(body, in_specs=ins, out_specs=[spec for spec, _ in outs],...]
    all_to_all x4, starting transfers between devices: 30.8 us -> 20.1 us  [exchange(): return lax.all_to_all(blocks, axis, 0, 0, tiled=True)]
    all_to_all x4, waiting for transfers between devices: 14.6 us -> 6.87 us  [exchange(): return lax.all_to_all(blocks, axis, 0, 0, tiled=True)]
    slice x3 -> x0, local copies, waits for them, and re-layouts: 2.55 us -> none  [the longest x1 1.65 us: halos(): yhi = lax.ppermute(own[0], 'gy', down)]
    concatenate x4 -> x0, other arithmetic: 2.41 us -> none  [the longest x2 1.6 us: halos(): first = jnp.concatenate([ylo[None, 0:32], own[:, 0:32], yhi[None, 0:32]], 0)]
  transfers between devices with their start and end apart: 12 -> 12, of which waited for: 5 -> 2; matrix products, arithmetic and copies ran while one was open for 5% -> 0% of each run, Pallas kernels for 13% -> 15%
where the time goes in v2:
time: 144 us; the launch traced here: 143 us
  blocking collectives  44.7 us (31%)
  Pallas kernels  43.2 us (30%)
  starting transfers between devices  42.7 us (30%)
  waiting for transfers between devices  6.89 us (5%)
  local copies, waits for them, and re-layouts  4.29 us (3%)
    all_to_all x4, blocking collectives, exchange(): return lax.all_to_all(blocks, axis, 0, 0, tiled=True)  44.7 us
    pallas_call x15, Pallas kernels, call(): pl.pallas_call(body, in_specs=ins, out_specs=[spec for spec, _ in outs],...  43.2 us
    all_to_all x4, starting transfers between devices, exchange(): return lax.all_to_all(blocks, axis, 0, 0, tiled=True)  20.1 us
    ppermute x2, starting transfers between devices, y_halos(): ylo = lax.ppermute(last, 'gy', [(i, i + 1) for i in range(GY - 1)])  9.9 us
    all_to_all x4, waiting for transfers between devices, exchange(): return lax.all_to_all(blocks, axis, 0, 0, tiled=True)  6.87 us
    ppermute x2, starting transfers between devices, z_halos(): zlo = lax.ppermute(back, 'gz', [(i, i + 1) for i in range(GZ - 1)])  6.24 us
    unnamed x48, local copies, waits for them, and re-layouts  4.29 us
    ppermute x2, starting transfers between devices, y_halos(): yhi = lax.ppermute(first, 'gy', [(i + 1, i) for i in range(GY - 1)])  3.84 us
  transfers between devices with their start and end apart: 12, of which 2 were waited for; matrix products, arithmetic and copies ran while one was open for 0% of the time, Pallas kernels for 15%

profile of v2, /device:TPU:1, one launch (start us, length us, event | category | flops | bytes accessed | tf_op | source)
XLA Modules:
  0.0 143.0 jit_solution(5376635980346195590)
XLA Ops:
  0.6 0.0 copy-start
  0.6 0.0 copy-start.3
  0.7 4.1 %shard_map.138 = (bf16[8,64,128]{2,1,0:T(8,128)(2,1)}, bf16[8,32,512]{2,1,0:T(8,128)(2,1)}, bf16[8,32,512]{2,1,0:T(8,128)(2,1)}, bf16[128,512]{1,0:T(8,128)(2,1)}, bf16[128,512]{1,0:T(8,128)(2,1)}) custom-call(bf16[8,128,512]{2,1,0:T(8,128)(2,1)} %bitcast.9, bf16[64,512]{1,0:T(8,128)(2,1)} %constant.12.clone.tx_hbm), custom_call_target="tpu_custom_call" | custom-call | tf_op jit(solution)/shard_map/pallas_call | solution.py:530
  4.8 4.0 %collective-permute-start = (bf16[8,32,512]{2,1,0:T(8,128)(2,1)}, bf16[8,32,512]{2,1,0:T(8,128)(2,1)S(1)}, u32[]{:S(2)}, u32[]{:S(2)}) collective-permute-start(bf16[8,32,512]{2,1,0:T(8,128)(2,1)} %get-tuple-element.43), channel_id=1, source_target_pairs={{0,1},{1,2},{2,3},{3,4},{4,5},{5,6},{6,7},{7,8},{8,9},{9,10},{10,1... | collective-permute-start | bytes 786440 | tf_op jit(solution)/shard_map/ppermute | solution.py:556
  8.8 1.3 collective-permute-start.1
  10.1 10.5 %all_to_all.40.recv_ref = bf16[8,64,128]{2,1,0:T(8,128)(2,1)S(1)} all-to-all(bf16[8,64,128]{2,1,0:T(8,128)(2,1)} %get-tuple-element.41), channel_id=1, replica_groups=mesh['gy'=8,'gz'=16] {'gy'}, dimensions={0} | all-to-all | bytes 262144 | tf_op jit(solution)/shard_map/all_to_all | solution.py:541
  20.6 1.0 copy-done.4
  21.7 0.3 shard_map.139
  22.0 15.1 %all_to_all.41.recv_ref = bf16[16,16,128]{2,1,0:T(8,128)(2,1)S(1)} all-to-all(bf16[16,16,128]{2,1,0:T(8,128)(2,1)S(1)} %shard_map.139), channel_id=1, replica_groups=mesh['gy'=8,'gz'=16] {'gz'}, dimensions={0} | all-to-all | bytes 131072 | tf_op jit(solution)/shard_map/all_to_all | solution.py:541
  37.1 0.0 copy-done
  37.1 0.9 copy-done.8
  38.0 0.9 copy-done.10
  38.9 1.4 shard_map.140
  40.3 0.0 copy-start.16
  40.3 0.0 collective-permute-done.zlo_ref
  40.3 0.0 copy-start.1
  40.3 0.0 collective-permute-done.1.zhi_ref
  40.3 0.0 copy-start.2
  40.3 0.0 copy-done.14
  40.4 4.4 %collective-permute-start.2 = (bf16[192,512]{1,0:T(8,128)(2,1)S(1)}, bf16[192,512]{1,0:T(8,128)(2,1)S(1)}, u32[]{:S(2)}, u32[]{:S(2)}) collective-permute-start(bf16[192,512]{1,0:T(8,128)(2,1)S(1)} %get-tuple-element.48), channel_id=1, source_target_pairs={{0,16},{16,32},{32,48},{48,64},{64,80},{80,96},{96,112},{1,17},{17... | collective-permute-start | bytes 589832 | tf_op jit(solution)/shard_map/ppermute | solution.py:566
  44.8 0.0 copy-done.16
  44.8 1.9 %collective-permute-start.3 = (bf16[192,512]{1,0:T(8,128)(2,1)S(1)}, bf16[192,512]{1,0:T(8,128)(2,1)S(1)}, u32[]{:S(2)}, u32[]{:S(2)}) collective-permute-start(bf16[192,512]{1,0:T(8,128)(2,1)S(1)} %get-tuple-element.49), channel_id=1, source_target_pairs={{16,0},{32,16},{48,32},{64,48},{80,64},{96,80},{112,96},{17,1},{33... | collective-permute-start | bytes 589832 | tf_op jit(solution)/shard_map/ppermute | solution.py:567
  46.7 9.4 %all_to_all.42.recv_ref = bf16[16,16,128]{2,1,0:T(8,128)(2,1)S(1)} all-to-all(bf16[16,16,128]{2,1,0:T(8,128)(2,1)S(1)} %get-tuple-element.42), channel_id=1, replica_groups=mesh['gy'=8,'gz'=16] {'gz'}, dimensions={0} | all-to-all | bytes 131072 | tf_op jit(solution)/shard_map/all_to_all | solution.py:541
  56.1 0.0 collective-permute-done.2.ylo_ref
  56.1 0.0 collective-permute-done.3.yhi_ref
  56.1 1.0 shard_map.142
  57.1 5.4 %all-to-all-start.3 = ((bf16[8,64,128]{2,1,0:T(8,128)(2,1)}), bf16[8,64,128]{2,1,0:T(8,128)(2,1)S(1)}, u32[]{:S(2)}, u32[]{:S(2)}) async-start(bf16[8,64,128]{2,1,0:T(8,128)(2,1)} %shard_map.142), calls=%async_computation.3 | async-start | bytes 262144 | tf_op jit(solution)/shard_map/all_to_all | solution.py:541
  62.5 7.0 %shard_map.143.local_ref = f32[8,128,512]{2,1,0:T(8,128)} custom-call(bf16[8,128,512]{2,1,0:T(8,128)(2,1)} %bitcast.10, bf16[8,32,512]{2,1,0:T(8,128)(2,1)} %copy-done.1, bf16[8,32,512]{2,1,0:T(8,128)(2,1)} %copy-done.2, bf16[192,512]{1,0:T(8,128)(2,1)} %copy-done.19, bf16[192,512]{1,0:T(8,128)(2,1)} %copy-done.20, bf16[3,3,32,96]{3,2,1,0:T(8,128)(2,1)} %kernel_hbm.3, ...), custom_call_target="tpu_custom_call" | custom-call | tf_op jit(solution)/shard_map/pallas_call | solution.py:530
  69.5 0.0 all-to-all-done.3.recv_ref
  69.5 0.0 copy-start.21
  69.5 0.6 copy-done.21
  70.2 5.7 %shard_map.144 = (bf16[8,128,512]{2,1,0:T(8,128)(2,1)}, bf16[8,32,512]{2,1,0:T(8,128)(2,1)}, bf16[8,32,512]{2,1,0:T(8,128)(2,1)}, bf16[128,512]{1,0:T(8,128)(2,1)}, bf16[128,512]{1,0:T(8,128)(2,1)}) custom-call(bf16[8,64,128]{2,1,0:T(8,128)(2,1)} %copy-done.21, f32[8,128,512]{2,1,0:T(8,128)} %shard_map.143.local_ref, bf16[8,128,512]{2,1,0:T(8,128)(2,1)} %bitcast.13, ...), custom_call_target="tpu_custom_call" | custom-call | tf_op jit(solution)/shard_map/pallas_call | solution.py:530
  75.9 0.0 copy-start.5
  75.9 0.0 copy-start.9
  75.9 0.0 copy-start.11
  76.0 6.1 %shard_map.145 = bf16[8,128,128]{2,1,0:T(8,128)(2,1)} custom-call(bf16[8,128,512]{2,1,0:T(8,128)(2,1)} %get-tuple-element.69.slope_ref.own_ref, bf16[8,128,512]{2,1,0:T(8,128)(2,1)} %bitcast.11, bf16[8,32,512]{2,1,0:T(8,128)(2,1)} %copy-done.1, bf16[8,32,512]{2,1,0:T(8,128)(2,1)} %copy-done.2, bf16[192,512]{1,0:T(8,128)(2,1)} %copy-done.19, ...), custom_call_target="tpu_custom_call" | custom-call | tf_op jit(solution)/shard_map/pallas_call | solution.py:530
  82.0 4.9 %all-to-all-start.4 = ((bf16[8,128,128]{2,1,0:T(8,128)(2,1)}), bf16[8,128,128]{2,1,0:T(8,128)(2,1)S(1)}, u32[]{:S(2)}, u32[]{:S(2)}) async-start(bf16[8,128,128]{2,1,0:T(8,128)(2,1)} %shard_map.145), calls=%async_computation.4 | async-start | bytes 524288 | tf_op jit(solution)/shard_map/all_to_all | solution.py:541
  87.0 2.2 %collective-permute-start.4 = (bf16[8,32,512]{2,1,0:T(8,128)(2,1)}, bf16[8,32,512]{2,1,0:T(8,128)(2,1)S(1)}, u32[]{:S(2)}, u32[]{:S(2)}) collective-permute-start(bf16[8,32,512]{2,1,0:T(8,128)(2,1)} %get-tuple-element.61), channel_id=1, source_target_pairs={{0,1},{1,2},{2,3},{3,4},{4,5},{5,6},{6,7},{7,8},{8,9},{9,10},{10,1... | collective-permute-start | bytes 786440 | tf_op jit(solution)/shard_map/ppermute | solution.py:556
  89.2 1.3 collective-permute-start.5
  90.5 3.0 %all-to-all-done.4.recv_ref = bf16[8,128,128]{2,1,0:T(8,128)(2,1)S(1)} async-done(((bf16[8,128,128]{2,1,0:T(8,128)(2,1)}), bf16[8,128,128]{2,1,0:T(8,128)(2,1)S(1)}, u32[]{:S(2)}, u32[]{:S(2)}) %all-to-all-start.4) | async-done | bytes 262176 | tf_op jit(solution)/shard_map/all_to_all | solution.py:541
  93.5 0.3 shard_map.146
  93.8 9.7 %all_to_all.43.recv_ref = bf16[16,24,128]{2,1,0:T(8,128)(2,1)S(1)} all-to-all(bf16[16,24,128]{2,1,0:T(8,128)(2,1)S(1)} %shard_map.146), channel_id=1, replica_groups=mesh['gy'=8,'gz'=16] {'gz'}, dimensions={0} | all-to-all | bytes 196608 | tf_op jit(solution)/shard_map/all_to_all | solution.py:541
  103.4 2.4 %shard_map.147 = (bf16[16,24,128]{2,1,0:T(8,128)(2,1)}, f32[128,128]{1,0:T(8,128)S(1)}) custom-call(bf16[16,24,128]{2,1,0:T(8,128)(2,1)S(1)} %all_to_all.43.recv_ref, bf16[64,8192]{1,0:T(8,128)(2,1)S(1)} %bitcast.8, bf16[2,128,256]{2,1,0:T(8,128)(2,1)S(1)} %copy-done.11, bf16[2,256,128]{2,1,0:T(8,128)(2,1)S(1)} %copy-done.9), custom_call_target="tpu_custom_call" | custom-call | tf_op jit(solution)/shard_map/pallas_call | solution.py:530
  105.9 0.0 collective-permute-done.4.zlo_ref
  105.9 0.0 collective-permute-done.5.zhi_ref
  105.9 0.0 copy-start.7
  105.9 0.0 copy-done.12
  105.9 0.0 copy-done.13
  106.0 5.5 %collective-permute-start.6 = (bf16[192,512]{1,0:T(8,128)(2,1)S(1)}, bf16[192,512]{1,0:T(8,128)(2,1)S(1)}, u32[]{:S(2)}, u32[]{:S(2)}) collective-permute-start(bf16[192,512]{1,0:T(8,128)(2,1)S(1)} %get-tuple-element.66), channel_id=1, source_target_pairs={{0,16},{16,32},{32,48},{48,64},{64,80},{80,96},{96,112},{1,17},{17... | collective-permute-start | bytes 589832 | tf_op jit(solution)/shard_map/ppermute | solution.py:566
  111.5 1.9 %collective-permute-start.7 = (bf16[192,512]{1,0:T(8,128)(2,1)S(1)}, bf16[192,512]{1,0:T(8,128)(2,1)S(1)}, u32[]{:S(2)}, u32[]{:S(2)}) collective-permute-start(bf16[192,512]{1,0:T(8,128)(2,1)S(1)} %get-tuple-element.67), channel_id=1, source_target_pairs={{16,0},{32,16},{48,32},{64,48},{80,64},{96,80},{112,96},{17,1},{33... | collective-permute-start | bytes 589832 | tf_op jit(solution)/shard_map/ppermute | solution.py:567
  113.4 3.7 %all-to-all-start.6 = ((bf16[16,24,128]{2,1,0:T(8,128)(2,1)}), bf16[16,24,128]{2,1,0:T(8,128)(2,1)S(1)}, u32[]{:S(2)}, u32[]{:S(2)}) async-start(bf16[16,24,128]{2,1,0:T(8,128)(2,1)} %get-tuple-element.57), calls=%async_computation.6 | async-start | bytes 196608 | tf_op jit(solution)/shard_map/all_to_all | solution.py:541
  117.1 0.0 copy-done.17
  117.1 2.6 %shard_map.148 = f32[64,8192]{1,0:T(8,128)} custom-call(f32[128,128]{1,0:T(8,128)} %copy-done.16, f32[128,128]{1,0:T(8,128)} %copy-done.17), custom_call_target="tpu_custom_call" | custom-call | tf_op jit(solution)/shard_map/pallas_call | solution.py:530
  119.7 3.9 %all-to-all-done.6.recv_ref = bf16[16,24,128]{2,1,0:T(8,128)(2,1)S(1)} async-done(((bf16[16,24,128]{2,1,0:T(8,128)(2,1)}), bf16[16,24,128]{2,1,0:T(8,128)(2,1)S(1)}, u32[]{:S(2)}, u32[]{:S(2)}) %all-to-all-start.6) | async-done | bytes 98336 | tf_op jit(solution)/shard_map/all_to_all | solution.py:541
  123.6 0.0 collective-permute-done.6.ylo_ref
  123.6 0.0 collective-permute-done.7.yhi_ref
  123.6 1.0 shard_map.150
  124.6 0.0 copy-done.6
  124.6 6.1 %all-to-all-start.7 = ((bf16[8,128,128]{2,1,0:T(8,128)(2,1)}), bf16[8,128,128]{2,1,0:T(8,128)(2,1)S(1)}, u32[]{:S(2)}, u32[]{:S(2)}) async-start(bf16[8,128,128]{2,1,0:T(8,128)(2,1)} %shard_map.150), calls=%async_computation.7 | async-start | bytes 524288 | tf_op jit(solution)/shard_map/all_to_all | solution.py:541
  130.7 0.0 copy-done.23
  130.7 7.0 %shard_map.151.conv_ref = f32[8,128,512]{2,1,0:T(8,128)} custom-call(bf16[8,128,512]{2,1,0:T(8,128)(2,1)} %get-tuple-element.69.slope_ref.own_ref, bf16[8,32,512]{2,1,0:T(8,128)(2,1)} %copy-done.6, bf16[8,32,512]{2,1,0:T(8,128)(2,1)} %copy-done.7, bf16[192,512]{1,0:T(8,128)(2,1)} %copy-done.22, bf16[192,512]{1,0:T(8,128)(2,1)} %copy-done.23, ...), custom_call_target="tpu_custom_call" | custom-call | tf_op jit(solution)/shard_map/pallas_call | solution.py:530
  137.6 0.0 all-to-all-done.7.recv_ref
  137.7 0.7 copy-done.18
  138.4 4.4 %shard_map.152 = (bf16[8,128,512]{2,1,0:T(8,128)(2,1)}, f32[3,3,32,96]{3,2,1,0:T(8,128)}, f32[1,32]{1,0:T(1,128)}) custom-call(bf16[8,128,128]{2,1,0:T(8,128)(2,1)} %copy-done.18, f32[8,128,512]{2,1,0:T(8,128)} %shard_map.151.conv_ref, bf16[192,512]{1,0:T(8,128)(2,1)} %constant.13.clone.txi_hbm), custom_call_target="tpu_custom_call" | custom-call | tf_op jit(solution)/shard_map/pallas_call | solution.py:530
  (27 shorter events, 0.1 us)
Async XLA Ops:
  0.6 36.5 %copy-start = (bf16[2,32,8192]{2,1,0:T(8,128)(2,1)S(1)}, bf16[2,32,8192]{2,1,0:T(8,128)(2,1)}, u32[]{:S(2)}) copy-start(bf16[2,32,8192]{2,1,0:T(8,128)(2,1)} %param.13) | copy-start | bytes 3145732
  0.6 55.5 %copy-start.3 = (bf16[2,512,256]{2,1,0:T(8,128)(2,1)S(1)}, bf16[2,512,256]{2,1,0:T(8,128)(2,1)}, u32[]{:S(2)}) copy-start(bf16[2,512,256]{2,1,0:T(8,128)(2,1)} %constant.15.clone.table_ref) | copy-start | bytes 1572868
  4.8 35.6 %collective-permute-start = (bf16[8,32,512]{2,1,0:T(8,128)(2,1)}, bf16[8,32,512]{2,1,0:T(8,128)(2,1)S(1)}, u32[]{:S(2)}, u32[]{:S(2)}) collective-permute-start(bf16[8,32,512]{2,1,0:T(8,128)(2,1)} %get-tuple-element.43), channel_id=1, source_target_pairs={{0,1},{1,2},{2,3},{3,4},{4,5},{5,6},{6,7},{7,8},{8,9},{9,10},{10,1... | collective-permute-start | bytes 786440 | tf_op jit(solution)/shard_map/ppermute | solution.py:556
  8.8 31.5 %collective-permute-start.1 = (bf16[8,32,512]{2,1,0:T(8,128)(2,1)}, bf16[8,32,512]{2,1,0:T(8,128)(2,1)S(1)}, u32[]{:S(2)}, u32[]{:S(2)}) collective-permute-start(bf16[8,32,512]{2,1,0:T(8,128)(2,1)} %get-tuple-element.44), channel_id=1, source_target_pairs={{1,0},{2,1},{3,2},{4,3},{5,4},{6,5},{7,6},{8,7},{9,8},{10,9},{11,1... | collective-permute-start | bytes 786440 | tf_op jit(solution)/shard_map/ppermute | solution.py:557
  20.6 1.0 copy-start.4
  21.7 18.7 %copy-start.14 = (bf16[128,512]{1,0:T(8,128)(2,1)S(1)}, bf16[128,512]{1,0:T(8,128)(2,1)}, u32[]{:S(2)}) copy-start(bf16[128,512]{1,0:T(8,128)(2,1)} %get-tuple-element.46.own_first_ref) | copy-start | bytes 393220
  21.7 18.7 %copy-start.15 = (bf16[128,512]{1,0:T(8,128)(2,1)S(1)}, bf16[128,512]{1,0:T(8,128)(2,1)}, u32[]{:S(2)}) copy-start(bf16[128,512]{1,0:T(8,128)(2,1)} %get-tuple-element.47.own_last_ref) | copy-start | bytes 393220
  37.1 0.9 copy-start.8
  38.0 0.9 copy-start.10
  40.3 4.5 %copy-start.16 = (f32[128,128]{1,0:T(8,128)}, f32[128,128]{1,0:T(8,128)S(1)}, u32[]{:S(2)}) copy-start(f32[128,128]{1,0:T(8,128)S(1)} %get-tuple-element.59.spec_ref) | copy-start | bytes 196612
  40.3 22.2 %copy-start.1 = (bf16[8,32,512]{2,1,0:T(8,128)(2,1)}, bf16[8,32,512]{2,1,0:T(8,128)(2,1)S(1)}, u32[]{:S(2)}) copy-start(bf16[8,32,512]{2,1,0:T(8,128)(2,1)S(1)} %collective-permute-done.zlo_ref) | copy-start | bytes 786436
  40.3 22.2 %copy-start.2 = (bf16[8,32,512]{2,1,0:T(8,128)(2,1)}, bf16[8,32,512]{2,1,0:T(8,128)(2,1)S(1)}, u32[]{:S(2)}) copy-start(bf16[8,32,512]{2,1,0:T(8,128)(2,1)S(1)} %collective-permute-done.1.zhi_ref) | copy-start | bytes 786436
  40.4 15.7 %collective-permute-start.2 = (bf16[192,512]{1,0:T(8,128)(2,1)S(1)}, bf16[192,512]{1,0:T(8,128)(2,1)S(1)}, u32[]{:S(2)}, u32[]{:S(2)}) collective-permute-start(bf16[192,512]{1,0:T(8,128)(2,1)S(1)} %get-tuple-element.48), channel_id=1, source_target_pairs={{0,16},{16,32},{32,48},{48,64},{64,80},{80,96},{96,112},{1,17},{17... | collective-permute-start | bytes 589832 | tf_op jit(solution)/shard_map/ppermute | solution.py:566
  44.8 11.3 %collective-permute-start.3 = (bf16[192,512]{1,0:T(8,128)(2,1)S(1)}, bf16[192,512]{1,0:T(8,128)(2,1)S(1)}, u32[]{:S(2)}, u32[]{:S(2)}) collective-permute-start(bf16[192,512]{1,0:T(8,128)(2,1)S(1)} %get-tuple-element.49), channel_id=1, source_target_pairs={{16,0},{32,16},{48,32},{64,48},{80,64},{96,80},{112,96},{17,1},{33... | collective-permute-start | bytes 589832 | tf_op jit(solution)/shard_map/ppermute | solution.py:567
  56.1 6.4 %copy-start.19 = (bf16[192,512]{1,0:T(8,128)(2,1)}, bf16[192,512]{1,0:T(8,128)(2,1)S(1)}, u32[]{:S(2)}) copy-start(bf16[192,512]{1,0:T(8,128)(2,1)S(1)} %collective-permute-done.2.ylo_ref) | copy-start | bytes 589828
  56.1 6.4 %copy-start.20 = (bf16[192,512]{1,0:T(8,128)(2,1)}, bf16[192,512]{1,0:T(8,128)(2,1)S(1)}, u32[]{:S(2)}) copy-start(bf16[192,512]{1,0:T(8,128)(2,1)S(1)} %collective-permute-done.3.yhi_ref) | copy-start | bytes 589828
  57.1 12.4 %all-to-all-start.3 = ((bf16[8,64,128]{2,1,0:T(8,128)(2,1)}), bf16[8,64,128]{2,1,0:T(8,128)(2,1)S(1)}, u32[]{:S(2)}, u32[]{:S(2)}) async-start(bf16[8,64,128]{2,1,0:T(8,128)(2,1)} %shard_map.142), calls=%async_computation.3 | async-start | bytes 262144 | tf_op jit(solution)/shard_map/all_to_all | solution.py:541
  69.5 0.7 copy-start.21
  75.9 17.6 %copy-start.5 = (bf16[2,256,512]{2,1,0:T(8,128)(2,1)S(1)}, bf16[2,256,512]{2,1,0:T(8,128)(2,1)}, u32[]{:S(2)}) copy-start(bf16[2,256,512]{2,1,0:T(8,128)(2,1)} %constant.14.clone.table_ref) | copy-start | bytes 1572868
  75.9 27.5 %copy-start.9 = (bf16[2,256,128]{2,1,0:T(8,128)(2,1)S(1)}, bf16[2,256,128]{2,1,0:T(8,128)(2,1)}, u32[]{:S(2)}) copy-start(bf16[2,256,128]{2,1,0:T(8,128)(2,1)} %constant.17.clone.tzi_ref) | copy-start | bytes 393220
  75.9 27.5 %copy-start.11 = (bf16[2,128,256]{2,1,0:T(8,128)(2,1)S(1)}, bf16[2,128,256]{2,1,0:T(8,128)(2,1)}, u32[]{:S(2)}) copy-start(bf16[2,128,256]{2,1,0:T(8,128)(2,1)} %constant.16.clone.tzf_ref) | copy-start | bytes 393220
  82.0 23.9 %copy-start.12 = (bf16[128,512]{1,0:T(8,128)(2,1)S(1)}, bf16[128,512]{1,0:T(8,128)(2,1)}, u32[]{:S(2)}) copy-start(bf16[128,512]{1,0:T(8,128)(2,1)} %get-tuple-element.64.own_first_ref) | copy-start | bytes 393220
  82.0 23.9 %copy-start.13 = (bf16[128,512]{1,0:T(8,128)(2,1)S(1)}, bf16[128,512]{1,0:T(8,128)(2,1)}, u32[]{:S(2)}) copy-start(bf16[128,512]{1,0:T(8,128)(2,1)} %get-tuple-element.65.own_last_ref) | copy-start | bytes 393220
  82.0 11.5 %all-to-all-start.4 = ((bf16[8,128,128]{2,1,0:T(8,128)(2,1)}), bf16[8,128,128]{2,1,0:T(8,128)(2,1)S(1)}, u32[]{:S(2)}, u32[]{:S(2)}) async-start(bf16[8,128,128]{2,1,0:T(8,128)(2,1)} %shard_map.145), calls=%async_computation.4 | async-start | bytes 524288 | tf_op jit(solution)/shard_map/all_to_all | solution.py:541
  87.0 18.9 %collective-permute-start.4 = (bf16[8,32,512]{2,1,0:T(8,128)(2,1)}, bf16[8,32,512]{2,1,0:T(8,128)(2,1)S(1)}, u32[]{:S(2)}, u32[]{:S(2)}) collective-permute-start(bf16[8,32,512]{2,1,0:T(8,128)(2,1)} %get-tuple-element.61), channel_id=1, source_target_pairs={{0,1},{1,2},{2,3},{3,4},{4,5},{5,6},{6,7},{7,8},{8,9},{9,10},{10,1... | collective-permute-start | bytes 786440 | tf_op jit(solution)/shard_map/ppermute | solution.py:556
  89.2 16.7 %collective-permute-start.5 = (bf16[8,32,512]{2,1,0:T(8,128)(2,1)}, bf16[8,32,512]{2,1,0:T(8,128)(2,1)S(1)}, u32[]{:S(2)}, u32[]{:S(2)}) collective-permute-start(bf16[8,32,512]{2,1,0:T(8,128)(2,1)} %get-tuple-element.62), channel_id=1, source_target_pairs={{1,0},{2,1},{3,2},{4,3},{5,4},{6,5},{7,6},{8,7},{9,8},{10,9},{11,1... | collective-permute-start | bytes 786440 | tf_op jit(solution)/shard_map/ppermute | solution.py:557
  105.9 11.3 %copy-start.17 = (f32[128,128]{1,0:T(8,128)}, f32[128,128]{1,0:T(8,128)S(1)}, u32[]{:S(2)}) copy-start(f32[128,128]{1,0:T(8,128)S(1)} %get-tuple-element.60.back_ref) | copy-start | bytes 196612
  105.9 18.7 %copy-start.6 = (bf16[8,32,512]{2,1,0:T(8,128)(2,1)}, bf16[8,32,512]{2,1,0:T(8,128)(2,1)S(1)}, u32[]{:S(2)}) copy-start(bf16[8,32,512]{2,1,0:T(8,128)(2,1)S(1)} %collective-permute-done.4.zlo_ref) | copy-start | bytes 786436
  105.9 18.7 %copy-start.7 = (bf16[8,32,512]{2,1,0:T(8,128)(2,1)}, bf16[8,32,512]{2,1,0:T(8,128)(2,1)S(1)}, u32[]{:S(2)}) copy-start(bf16[8,32,512]{2,1,0:T(8,128)(2,1)S(1)} %collective-permute-done.5.zhi_ref) | copy-start | bytes 786436
  106.0 17.6 %collective-permute-start.6 = (bf16[192,512]{1,0:T(8,128)(2,1)S(1)}, bf16[192,512]{1,0:T(8,128)(2,1)S(1)}, u32[]{:S(2)}, u32[]{:S(2)}) collective-permute-start(bf16[192,512]{1,0:T(8,128)(2,1)S(1)} %get-tuple-element.66), channel_id=1, source_target_pairs={{0,16},{16,32},{32,48},{48,64},{64,80},{80,96},{96,112},{1,17},{17... | collective-permute-start | bytes 589832 | tf_op jit(solution)/shard_map/ppermute | solution.py:566
  111.5 12.1 %collective-permute-start.7 = (bf16[192,512]{1,0:T(8,128)(2,1)S(1)}, bf16[192,512]{1,0:T(8,128)(2,1)S(1)}, u32[]{:S(2)}, u32[]{:S(2)}) collective-permute-start(bf16[192,512]{1,0:T(8,128)(2,1)S(1)} %get-tuple-element.67), channel_id=1, source_target_pairs={{16,0},{32,16},{48,32},{64,48},{80,64},{96,80},{112,96},{17,1},{33... | collective-permute-start | bytes 589832 | tf_op jit(solution)/shard_map/ppermute | solution.py:567
  113.4 10.2 %all-to-all-start.6 = ((bf16[16,24,128]{2,1,0:T(8,128)(2,1)}), bf16[16,24,128]{2,1,0:T(8,128)(2,1)S(1)}, u32[]{:S(2)}, u32[]{:S(2)}) async-start(bf16[16,24,128]{2,1,0:T(8,128)(2,1)} %get-tuple-element.57), calls=%async_computation.6 | async-start | bytes 196608 | tf_op jit(solution)/shard_map/all_to_all | solution.py:541
  123.6 7.1 %copy-start.22 = (bf16[192,512]{1,0:T(8,128)(2,1)}, bf16[192,512]{1,0:T(8,128)(2,1)S(1)}, u32[]{:S(2)}) copy-start(bf16[192,512]{1,0:T(8,128)(2,1)S(1)} %collective-permute-done.6.ylo_ref) | copy-start | bytes 589828
  123.6 7.1 %copy-start.23 = (bf16[192,512]{1,0:T(8,128)(2,1)}, bf16[192,512]{1,0:T(8,128)(2,1)S(1)}, u32[]{:S(2)}) copy-start(bf16[192,512]{1,0:T(8,128)(2,1)S(1)} %collective-permute-done.7.yhi_ref) | copy-start | bytes 589828
  124.6 13.0 %all-to-all-start.7 = ((bf16[8,128,128]{2,1,0:T(8,128)(2,1)}), bf16[8,128,128]{2,1,0:T(8,128)(2,1)S(1)}, u32[]{:S(2)}, u32[]{:S(2)}) async-start(bf16[8,128,128]{2,1,0:T(8,128)(2,1)} %shard_map.150), calls=%async_computation.7 | async-start | bytes 524288 | tf_op jit(solution)/shard_map/all_to_all | solution.py:541
  137.7 0.7 copy-start.18

commit v3 on v2

--- a/solution.py
+++ b/solution.py
@@ -215,14 +215,11 @@
 
 
 def analyse_kernel(own_ref, tx_hbm, send_ref, front_ref, back_ref, first_ref, last_ref, field, tx, in_sems, out_sems):
-    fetched = begin([(tx_hbm, tx)] + [(own_ref.at[y], field.at[y]) for y in range(YL)], in_sems)
-    fetched[0].wait()
-    lines = []
-    for y in range(YL):
-        fetched[1 + y].wait()
-        lines.append(dot_nt(tx[...], field[y]))
+    finish(begin([(tx_hbm, tx), (own_ref, field)], in_sems))
     faces = begin(face_copies(field, front_ref, back_ref, first_ref, last_ref), out_sems)
+    lines = [dot_nt(tx[...], field[y]) for y in range(YL)]
     pack_lines(lines, send_ref)
+    send_ref[:, LINE_ROWS:] = jnp.zeros((GY, LINE_ROWS, 128), BF16)
     finish(faces)
 
 
@@ -279,7 +276,7 @@
         (zlo_ref, pad.at[1:9, 0:32]),
         (zhi_ref, pad.at[1:9, 160:192]),
         (ylo_ref, pad.at[0]),
-        (yhi_ref, pad.at[9]),
+        (yhi_ref, pad.at[YL + 1]),
     ]
 
 
@@ -298,11 +295,11 @@
         real = jnp.where(lane == k, fold_tiles(s_re * w_re - s_im * w_im), real)
         imag = jnp.where(lane == k, fold_tiles(s_re * w_im + s_im * w_re), imag)
     modes = jnp.concatenate([real, imag], 0) * gain_lanes()
-    send_ref[...] = z_inverse(modes, tzi_ref).astype(BF16).reshape(GZ, MODE_ROWS, 128)
+    send_ref[:, MODE_ROWS:] = jnp.zeros((GZ, 3 * MODE_ROWS, 128), BF16)
+    send_ref[:, 0:MODE_ROWS] = z_inverse(modes, tzi_ref).astype(BF16).reshape(GZ, MODE_ROWS, 128)
 
 
 def build_taps(kernel_ref, taps, flip):
-    zero = jnp.zeros((C, C), F32)
     row = lax.broadcasted_iota(jnp.int32, (C, C), 0)
     eye = jnp.where(row == lane_of((C, C)), 1.0, 0.0).astype(BF16)
     tap = {}
@@ -317,14 +314,14 @@
                 for dx in range(3):
                     tap[dx, dy, dz] = whole[:, dx * C : dx * C + C]
     for dx in range(3):
+        parts = []
+        for dy in range(3):
+            parts += [tap[dx, dy, dz] for dz in range(3)] + [jnp.zeros((C, 96), F32)]
+        base = jnp.concatenate(parts + [jnp.zeros((C, 64), F32)], 1)
         for z in range(ZL):
-            parts = [
-                tap[dx, dy, zin - z] if 0 <= zin - z < 3 else zero
-                for dy in range(3)
-                for zin in range(ZL + 2)
-            ]
             row = (dx * ZL + z) * C
-            taps[row : row + C, :] = jnp.concatenate(parts, 1).astype(BF16)
+            moved = pltpu.roll(base, z * C, 1) if z else base
+            taps[row : row + C, :] = moved[:, 0:576].astype(BF16)
 
 
 def conv_kernel(
@@ -337,80 +334,67 @@
         in_sems,
     )
     finish(fetched[0:2])
+    padded = fetched[2:]
     build_taps(kernel_ref, taps, flip)
     if not flip:
         row = lax.broadcasted_iota(jnp.int32, (128, C), 0) & 31
         picked = jnp.where(row == lane_of((128, C)), bias_ref[...], 0.0)
         bias = jnp.sum(picked, axis=1, keepdims=True)
-    finish(fetched[2:])
-
-    def step(y, carry):
-        window = pad[pl.ds(y, 3)].reshape(576, NX)
-        wide = dot(taps[...], window)
+    finish(padded)
+    copies = []
+    for y in range(YL):
+        wide = dot(taps[...], pad[y : y + 3].reshape(576, NX))
         total = wide[128:256] + shift_right(wide[0:128]) + shift_left(wide[256:384])
-        buffer[y] = total if flip else total + bias
-        pltpu.make_async_copy(buffer.at[y], out_ref.at[y], out_sems.at[y]).start()
-        return carry
-
-    lax.fori_loop(0, YL, step, 0)
-    for y in range(YL):
-        pltpu.make_async_copy(buffer.at[y], out_ref.at[y], out_sems.at[y]).wait()
+        buffer[y] = (total if flip else total + bias).astype(BF16)
+        if y % 4 == 3:
+            half = slice(y - 3, y + 1)
+            copies += begin([(buffer.at[half], out_ref.at[half])], out_sems.at[y // 4 : y // 4 + 1])
+    finish(copies)
 
 
 def slope_kernel(
-    recv_ref, local_ref, cot_ref, txi_hbm, slope_ref, front_ref, back_ref, first_ref, last_ref,
-    recv, local, cot, txi, field_ref, slopes, in_sems, out_sems,
+    recv_ref, local_ref, cot_ref, own_ref, zlo_ref, zhi_ref, ylo_ref, yhi_ref, txi_hbm, tx_hbm,
+    slope_ref, front_ref, back_ref, first_ref, last_ref, send_ref,
+    recv, local, cot, pad, txi, tx, field_ref, slopes, sums_ref, in_sems, out_sems,
 ):
     fetched = begin(
-        [(recv_ref, recv), (txi_hbm, txi)]
-        + [(local_ref.at[y], local.at[y]) for y in range(YL)]
-        + [(cot_ref.at[y], cot.at[y]) for y in range(YL)],
+        [(recv_ref, recv), (txi_hbm, txi), (tx_hbm, tx), (local_ref, local), (cot_ref, cot)]
+        + pad_copies(pad, own_ref, zlo_ref, zhi_ref, ylo_ref, yhi_ref),
         in_sems,
     )
     fetched[0].wait()
     place_fields(recv, field_ref)
-    fetched[1].wait()
+    finish(fetched[1:5])
     root = math.sqrt(2.0 / math.pi)
-    copies = []
+    lines = []
     for y in range(YL):
-        fetched[2 + y].wait()
-        fetched[2 + YL + y].wait()
-        pre = x_inverse(field_ref[y * 64 : y * 64 + 64], txi[...]) + local[y]
+        pre = x_inverse(field_ref[y * 64 : y * 64 + 64], txi[...]) + local[y].astype(F32)
         square = pre * pre
         bent = jnp.tanh(root * pre * (1.0 + 0.044715 * square))
         rate = 0.5 * (1.0 + bent) + 0.5 * root * pre * (1.0 - bent * bent) * (
             1.0 + 3.0 * 0.044715 * square
         )
-        slopes[y] = (cot[y].astype(F32) * rate).astype(BF16)
-        copies += begin([(slopes.at[y], slope_ref.at[y])], out_sems.at[y : y + 1])
-    copies += begin(face_copies(slopes, front_ref, back_ref, first_ref, last_ref), out_sems.at[YL : YL + 4])
-    finish(copies)
-
-
-def back_kernel(
-    slope_ref, own_ref, zlo_ref, zhi_ref, ylo_ref, yhi_ref, tx_hbm, send_ref,
-    slopes, pad, tx, sums_ref, in_sems,
-):
-    fetched = begin(
-        [(tx_hbm, tx)]
-        + [(slope_ref.at[y], slopes.at[y]) for y in range(YL)]
-        + pad_copies(pad, own_ref, zlo_ref, zhi_ref, ylo_ref, yhi_ref),
-        in_sems,
-    )
-    sums_ref[...] = jnp.zeros_like(sums_ref)
-    finish(fetched)
-    lines = []
+        slope = (cot[y].astype(F32) * rate).astype(BF16)
+        slopes[y] = slope
+        lines.append(dot_nt(tx[...], slope))
+    copies = begin(
+        face_copies(slopes, front_ref, back_ref, first_ref, last_ref) + [(slopes, slope_ref)], out_sems
+    )
+    pack_lines(lines, send_ref)
+    finish(fetched[5:])
     bias = jnp.zeros((128, 1), F32)
-    for y in range(YL):
-        slope = slopes[y]
-        lines.append(dot_nt(tx[...], slope))
-        wide = slope.astype(F32)
-        bias = bias + jnp.sum(wide, axis=1, keepdims=True)
-        three = jnp.concatenate(
-            [shift_left(wide).astype(BF16), slope, shift_right(wide).astype(BF16)], 0
-        )
-        sums_ref[...] += dot_nt(three, pad[y : y + 3].reshape(576, NX))
-    pack_lines(lines, send_ref)
+    for start in range(0, YL, 4):
+        left, right = [], []
+        for y in range(start, start + 4):
+            slope = slopes[y]
+            wide = slope.astype(F32)
+            bias = bias + jnp.sum(wide, axis=1, keepdims=True)
+            left.append(
+                jnp.concatenate([shift_left(wide).astype(BF16), slope, shift_right(wide).astype(BF16)], 0)
+            )
+            right.append(pad[y : y + 3].reshape(576, NX))
+        part = dot_nt(jnp.concatenate(left, 1), jnp.concatenate(right, 1))
+        sums_ref[...] = part if start == 0 else sums_ref[...] + part
     bias32 = bias[0:32] + bias[32:64] + bias[64:96] + bias[96:128]
     pieces = []
     for dx in range(3):
@@ -430,6 +414,7 @@
         high, low = split(rows)
         send_ref[g, LINE_ROWS : LINE_ROWS + GRAD_ROWS] = high
         send_ref[g, LINE_ROWS + GRAD_ROWS : LINE_ROWS + 2 * GRAD_ROWS] = low
+    finish(copies)
 
 
 def adjoint_kernel(recv_ref, weight_ref, tzf_ref, tzi_ref, send_ref, spec_ref, rows_ref):
@@ -450,6 +435,7 @@
         high, low = split(both)
         gather.append(dot(high, matrix) + dot(low, matrix))
     modes = (gather[0] + gather[1] + gather[2] + gather[3]) * gain_lanes()
+    send_ref[:, MODE_ROWS:] = jnp.zeros((GZ, 3 * MODE_ROWS, 128), BF16)
     block = z_inverse(modes, tzi_ref).astype(BF16)
     send_ref[:, 0:MODE_ROWS] = block.reshape(GZ, MODE_ROWS, 128)
     total = jnp.sum(recv_ref[:, MODE_ROWS : MODE_ROWS + TAIL_ROWS].astype(F32), axis=0)
@@ -485,18 +471,17 @@
     recv_ref, conv_ref, txi_hbm, grad_ref, kernel_ref, bias_ref,
     recv, conv, txi, field_ref, grads, in_sems, out_sems,
 ):
-    fetched = begin(
-        [(recv_ref, recv), (txi_hbm, txi)] + [(conv_ref.at[y], conv.at[y]) for y in range(YL)], in_sems
-    )
+    fetched = begin([(recv_ref, recv), (txi_hbm, txi), (conv_ref, conv)], in_sems)
     fetched[0].wait()
     place_fields(recv, field_ref)
-    fetched[1].wait()
+    finish(fetched[1:])
     copies = []
     for y in range(YL):
         back = x_inverse(field_ref[y * 64 : y * 64 + 64], txi[...])
-        fetched[2 + y].wait()
-        grads[y] = (back + conv[y]).astype(BF16)
-        copies += begin([(grads.at[y], grad_ref.at[y])], out_sems.at[y : y + 1])
+        grads[y] = (back + conv[y].astype(F32)).astype(BF16)
+        if y % 4 == 3:
+            half = slice(y - 3, y + 1)
+            copies += begin([(grads.at[half], grad_ref.at[half])], out_sems.at[y // 4 : y // 4 + 1])
     piece = []
     for g in range(7):
         high = recv[g, LINE_ROWS : LINE_ROWS + GRAD_ROWS].astype(F32)
@@ -572,10 +557,10 @@
     return call(
         functools.partial(conv_kernel, flip),
         [HBM] * 7,
-        [(HBM, shape((YL, 128, NX), F32))],
+        [(HBM, FIELD)],
         [
-            PAD, vmem((384, 576), BF16), vmem((YL, 128, NX), F32),
-            vmem((3, 3, C, 3 * C), BF16), vmem((1, C), F32), sems(7), sems(YL),
+            PAD, vmem((384, 576), BF16), vmem((YL, 128, NX), BF16),
+            vmem((3, 3, C, 3 * C), BF16), vmem((1, C), F32), sems(7), sems(2),
         ],
         LARGE,
         own, *halo, kernel, bias,
@@ -607,8 +592,8 @@
     send, front, back, first, last = call(
         analyse_kernel,
         [HBM] * 2,
-        [lines_out(LINE_ROWS)] + faces_out,
-        [vmem((YL, 128, NX), BF16), vmem((64, NX), BF16), sems(1 + YL), sems(4)],
+        [lines_out(2 * LINE_ROWS)] + faces_out,
+        [vmem((YL, 128, NX), BF16), vmem((64, NX), BF16), sems(2), sems(4)],
         LARGE,
         own, tx,
     )
@@ -620,7 +605,7 @@
     send, spectrum = call(
         mix_kernel,
         [AUTO] * 4,
-        [modes_out(MODE_ROWS), spectrum_out],
+        [modes_out(4 * MODE_ROWS), spectrum_out],
         [vmem((256, 128), F32)],
         SMALL,
         recv, weight, tzf, tzi,
@@ -631,27 +616,17 @@
     (send,) = call(spread_kernel, [AUTO] * 2, [lines_out(LINE_ROWS)], [], SMALL, recv, tyi)
     local = conv(False, after(own, send), halo, kernel_weight, bias)
     recv = exchange(send, "gy")
-    slope, front, back, first, last = call(
+    slope, front, back, first, last, send = call(
         slope_kernel,
-        [HBM] * 4,
-        [(HBM, FIELD)] + faces_out,
+        [HBM] * 10,
+        [(HBM, FIELD)] + faces_out + [lines_out(both_rows)],
         [
-            vmem((GY, LINE_ROWS, 128), BF16), vmem((YL, 128, NX), F32), vmem((YL, 128, NX), BF16),
-            vmem((192, NX), BF16), vmem((512, 128), F32), vmem((YL, 128, NX), BF16),
-            sems(2 + 2 * YL), sems(YL + 4),
+            vmem((GY, LINE_ROWS, 128), BF16), vmem((YL, 128, NX), BF16), vmem((YL, 128, NX), BF16), PAD,
+            vmem((192, NX), BF16), vmem((64, NX), BF16), vmem((512, 128), F32), vmem((YL, 128, NX), BF16),
+            vmem((384, 576), F32), sems(10), sems(5),
         ],
         LARGE,
-        recv, local, cot, txi,
-    )
-    (send,) = call(
-        back_kernel,
-        [HBM] * 7,
-        [lines_out(both_rows)],
-        [
-            vmem((YL, 128, NX), BF16), PAD, vmem((64, NX), BF16), vmem((384, 576), F32), sems(6 + YL),
-        ],
-        LARGE,
-        slope, own, *halo, tx,
+        recv, local, cot, own, *halo, txi, tx,
     )
     recv = exchange(send, "gy")
 
@@ -668,7 +643,7 @@
     send, back = call(
         adjoint_kernel,
         [AUTO] * 4,
-        [modes_out(tail_rows), spectrum_out],
+        [modes_out(4 * MODE_ROWS), spectrum_out],
         [vmem((256, 128), F32)],
         SMALL,
         recv, weight, tzf, tzi,
@@ -699,8 +674,8 @@
         [HBM] * 3,
         [(HBM, FIELD), (AUTO, shape((3, 3, C, 3 * C), F32)), (AUTO, shape((1, C), F32))],
         [
-            vmem((GY, both_rows, 128), BF16), vmem((YL, 128, NX), F32), vmem((192, NX), BF16),
-            vmem((512, 128), F32), vmem((YL, 128, NX), BF16), sems(2 + YL), sems(YL),
+            vmem((GY, both_rows, 128), BF16), vmem((YL, 128, NX), BF16), vmem((192, NX), BF16),
+            vmem((512, 128), F32), vmem((YL, 128, NX), BF16), sems(3), sems(2),
         ],
         LARGE,
         recv, conv_field, txi,

time: 144 us -> 129 us (0.90)
  blocking collectives: 44.7 us -> 27.5 us
  Pallas kernels: 43.2 us -> 33.8 us
  waiting for transfers between devices: 6.89 us -> 12.8 us
  starting transfers between devices: 42.7 us -> 47.6 us
    all_to_all x4 -> x2, blocking collectives: 44.7 us -> 27.5 us  [exchange(): return lax.all_to_all(blocks, axis, 0, 0, tiled=True)]
    pallas_call x15 -> x14, Pallas kernels: 43.2 us -> 33.8 us  [call(): pl.pallas_call(body, in_specs=ins, out_specs=[spec for spec, _ in outs],...]
    ppermute x2, waiting for transfers between devices: 0.01 us -> 6.85 us  [y_halos(): yhi = lax.ppermute(first, 'gy', [(i + 1, i) for i in range(GY - 1)])]
    all_to_all x4 -> x6, starting transfers between devices: 20.1 us -> 25.5 us  [exchange(): return lax.all_to_all(blocks, axis, 0, 0, tiled=True)]
    all_to_all x4 -> x6, waiting for transfers between devices: 6.87 us -> 5.27 us  [exchange(): return lax.all_to_all(blocks, axis, 0, 0, tiled=True)]
  transfers between devices with their start and end apart: 12 -> 14, of which waited for: 2 -> 7; matrix products, arithmetic and copies ran while one was open for 0% -> 0% of each run, Pallas kernels for 15% -> 14%
where the time goes in v3:
time: 129 us; the launch traced here: 128 us
  starting transfers between devices  47.6 us (37%)
  Pallas kernels  33.8 us (26%)
  blocking collectives  27.5 us (21%)
  waiting for transfers between devices  12.8 us (10%)
  local copies, waits for them, and re-layouts  4.9 us (4%)
    pallas_call x14, Pallas kernels, call(): pl.pallas_call(body, in_specs=ins, out_specs=[spec for spec, _ in outs],...  33.8 us
    all_to_all x2, blocking collectives, exchange(): return lax.all_to_all(blocks, axis, 0, 0, tiled=True)  27.5 us
    all_to_all x6, starting transfers between devices, exchange(): return lax.all_to_all(blocks, axis, 0, 0, tiled=True)  25.5 us
    ppermute x2, starting transfers between devices, y_halos(): ylo = lax.ppermute(last, 'gy', [(i, i + 1) for i in range(GY - 1)])  9.05 us
    ppermute x2, waiting for transfers between devices, y_halos(): yhi = lax.ppermute(first, 'gy', [(i + 1, i) for i in range(GY - 1)])  6.85 us
    ppermute x2, starting transfers between devices, z_halos(): zlo = lax.ppermute(back, 'gz', [(i, i + 1) for i in range(GZ - 1)])  6.64 us
    all_to_all x6, waiting for transfers between devices, exchange(): return lax.all_to_all(blocks, axis, 0, 0, tiled=True)  5.27 us
    unnamed x48, local copies, waits for them, and re-layouts  4.9 us
  transfers between devices with their start and end apart: 14, of which 7 were waited for; matrix products, arithmetic and copies ran while one was open for 0% of the time, Pallas kernels for 14%

profile of v3, /device:TPU:1, one launch (start us, length us, event | category | flops | bytes accessed | tf_op | source)
XLA Modules:
  0.0 127.7 jit_solution(11103950823811896503)
XLA Ops:
  0.6 0.0 copy-start
  0.6 3.0 %shard_map.138 = (bf16[8,128,128]{2,1,0:T(8,128)(2,1)}, bf16[8,32,512]{2,1,0:T(8,128)(2,1)}, bf16[8,32,512]{2,1,0:T(8,128)(2,1)}, bf16[128,512]{1,0:T(8,128)(2,1)}, bf16[128,512]{1,0:T(8,128)(2,1)}) custom-call(bf16[8,128,512]{2,1,0:T(8,128)(2,1)} %bitcast.9, bf16[64,512]{1,0:T(8,128)(2,1)} %constant.12.clone.tx_hbm), custom_call_target="tpu_custom_call" | custom-call | tf_op jit(solution)/shard_map/pallas_call | solution.py:515
  3.6 0.0 copy-start.3
  3.7 5.9 %all-to-all-start = ((bf16[8,128,128]{2,1,0:T(8,128)(2,1)}), bf16[8,128,128]{2,1,0:T(8,128)(2,1)S(1)}, u32[]{:S(2)}, u32[]{:S(2)}) async-start(bf16[8,128,128]{2,1,0:T(8,128)(2,1)} %get-tuple-element.42), calls=%async_computation | async-start | bytes 524288 | tf_op jit(solution)/shard_map/all_to_all | solution.py:526
  9.6 3.2 %collective-permute-start = (bf16[8,32,512]{2,1,0:T(8,128)(2,1)}, bf16[8,32,512]{2,1,0:T(8,128)(2,1)S(1)}, u32[]{:S(2)}, u32[]{:S(2)}) collective-permute-start(bf16[8,32,512]{2,1,0:T(8,128)(2,1)} %get-tuple-element.44), channel_id=1, source_target_pairs={{0,1},{1,2},{2,3},{3,4},{4,5},{5,6},{6,7},{7,8},{8,9},{9,10},{10,1... | collective-permute-start | bytes 786440 | tf_op jit(solution)/shard_map/ppermute | solution.py:541
  12.8 1.3 %collective-permute-start.1 = (bf16[8,32,512]{2,1,0:T(8,128)(2,1)}, bf16[8,32,512]{2,1,0:T(8,128)(2,1)S(1)}, u32[]{:S(2)}, u32[]{:S(2)}) collective-permute-start(bf16[8,32,512]{2,1,0:T(8,128)(2,1)} %get-tuple-element.45), channel_id=1, source_target_pairs={{1,0},{2,1},{3,2},{4,3},{5,4},{6,5},{7,6},{8,7},{9,8},{10,9},{11,1... | collective-permute-start | bytes 786440 | tf_op jit(solution)/shard_map/ppermute | solution.py:542
  14.1 2.0 %all-to-all-done.recv_ref = bf16[8,128,128]{2,1,0:T(8,128)(2,1)S(1)} async-done(((bf16[8,128,128]{2,1,0:T(8,128)(2,1)}), bf16[8,128,128]{2,1,0:T(8,128)(2,1)S(1)}, u32[]{:S(2)}, u32[]{:S(2)}) %all-to-all-start) | async-done | bytes 262176 | tf_op jit(solution)/shard_map/all_to_all | solution.py:526
  16.1 1.0 copy-done.4
  17.2 0.3 shard_map.139
  17.4 14.1 %all_to_all.40.recv_ref = bf16[16,16,128]{2,1,0:T(8,128)(2,1)S(1)} all-to-all(bf16[16,16,128]{2,1,0:T(8,128)(2,1)S(1)} %shard_map.139), channel_id=1, replica_groups=mesh['gy'=8,'gz'=16] {'gz'}, dimensions={0} | all-to-all | bytes 131072 | tf_op jit(solution)/shard_map/all_to_all | solution.py:526
  31.5 0.0 copy-done
  31.5 0.9 copy-done.8
  32.4 0.9 copy-done.10
  33.3 2.1 %shard_map.140 = (bf16[16,64,128]{2,1,0:T(8,128)(2,1)}, f32[128,128]{1,0:T(8,128)S(1)}) custom-call(bf16[16,16,128]{2,1,0:T(8,128)(2,1)S(1)} %all_to_all.40.recv_ref, bf16[64,8192]{1,0:T(8,128)(2,1)S(1)} %bitcast.7, bf16[2,128,256]{2,1,0:T(8,128)(2,1)S(1)} %copy-done.10, bf16[2,256,128]{2,1,0:T(8,128)(2,1)S(1)} %copy-done.8), custom_call_target="tpu_custom_call" | custom-call | tf_op jit(solution)/shard_map/pallas_call | solution.py:515
  35.4 0.6 copy-done.16
  36.0 3.5 %all-to-all-start.2 = ((bf16[16,64,128]{2,1,0:T(8,128)(2,1)}), bf16[16,64,128]{2,1,0:T(8,128)(2,1)S(1)}, u32[]{:S(2)}, u32[]{:S(2)}) async-start(bf16[16,64,128]{2,1,0:T(8,128)(2,1)} %get-tuple-element.43), calls=%async_computation.2 | async-start | bytes 524288 | tf_op jit(solution)/shard_map/all_to_all | solution.py:526
  39.6 0.0 collective-permute-done.zlo_ref
  39.6 0.0 copy-start.1
  39.6 0.0 collective-permute-done.1.zhi_ref
  39.6 0.0 copy-start.2
  39.6 0.0 copy-done.14
  39.6 0.0 copy-done.15
  39.7 4.5 %collective-permute-start.2 = (bf16[192,512]{1,0:T(8,128)(2,1)S(1)}, bf16[192,512]{1,0:T(8,128)(2,1)S(1)}, u32[]{:S(2)}, u32[]{:S(2)}) collective-permute-start(bf16[192,512]{1,0:T(8,128)(2,1)S(1)} %get-tuple-element.49), channel_id=1, source_target_pairs={{0,16},{16,32},{32,48},{48,64},{64,80},{80,96},{96,112},{1,17},{17... | collective-permute-start | bytes 589832 | tf_op jit(solution)/shard_map/ppermute | solution.py:551
  44.2 1.9 %collective-permute-start.3 = (bf16[192,512]{1,0:T(8,128)(2,1)S(1)}, bf16[192,512]{1,0:T(8,128)(2,1)S(1)}, u32[]{:S(2)}, u32[]{:S(2)}) collective-permute-start(bf16[192,512]{1,0:T(8,128)(2,1)S(1)} %get-tuple-element.50), channel_id=1, source_target_pairs={{16,0},{32,16},{48,32},{64,48},{80,64},{96,80},{112,96},{17,1},{33... | collective-permute-start | bytes 589832 | tf_op jit(solution)/shard_map/ppermute | solution.py:552
  46.1 0.7 collective-permute-done.2.ylo_ref
  46.8 4.4 %collective-permute-done.3.yhi_ref = bf16[192,512]{1,0:T(8,128)(2,1)S(1)} collective-permute-done((bf16[192,512]{1,0:T(8,128)(2,1)S(1)}, bf16[192,512]{1,0:T(8,128)(2,1)S(1)}, u32[]{:S(2)}, u32[]{:S(2)}) %collective-permute-start.3) | collective-permute-done | bytes 196640 | tf_op jit(solution)/shard_map/ppermute | solution.py:552
  51.2 0.0 all-to-all-done.2.recv_ref
  51.2 0.0 copy-done.3
  51.2 1.0 shard_map.142
  52.2 3.8 %all-to-all-start.3 = ((bf16[8,64,128]{2,1,0:T(8,128)(2,1)}), bf16[8,64,128]{2,1,0:T(8,128)(2,1)S(1)}, u32[]{:S(2)}, u32[]{:S(2)}) async-start(bf16[8,64,128]{2,1,0:T(8,128)(2,1)} %shard_map.142), calls=%async_computation.3 | async-start | bytes 262144 | tf_op jit(solution)/shard_map/all_to_all | solution.py:526
  56.0 0.0 copy-done.1
  56.0 0.0 copy-done.2
  56.0 0.0 copy-done.19
  56.0 0.0 copy-done.20
  56.0 5.1 %shard_map.143.local_ref = bf16[8,128,512]{2,1,0:T(8,128)(2,1)} custom-call(bf16[8,128,512]{2,1,0:T(8,128)(2,1)} %bitcast.10, bf16[8,32,512]{2,1,0:T(8,128)(2,1)} %copy-done.1, bf16[8,32,512]{2,1,0:T(8,128)(2,1)} %copy-done.2, bf16[192,512]{1,0:T(8,128)(2,1)} %copy-done.19, bf16[192,512]{1,0:T(8,128)(2,1)} %copy-done.20, bf16[3,3,32,96]{3,2,1,0:T(8,128)(2,1)} %kernel_hbm.3, ...), custom_call_target="tpu_custom_call" | custom-call | tf_op jit(solution)/shard_map/pallas_call | solution.py:515
  61.1 0.1 all-to-all-done.3.recv_ref
  61.3 0.7 copy-done.21
  61.9 7.5 %shard_map.144 = (bf16[8,128,512]{2,1,0:T(8,128)(2,1)}, bf16[8,32,512]{2,1,0:T(8,128)(2,1)}, bf16[8,32,512]{2,1,0:T(8,128)(2,1)}, bf16[128,512]{1,0:T(8,128)(2,1...) custom-call(bf16[8,64,128]{2,1,0:T(8,128)(2,1)} %copy-done.21, bf16[8,128,512]{2,1,0:T(8,128)(2,1)} %shard_map.143.local_ref, ...), custom_call_target="tpu_custom_call" | custom-call | tf_op jit(solution)/shard_map/pallas_call | solution.py:515
  69.4 0.0 copy-start.12
  69.4 4.8 %all-to-all-start.4 = ((bf16[8,128,128]{2,1,0:T(8,128)(2,1)}), bf16[8,128,128]{2,1,0:T(8,128)(2,1)S(1)}, u32[]{:S(2)}, u32[]{:S(2)}) async-start(bf16[8,128,128]{2,1,0:T(8,128)(2,1)} %get-tuple-element.57), calls=%async_computation.4 | async-start | bytes 524288 | tf_op jit(solution)/shard_map/all_to_all | solution.py:526
  74.3 3.4 %collective-permute-start.4 = (bf16[8,32,512]{2,1,0:T(8,128)(2,1)}, bf16[8,32,512]{2,1,0:T(8,128)(2,1)S(1)}, u32[]{:S(2)}, u32[]{:S(2)}) collective-permute-start(bf16[8,32,512]{2,1,0:T(8,128)(2,1)} %get-tuple-element.62), channel_id=1, source_target_pairs={{0,1},{1,2},{2,3},{3,4},{4,5},{5,6},{6,7},{7,8},{8,9},{9,10},{10,1... | collective-permute-start | bytes 786440 | tf_op jit(solution)/shard_map/ppermute | solution.py:541
  77.7 1.3 %collective-permute-start.5 = (bf16[8,32,512]{2,1,0:T(8,128)(2,1)}, bf16[8,32,512]{2,1,0:T(8,128)(2,1)S(1)}, u32[]{:S(2)}, u32[]{:S(2)}) collective-permute-start(bf16[8,32,512]{2,1,0:T(8,128)(2,1)} %get-tuple-element.63), channel_id=1, source_target_pairs={{1,0},{2,1},{3,2},{4,3},{5,4},{6,5},{7,6},{8,7},{9,8},{10,9},{11,1... | collective-permute-start | bytes 786440 | tf_op jit(solution)/shard_map/ppermute | solution.py:542
  79.0 1.8 %all-to-all-done.4.recv_ref = bf16[8,128,128]{2,1,0:T(8,128)(2,1)S(1)} async-done(((bf16[8,128,128]{2,1,0:T(8,128)(2,1)}), bf16[8,128,128]{2,1,0:T(8,128)(2,1)S(1)}, u32[]{:S(2)}, u32[]{:S(2)}) %all-to-all-start.4) | async-done | bytes 262176 | tf_op jit(solution)/shard_map/all_to_all | solution.py:526
  80.8 0.3 shard_map.145
  81.1 13.4 %all_to_all.41.recv_ref = bf16[16,24,128]{2,1,0:T(8,128)(2,1)S(1)} all-to-all(bf16[16,24,128]{2,1,0:T(8,128)(2,1)S(1)} %shard_map.145), channel_id=1, replica_groups=mesh['gy'=8,'gz'=16] {'gz'}, dimensions={0} | all-to-all | bytes 196608 | tf_op jit(solution)/shard_map/all_to_all | solution.py:526
  94.4 0.0 copy-done.9
  94.4 2.5 %shard_map.146 = (bf16[16,64,128]{2,1,0:T(8,128)(2,1)}, f32[128,128]{1,0:T(8,128)S(1)}) custom-call(bf16[16,24,128]{2,1,0:T(8,128)(2,1)S(1)} %all_to_all.41.recv_ref, bf16[64,8192]{1,0:T(8,128)(2,1)S(1)} %bitcast.8, bf16[2,128,256]{2,1,0:T(8,128)(2,1)S(1)} %copy-done.11, bf16[2,256,128]{2,1,0:T(8,128)(2,1)S(1)} %copy-done.9), custom_call_target="tpu_custom_call" | custom-call | tf_op jit(solution)/shard_map/pallas_call | solution.py:515
  96.9 3.5 %all-to-all-start.6 = ((bf16[16,64,128]{2,1,0:T(8,128)(2,1)}), bf16[16,64,128]{2,1,0:T(8,128)(2,1)S(1)}, u32[]{:S(2)}, u32[]{:S(2)}) async-start(bf16[16,64,128]{2,1,0:T(8,128)(2,1)} %get-tuple-element.58), calls=%async_computation.6 | async-start | bytes 524288 | tf_op jit(solution)/shard_map/all_to_all | solution.py:526
  100.5 0.0 collective-permute-done.4.zlo_ref
  100.5 0.0 collective-permute-done.5.zhi_ref
  100.6 4.5 %collective-permute-start.6 = (bf16[192,512]{1,0:T(8,128)(2,1)S(1)}, bf16[192,512]{1,0:T(8,128)(2,1)S(1)}, u32[]{:S(2)}, u32[]{:S(2)}) collective-permute-start(bf16[192,512]{1,0:T(8,128)(2,1)S(1)} %get-tuple-element.67), channel_id=1, source_target_pairs={{0,16},{16,32},{32,48},{48,64},{64,80},{80,96},{96,112},{1,17},{17... | collective-permute-start | bytes 589832 | tf_op jit(solution)/shard_map/ppermute | solution.py:551
  105.1 1.9 %collective-permute-start.7 = (bf16[192,512]{1,0:T(8,128)(2,1)S(1)}, bf16[192,512]{1,0:T(8,128)(2,1)S(1)}, u32[]{:S(2)}, u32[]{:S(2)}) collective-permute-start(bf16[192,512]{1,0:T(8,128)(2,1)S(1)} %get-tuple-element.68), channel_id=1, source_target_pairs={{16,0},{32,16},{48,32},{64,48},{80,64},{96,80},{112,96},{17,1},{33... | collective-permute-start | bytes 589832 | tf_op jit(solution)/shard_map/ppermute | solution.py:552
  107.0 2.6 %shard_map.147 = f32[64,8192]{1,0:T(8,128)} custom-call(f32[128,128]{1,0:T(8,128)} %copy-done.16, f32[128,128]{1,0:T(8,128)} %copy-done.17), custom_call_target="tpu_custom_call" | custom-call | tf_op jit(solution)/shard_map/pallas_call | solution.py:515
  109.6 0.0 collective-permute-done.6.ylo_ref
  109.6 2.5 %collective-permute-done.7.yhi_ref = bf16[192,512]{1,0:T(8,128)(2,1)S(1)} collective-permute-done((bf16[192,512]{1,0:T(8,128)(2,1)S(1)}, bf16[192,512]{1,0:T(8,128)(2,1)S(1)}, u32[]{:S(2)}, u32[]{:S(2)}) %collective-permute-start.7) | collective-permute-done | bytes 196640 | tf_op jit(solution)/shard_map/ppermute | solution.py:552
  112.1 0.0 all-to-all-done.6.recv_ref
  112.1 1.0 shard_map.149
  113.1 0.0 copy-done.7
  113.1 3.8 %all-to-all-start.7 = ((bf16[8,128,128]{2,1,0:T(8,128)(2,1)}), bf16[8,128,128]{2,1,0:T(8,128)(2,1)S(1)}, u32[]{:S(2)}, u32[]{:S(2)}) async-start(bf16[8,128,128]{2,1,0:T(8,128)(2,1)} %shard_map.149), calls=%async_computation.7 | async-start | bytes 524288 | tf_op jit(solution)/shard_map/all_to_all | solution.py:526
  116.9 0.0 copy-done.23
  117.0 5.1 %shard_map.150.conv_ref = bf16[8,128,512]{2,1,0:T(8,128)(2,1)} custom-call(bf16[8,128,512]{2,1,0:T(8,128)(2,1)} %get-tuple-element.71.own_ref, bf16[8,32,512]{2,1,0:T(8,128)(2,1)} %copy-done.6, bf16[8,32,512]{2,1,0:T(8,128)(2,1)} %copy-done.7, bf16[192,512]{1,0:T(8,128)(2,1)} %copy-done.22, bf16[192,512]{1,0:T(8,128)(2,1)} %copy-done.23, ...), custom_call_target="tpu_custom_call" | custom-call | tf_op jit(solution)/shard_map/pallas_call | solution.py:515
  122.1 1.4 %all-to-all-done.7.recv_ref = bf16[8,128,128]{2,1,0:T(8,128)(2,1)S(1)} async-done(((bf16[8,128,128]{2,1,0:T(8,128)(2,1)}), bf16[8,128,128]{2,1,0:T(8,128)(2,1)S(1)}, u32[]{:S(2)}, u32[]{:S(2)}) %all-to-all-start.7) | async-done | bytes 262176 | tf_op jit(solution)/shard_map/all_to_all | solution.py:526
  123.5 0.7 copy-done.18
  124.2 3.4 %shard_map.151 = (bf16[8,128,512]{2,1,0:T(8,128)(2,1)}, f32[3,3,32,96]{3,2,1,0:T(8,128)}, f32[1,32]{1,0:T(1,128)}) custom-call(bf16[8,128,128]{2,1,0:T(8,128)(2,1)} %copy-done.18, bf16[8,128,512]{2,1,0:T(8,128)(2,1)} %shard_map.150.conv_ref, bf16[192,512]{1,0:T(8,128)(2,1)} %constant.13.clone.txi_hbm), custom_call_target="tpu_custom_call" | custom-call | tf_op jit(solution)/shard_map/pallas_call | solution.py:515
  (28 shorter events, 0.1 us)
Async XLA Ops:
  0.6 30.9 %copy-start = (bf16[2,32,8192]{2,1,0:T(8,128)(2,1)S(1)}, bf16[2,32,8192]{2,1,0:T(8,128)(2,1)}, u32[]{:S(2)}) copy-start(bf16[2,32,8192]{2,1,0:T(8,128)(2,1)} %param.13) | copy-start | bytes 3145732
  3.6 47.6 %copy-start.3 = (bf16[2,512,256]{2,1,0:T(8,128)(2,1)S(1)}, bf16[2,512,256]{2,1,0:T(8,128)(2,1)}, u32[]{:S(2)}) copy-start(bf16[2,512,256]{2,1,0:T(8,128)(2,1)} %constant.15.clone.table_ref) | copy-start | bytes 1572868
  3.7 12.4 %all-to-all-start = ((bf16[8,128,128]{2,1,0:T(8,128)(2,1)}), bf16[8,128,128]{2,1,0:T(8,128)(2,1)S(1)}, u32[]{:S(2)}, u32[]{:S(2)}) async-start(bf16[8,128,128]{2,1,0:T(8,128)(2,1)} %get-tuple-element.42), calls=%async_computation | async-start | bytes 524288 | tf_op jit(solution)/shard_map/all_to_all | solution.py:526
  9.6 30.0 %collective-permute-start = (bf16[8,32,512]{2,1,0:T(8,128)(2,1)}, bf16[8,32,512]{2,1,0:T(8,128)(2,1)S(1)}, u32[]{:S(2)}, u32[]{:S(2)}) collective-permute-start(bf16[8,32,512]{2,1,0:T(8,128)(2,1)} %get-tuple-element.44), channel_id=1, source_target_pairs={{0,1},{1,2},{2,3},{3,4},{4,5},{5,6},{6,7},{7,8},{8,9},{9,10},{10,1... | collective-permute-start | bytes 786440 | tf_op jit(solution)/shard_map/ppermute | solution.py:541
  12.8 26.8 %collective-permute-start.1 = (bf16[8,32,512]{2,1,0:T(8,128)(2,1)}, bf16[8,32,512]{2,1,0:T(8,128)(2,1)S(1)}, u32[]{:S(2)}, u32[]{:S(2)}) collective-permute-start(bf16[8,32,512]{2,1,0:T(8,128)(2,1)} %get-tuple-element.45), channel_id=1, source_target_pairs={{1,0},{2,1},{3,2},{4,3},{5,4},{6,5},{7,6},{8,7},{9,8},{10,9},{11,1... | collective-permute-start | bytes 786440 | tf_op jit(solution)/shard_map/ppermute | solution.py:542
  16.1 1.0 copy-start.4
  17.1 22.5 %copy-start.14 = (bf16[128,512]{1,0:T(8,128)(2,1)S(1)}, bf16[128,512]{1,0:T(8,128)(2,1)}, u32[]{:S(2)}) copy-start(bf16[128,512]{1,0:T(8,128)(2,1)} %get-tuple-element.47.own_first_ref) | copy-start | bytes 393220
  17.1 22.5 %copy-start.15 = (bf16[128,512]{1,0:T(8,128)(2,1)S(1)}, bf16[128,512]{1,0:T(8,128)(2,1)}, u32[]{:S(2)}) copy-start(bf16[128,512]{1,0:T(8,128)(2,1)} %get-tuple-element.48.own_last_ref) | copy-start | bytes 393220
  31.5 0.9 copy-start.8
  32.4 0.9 copy-start.10
  35.4 0.6 copy-start.16
  36.0 15.2 %all-to-all-start.2 = ((bf16[16,64,128]{2,1,0:T(8,128)(2,1)}), bf16[16,64,128]{2,1,0:T(8,128)(2,1)S(1)}, u32[]{:S(2)}, u32[]{:S(2)}) async-start(bf16[16,64,128]{2,1,0:T(8,128)(2,1)} %get-tuple-element.43), calls=%async_computation.2 | async-start | bytes 524288 | tf_op jit(solution)/shard_map/all_to_all | solution.py:526
  39.6 16.4 %copy-start.1 = (bf16[8,32,512]{2,1,0:T(8,128)(2,1)}, bf16[8,32,512]{2,1,0:T(8,128)(2,1)S(1)}, u32[]{:S(2)}) copy-start(bf16[8,32,512]{2,1,0:T(8,128)(2,1)S(1)} %collective-permute-done.zlo_ref) | copy-start | bytes 786436
  39.6 16.4 %copy-start.2 = (bf16[8,32,512]{2,1,0:T(8,128)(2,1)}, bf16[8,32,512]{2,1,0:T(8,128)(2,1)S(1)}, u32[]{:S(2)}) copy-start(bf16[8,32,512]{2,1,0:T(8,128)(2,1)S(1)} %collective-permute-done.1.zhi_ref) | copy-start | bytes 786436
  39.7 7.2 %collective-permute-start.2 = (bf16[192,512]{1,0:T(8,128)(2,1)S(1)}, bf16[192,512]{1,0:T(8,128)(2,1)S(1)}, u32[]{:S(2)}, u32[]{:S(2)}) collective-permute-start(bf16[192,512]{1,0:T(8,128)(2,1)S(1)} %get-tuple-element.49), channel_id=1, source_target_pairs={{0,16},{16,32},{32,48},{48,64},{64,80},{80,96},{96,112},{1,17},{17... | collective-permute-start | bytes 589832 | tf_op jit(solution)/shard_map/ppermute | solution.py:551
  44.2 7.0 %collective-permute-start.3 = (bf16[192,512]{1,0:T(8,128)(2,1)S(1)}, bf16[192,512]{1,0:T(8,128)(2,1)S(1)}, u32[]{:S(2)}, u32[]{:S(2)}) collective-permute-start(bf16[192,512]{1,0:T(8,128)(2,1)S(1)} %get-tuple-element.50), channel_id=1, source_target_pairs={{16,0},{32,16},{48,32},{64,48},{80,64},{96,80},{112,96},{17,1},{33... | collective-permute-start | bytes 589832 | tf_op jit(solution)/shard_map/ppermute | solution.py:552
  46.8 9.2 %copy-start.19 = (bf16[192,512]{1,0:T(8,128)(2,1)}, bf16[192,512]{1,0:T(8,128)(2,1)S(1)}, u32[]{:S(2)}) copy-start(bf16[192,512]{1,0:T(8,128)(2,1)S(1)} %collective-permute-done.2.ylo_ref) | copy-start | bytes 589828
  51.2 4.8 %copy-start.20 = (bf16[192,512]{1,0:T(8,128)(2,1)}, bf16[192,512]{1,0:T(8,128)(2,1)S(1)}, u32[]{:S(2)}) copy-start(bf16[192,512]{1,0:T(8,128)(2,1)S(1)} %collective-permute-done.3.yhi_ref) | copy-start | bytes 589828
  52.2 9.1 %all-to-all-start.3 = ((bf16[8,64,128]{2,1,0:T(8,128)(2,1)}), bf16[8,64,128]{2,1,0:T(8,128)(2,1)S(1)}, u32[]{:S(2)}, u32[]{:S(2)}) async-start(bf16[8,64,128]{2,1,0:T(8,128)(2,1)} %shard_map.142), calls=%async_computation.3 | async-start | bytes 262144 | tf_op jit(solution)/shard_map/all_to_all | solution.py:526
  61.3 0.7 copy-start.21
  61.9 18.8 %copy-start.5 = (bf16[2,256,512]{2,1,0:T(8,128)(2,1)S(1)}, bf16[2,256,512]{2,1,0:T(8,128)(2,1)}, u32[]{:S(2)}) copy-start(bf16[2,256,512]{2,1,0:T(8,128)(2,1)} %constant.14.clone.table_ref) | copy-start | bytes 1572868
  61.9 32.5 %copy-start.9 = (bf16[2,256,128]{2,1,0:T(8,128)(2,1)S(1)}, bf16[2,256,128]{2,1,0:T(8,128)(2,1)}, u32[]{:S(2)}) copy-start(bf16[2,256,128]{2,1,0:T(8,128)(2,1)} %constant.17.clone.tzi_ref) | copy-start | bytes 393220
  61.9 32.5 %copy-start.11 = (bf16[2,128,256]{2,1,0:T(8,128)(2,1)S(1)}, bf16[2,128,256]{2,1,0:T(8,128)(2,1)}, u32[]{:S(2)}) copy-start(bf16[2,128,256]{2,1,0:T(8,128)(2,1)} %constant.16.clone.tzf_ref) | copy-start | bytes 393220
  69.4 31.1 %copy-start.12 = (bf16[128,512]{1,0:T(8,128)(2,1)S(1)}, bf16[128,512]{1,0:T(8,128)(2,1)}, u32[]{:S(2)}) copy-start(bf16[128,512]{1,0:T(8,128)(2,1)} %get-tuple-element.65.own_first_ref) | copy-start | bytes 393220
  69.4 31.1 %copy-start.13 = (bf16[128,512]{1,0:T(8,128)(2,1)S(1)}, bf16[128,512]{1,0:T(8,128)(2,1)}, u32[]{:S(2)}) copy-start(bf16[128,512]{1,0:T(8,128)(2,1)} %get-tuple-element.66.own_last_ref) | copy-start | bytes 393220
  69.4 11.3 %all-to-all-start.4 = ((bf16[8,128,128]{2,1,0:T(8,128)(2,1)}), bf16[8,128,128]{2,1,0:T(8,128)(2,1)S(1)}, u32[]{:S(2)}, u32[]{:S(2)}) async-start(bf16[8,128,128]{2,1,0:T(8,128)(2,1)} %get-tuple-element.57), calls=%async_computation.4 | async-start | bytes 524288 | tf_op jit(solution)/shard_map/all_to_all | solution.py:526
  74.3 26.2 %collective-permute-start.4 = (bf16[8,32,512]{2,1,0:T(8,128)(2,1)}, bf16[8,32,512]{2,1,0:T(8,128)(2,1)S(1)}, u32[]{:S(2)}, u32[]{:S(2)}) collective-permute-start(bf16[8,32,512]{2,1,0:T(8,128)(2,1)} %get-tuple-element.62), channel_id=1, source_target_pairs={{0,1},{1,2},{2,3},{3,4},{4,5},{5,6},{6,7},{7,8},{8,9},{9,10},{10,1... | collective-permute-start | bytes 786440 | tf_op jit(solution)/shard_map/ppermute | solution.py:541
  77.7 22.8 %collective-permute-start.5 = (bf16[8,32,512]{2,1,0:T(8,128)(2,1)}, bf16[8,32,512]{2,1,0:T(8,128)(2,1)S(1)}, u32[]{:S(2)}, u32[]{:S(2)}) collective-permute-start(bf16[8,32,512]{2,1,0:T(8,128)(2,1)} %get-tuple-element.63), channel_id=1, source_target_pairs={{1,0},{2,1},{3,2},{4,3},{5,4},{6,5},{7,6},{8,7},{9,8},{10,9},{11,1... | collective-permute-start | bytes 786440 | tf_op jit(solution)/shard_map/ppermute | solution.py:542
  96.9 10.1 %copy-start.17 = (f32[128,128]{1,0:T(8,128)}, f32[128,128]{1,0:T(8,128)S(1)}, u32[]{:S(2)}) copy-start(f32[128,128]{1,0:T(8,128)S(1)} %get-tuple-element.61.back_ref) | copy-start | bytes 196612
  96.9 15.1 %all-to-all-start.6 = ((bf16[16,64,128]{2,1,0:T(8,128)(2,1)}), bf16[16,64,128]{2,1,0:T(8,128)(2,1)S(1)}, u32[]{:S(2)}, u32[]{:S(2)}) async-start(bf16[16,64,128]{2,1,0:T(8,128)(2,1)} %get-tuple-element.58), calls=%async_computation.6 | async-start | bytes 524288 | tf_op jit(solution)/shard_map/all_to_all | solution.py:526
  100.5 12.6 %copy-start.6 = (bf16[8,32,512]{2,1,0:T(8,128)(2,1)}, bf16[8,32,512]{2,1,0:T(8,128)(2,1)S(1)}, u32[]{:S(2)}) copy-start(bf16[8,32,512]{2,1,0:T(8,128)(2,1)S(1)} %collective-permute-done.4.zlo_ref) | copy-start | bytes 786436
  100.5 12.6 %copy-start.7 = (bf16[8,32,512]{2,1,0:T(8,128)(2,1)}, bf16[8,32,512]{2,1,0:T(8,128)(2,1)S(1)}, u32[]{:S(2)}) copy-start(bf16[8,32,512]{2,1,0:T(8,128)(2,1)S(1)} %collective-permute-done.5.zhi_ref) | copy-start | bytes 786436
  100.6 9.0 %collective-permute-start.6 = (bf16[192,512]{1,0:T(8,128)(2,1)S(1)}, bf16[192,512]{1,0:T(8,128)(2,1)S(1)}, u32[]{:S(2)}, u32[]{:S(2)}) collective-permute-start(bf16[192,512]{1,0:T(8,128)(2,1)S(1)} %get-tuple-element.67), channel_id=1, source_target_pairs={{0,16},{16,32},{32,48},{48,64},{64,80},{80,96},{96,112},{1,17},{17... | collective-permute-start | bytes 589832 | tf_op jit(solution)/shard_map/ppermute | solution.py:551
  105.1 7.0 %collective-permute-start.7 = (bf16[192,512]{1,0:T(8,128)(2,1)S(1)}, bf16[192,512]{1,0:T(8,128)(2,1)S(1)}, u32[]{:S(2)}, u32[]{:S(2)}) collective-permute-start(bf16[192,512]{1,0:T(8,128)(2,1)S(1)} %get-tuple-element.68), channel_id=1, source_target_pairs={{16,0},{32,16},{48,32},{64,48},{80,64},{96,80},{112,96},{17,1},{33... | collective-permute-start | bytes 589832 | tf_op jit(solution)/shard_map/ppermute | solution.py:552
  109.6 7.3 %copy-start.22 = (bf16[192,512]{1,0:T(8,128)(2,1)}, bf16[192,512]{1,0:T(8,128)(2,1)S(1)}, u32[]{:S(2)}) copy-start(bf16[192,512]{1,0:T(8,128)(2,1)S(1)} %collective-permute-done.6.ylo_ref) | copy-start | bytes 589828
  112.1 4.9 %copy-start.23 = (bf16[192,512]{1,0:T(8,128)(2,1)}, bf16[192,512]{1,0:T(8,128)(2,1)S(1)}, u32[]{:S(2)}) copy-start(bf16[192,512]{1,0:T(8,128)(2,1)S(1)} %collective-permute-done.7.yhi_ref) | copy-start | bytes 589828
  113.1 10.3 %all-to-all-start.7 = ((bf16[8,128,128]{2,1,0:T(8,128)(2,1)}), bf16[8,128,128]{2,1,0:T(8,128)(2,1)S(1)}, u32[]{:S(2)}, u32[]{:S(2)}) async-start(bf16[8,128,128]{2,1,0:T(8,128)(2,1)} %shard_map.149), calls=%async_computation.7 | async-start | bytes 524288 | tf_op jit(solution)/shard_map/all_to_all | solution.py:526
  123.4 0.7 copy-start.18

commit v4 on v3

--- a/solution.py
+++ b/solution.py
@@ -22,6 +22,7 @@
 SCALE = 1.0 / math.sqrt(NX * NY * NZ)
 F32, BF16 = jnp.float32, jnp.bfloat16
 LARGE = 60 * 1024 * 1024
+MEDIUM = 48 * 1024 * 1024
 SMALL = 16 * 1024 * 1024
 
 
@@ -62,28 +63,48 @@
     turn = angle(freqs(32, NY), np.arange(NY), NY)
     table = rotation(turn, -1.0).reshape(GZ, 2, 2, NY, 2)
     full = np.einsum("gkpyq,ab->gakpyqb", table, np.eye(KXL)).reshape(256, 512)
-    return np.stack(split_np(full))
+    return full
 
 
 def z_forward_table():
     turn = angle(freqs(32, NZ), np.arange(NZ), NZ)
     table = SCALE * rotation(turn, -1.0).reshape(32, 2, GZ, ZL, 2)
     full = np.einsum("kpgzq,ab->pakzbqg", table, np.eye(2)).reshape(128, 256)
-    return np.stack(split_np(full))
+    return full
 
 
 def z_inverse_table():
     turn = angle(np.arange(NZ), freqs(32, NZ), NZ)
     table = SCALE * rotation(turn, 1.0).reshape(GZ, ZL, 2, 32, 2)
     full = np.einsum("gzpkq,ab->gapzqbk", table, np.eye(2)).reshape(256, 128)
-    return np.stack(split_np(full))
+    return full
 
 
 def y_inverse_table():
     turn = angle(np.arange(NY), freqs(32, NY), NY)
     table = rotation(turn, 1.0).reshape(GY, YL, 2, GZ, 2, 2)
     full = np.einsum("dypgkq,ab->dapygkqb", table, np.eye(ZL)).reshape(512, 256)
-    return np.stack(split_np(full))
+    return full
+
+
+def side_by_side(table):
+    return np.concatenate(split_np(table), 1)
+
+
+def joint_table():
+    z_inverse = side_by_side(z_inverse_table())
+    return np.concatenate(
+        [
+            *split_np(y_forward_table()),
+            side_by_side(y_inverse_table()),
+            side_by_side(z_forward_table()),
+            np.concatenate([z_inverse, np.zeros_like(z_inverse)], 1),
+        ],
+        0,
+    )
+
+
+Y_INVERSE, Z_FORWARD, Z_INVERSE = 512, 1024, 1152
 
 
 def split(value):
@@ -137,12 +158,15 @@
             swap_blocks([rows_ref[pl.ds(k * 4 + j, GZ, stride=16), :] for k in range(KXL)])
         )
     joined = jnp.concatenate([turned[j][z] for z in range(ZL) for j in range(4)], 0).astype(BF16)
-    return dot(table_ref[0], joined) + dot(table_ref[1], joined)
+    rows = slice(Z_FORWARD, Z_FORWARD + 128)
+    return dot(table_ref[rows, 0:256], joined) + dot(table_ref[rows, 256:512], joined)
 
 
 def z_inverse(modes, table_ref):
     high, low = split(modes)
-    return dot(table_ref[0], high) + dot(table_ref[1], high) + dot(table_ref[0], low)
+    rows = slice(Z_INVERSE, Z_INVERSE + 256)
+    table_high, table_low = table_ref[rows, 0:128], table_ref[rows, 128:256]
+    return dot(table_high, high) + dot(table_low, high) + dot(table_high, low)
 
 
 def gain_lanes():
@@ -225,7 +249,7 @@
 
 def y_kernel(recv_ref, table_ref, send_ref):
     lines = recv_ref[:, 0:LINE_ROWS].reshape(512, 128)
-    out = dot(table_ref[0], lines) + dot(table_ref[1], lines)
+    out = dot(table_ref[0:256], lines) + dot(table_ref[256:512], lines)
     send_ref[:, 0:MODE_ROWS] = out.astype(BF16).reshape(GZ, MODE_ROWS, 128)
 
 
@@ -247,7 +271,8 @@
 
 def spread_kernel(recv_ref, table_ref, send_ref):
     modes = recv_ref[:, 0:MODE_ROWS].reshape(256, 128)
-    out = dot(table_ref[0], modes) + dot(table_ref[1], modes)
+    rows = slice(Y_INVERSE, Y_INVERSE + 512)
+    out = dot(table_ref[rows, 0:256], modes) + dot(table_ref[rows, 256:512], modes)
     send_ref[:, 0:LINE_ROWS] = out.astype(BF16).reshape(GY, LINE_ROWS, 128)
 
 
@@ -263,25 +288,32 @@
         send_ref[g, LINE_ROWS : LINE_ROWS + 2 * GRAD_ROWS] = both
 
 
-def edges_kernel(own_first_ref, own_last_ref, zlo_ref, zhi_ref, first_ref, last_ref):
-    for y, own, row in ((0, own_first_ref, first_ref), (YL - 1, own_last_ref, last_ref)):
-        row[0:32] = zlo_ref[y]
-        row[32:160] = own[...]
-        row[160:192] = zhi_ref[y]
-
-
-def pad_copies(pad, own_ref, zlo_ref, zhi_ref, ylo_ref, yhi_ref):
+def own_core():
+    return lax.rem(lax.axis_index("gy"), 2)
+
+
+def edges_kernel(own_first_ref, own_last_ref, zlo_ref, zhi_ref, inner_ref, outer_ref):
+    first, last = [
+        jnp.concatenate([zlo_ref[y], own[...], zhi_ref[y]], 0)
+        for y, own in ((0, own_first_ref), (YL - 1, own_last_ref))
+    ]
+    even = own_core() == 0
+    inner_ref[...] = jnp.where(even, last, first)
+    outer_ref[...] = jnp.where(even, first, last)
+
+
+def pad_copies(pad, own_ref, zlo_ref, zhi_ref, inner_ref, outer_ref):
     return [
         (own_ref, pad.at[1:9, 32:160]),
         (zlo_ref, pad.at[1:9, 0:32]),
         (zhi_ref, pad.at[1:9, 160:192]),
-        (ylo_ref, pad.at[0]),
-        (yhi_ref, pad.at[YL + 1]),
+        (inner_ref, pad.at[(1 - own_core()) * (YL + 1)]),
+        (outer_ref, pad.at[own_core() * (YL + 1)]),
     ]
 
 
-def mix_kernel(recv_ref, weight_ref, tzf_ref, tzi_ref, send_ref, spec_ref, rows_ref):
-    spectrum = collect_spectrum(recv_ref, tzf_ref, rows_ref)
+def mix_kernel(recv_ref, weight_ref, table_ref, send_ref, spec_ref, rows_ref):
+    spectrum = collect_spectrum(recv_ref, table_ref, rows_ref)
     spec_ref[...] = spectrum
     matrix = repeat_matrix()
     lane = lane_of((64, 128)) // 32
@@ -296,7 +328,7 @@
         imag = jnp.where(lane == k, fold_tiles(s_re * w_im + s_im * w_re), imag)
     modes = jnp.concatenate([real, imag], 0) * gain_lanes()
     send_ref[:, MODE_ROWS:] = jnp.zeros((GZ, 3 * MODE_ROWS, 128), BF16)
-    send_ref[:, 0:MODE_ROWS] = z_inverse(modes, tzi_ref).astype(BF16).reshape(GZ, MODE_ROWS, 128)
+    send_ref[:, 0:MODE_ROWS] = z_inverse(modes, table_ref).astype(BF16).reshape(GZ, MODE_ROWS, 128)
 
 
 def build_taps(kernel_ref, taps, flip):
@@ -325,12 +357,12 @@
 
 
 def conv_kernel(
-    flip, own_ref, zlo_ref, zhi_ref, ylo_ref, yhi_ref, kernel_hbm, bias_hbm, out_ref,
+    flip, own_ref, zlo_ref, zhi_ref, inner_ref, outer_ref, kernel_hbm, bias_hbm, out_ref,
     pad, taps, buffer, kernel_ref, bias_ref, in_sems, out_sems,
 ):
     fetched = begin(
         [(kernel_hbm, kernel_ref), (bias_hbm, bias_ref)]
-        + pad_copies(pad, own_ref, zlo_ref, zhi_ref, ylo_ref, yhi_ref),
+        + pad_copies(pad, own_ref, zlo_ref, zhi_ref, inner_ref, outer_ref),
         in_sems,
     )
     finish(fetched[0:2])
@@ -353,13 +385,13 @@
 
 
 def slope_kernel(
-    recv_ref, local_ref, cot_ref, own_ref, zlo_ref, zhi_ref, ylo_ref, yhi_ref, txi_hbm, tx_hbm,
+    recv_ref, local_ref, cot_ref, own_ref, zlo_ref, zhi_ref, inner_ref, outer_ref, txi_hbm, tx_hbm,
     slope_ref, front_ref, back_ref, first_ref, last_ref, send_ref,
     recv, local, cot, pad, txi, tx, field_ref, slopes, sums_ref, in_sems, out_sems,
 ):
     fetched = begin(
         [(recv_ref, recv), (txi_hbm, txi), (tx_hbm, tx), (local_ref, local), (cot_ref, cot)]
-        + pad_copies(pad, own_ref, zlo_ref, zhi_ref, ylo_ref, yhi_ref),
+        + pad_copies(pad, own_ref, zlo_ref, zhi_ref, inner_ref, outer_ref),
         in_sems,
     )
     fetched[0].wait()
@@ -417,8 +449,8 @@
     finish(copies)
 
 
-def adjoint_kernel(recv_ref, weight_ref, tzf_ref, tzi_ref, send_ref, spec_ref, rows_ref):
-    spectrum = collect_spectrum(recv_ref, tzf_ref, rows_ref)
+def adjoint_kernel(recv_ref, weight_ref, table_ref, send_ref, spec_ref, rows_ref):
+    spectrum = collect_spectrum(recv_ref, table_ref, rows_ref)
     spec_ref[...] = spectrum
     row = lax.broadcasted_iota(jnp.int32, (1024, 128), 0) // 32
     lane = lane_of((1024, 128))
@@ -436,7 +468,7 @@
         gather.append(dot(high, matrix) + dot(low, matrix))
     modes = (gather[0] + gather[1] + gather[2] + gather[3]) * gain_lanes()
     send_ref[:, MODE_ROWS:] = jnp.zeros((GZ, 3 * MODE_ROWS, 128), BF16)
-    block = z_inverse(modes, tzi_ref).astype(BF16)
+    block = z_inverse(modes, table_ref).astype(BF16)
     send_ref[:, 0:MODE_ROWS] = block.reshape(GZ, MODE_ROWS, 128)
     total = jnp.sum(recv_ref[:, MODE_ROWS : MODE_ROWS + TAIL_ROWS].astype(F32), axis=0)
     total = total + pltpu.roll(total, TAIL_ROWS - 2, 0)
@@ -547,10 +579,13 @@
     return call(edges_kernel, [AUTO] * 4, [(AUTO, EDGE)] * 2, [], SMALL, first, last, zlo, zhi)
 
 
-def y_halos(first, last):
-    ylo = lax.ppermute(last, "gy", [(i, i + 1) for i in range(GY - 1)])
-    yhi = lax.ppermute(first, "gy", [(i + 1, i) for i in range(GY - 1)])
-    return ylo, yhi
+def y_halos(inner, outer):
+    ahead = [(i, i + 1) for i in range(1, GY - 1, 2)]
+    behind = [(i, i - 1) for i in range(2, GY, 2)]
+    return (
+        lax.ppermute(inner, "gy", [(i, i ^ 1) for i in range(GY)]),
+        lax.ppermute(outer, "gy", ahead + behind),
+    )
 
 
 def conv(flip, own, halo, kernel, bias):
@@ -574,10 +609,7 @@
     bias = channel_bias.reshape(1, C)
     tx = jnp.asarray(x_forward_table())
     txi = jnp.asarray(x_inverse_table())
-    ty = jnp.asarray(y_forward_table())
-    tyi = jnp.asarray(y_inverse_table())
-    tzf = jnp.asarray(z_forward_table())
-    tzi = jnp.asarray(z_inverse_table())
+    table = jnp.asarray(joint_table())
     faces_out = [(HBM, SIDE)] * 2 + [(HBM, FACE)] * 2
     spectrum_out = (AUTO, shape((128, 128), F32))
 
@@ -600,20 +632,20 @@
     recv = exchange(send, "gy")
 
     zlo, zhi = z_halos(front, back)
-    (send,) = call(y_kernel, [AUTO] * 2, [modes_out(MODE_ROWS)], [], SMALL, recv, ty)
+    (send,) = call(y_kernel, [AUTO] * 2, [modes_out(MODE_ROWS)], [], SMALL, recv, table)
     recv = exchange(send, "gz")
     send, spectrum = call(
         mix_kernel,
-        [AUTO] * 4,
+        [AUTO] * 3,
         [modes_out(4 * MODE_ROWS), spectrum_out],
         [vmem((256, 128), F32)],
         SMALL,
-        recv, weight, tzf, tzi,
+        recv, weight, table,
     )
     halo = (zlo, zhi, *y_halos(*y_edges(after(first, send), last, zlo, zhi)))
     recv = exchange(send, "gz")
     recv, *halo = lax.optimization_barrier((recv, *halo))
-    (send,) = call(spread_kernel, [AUTO] * 2, [lines_out(LINE_ROWS)], [], SMALL, recv, tyi)
+    (send,) = call(spread_kernel, [AUTO] * 2, [lines_out(LINE_ROWS)], [], SMALL, recv, table)
     local = conv(False, after(own, send), halo, kernel_weight, bias)
     recv = exchange(send, "gy")
     slope, front, back, first, last, send = call(
@@ -637,16 +669,16 @@
         [modes_out(tail_rows)],
         [vmem((GRAD_ROWS, 128), F32), vmem((GZ * TAIL_ROWS, 128), F32)],
         SMALL,
-        recv, ty,
+        recv, table,
     )
     recv = exchange(send, "gz")
     send, back = call(
         adjoint_kernel,
-        [AUTO] * 4,
+        [AUTO] * 3,
         [modes_out(4 * MODE_ROWS), spectrum_out],
         [vmem((256, 128), F32)],
         SMALL,
-        recv, weight, tzf, tzi,
+        recv, weight, table,
     )
     halo = (zlo, zhi, *y_halos(*y_edges(after(first, send), last, zlo, zhi)))
     recv = exchange(send, "gz")
@@ -655,7 +687,7 @@
         [AUTO] * 2,
         [(HBM, shape((64, 8192), F32))],
         [vmem((64, 8192), F32), sems(KXL)],
-        LARGE,
+        MEDIUM,
         after(spectrum, send), back,
     )
     recv, grad_spectral, *halo = lax.optimization_barrier((recv, grad_spectral, *halo))
@@ -665,7 +697,7 @@
         [lines_out(both_rows)],
         [vmem((GZ * TAIL_ROWS, 128), F32), vmem((2 * GRAD_ROWS, 128), F32)],
         SMALL,
-        recv, tyi,
+        recv, table,
     )
     recv = exchange(send, "gy")
     conv_field = conv(True, after(slope, send), halo, kernel_weight, bias)
@@ -677,7 +709,7 @@
             vmem((GY, both_rows, 128), BF16), vmem((YL, 128, NX), BF16), vmem((192, NX), BF16),
             vmem((512, 128), F32), vmem((YL, 128, NX), BF16), sems(3), sems(2),
         ],
-        LARGE,
+        MEDIUM,
         recv, conv_field, txi,
     )
     return (

time: 129 us -> 122 us (0.946)
  starting transfers between devices: 47.6 us -> 44 us
  local copies, waits for them, and re-layouts: 4.9 us -> 2.58 us
  waiting for transfers between devices: 12.8 us -> 15 us
  Pallas kernels: 33.8 us -> 32.2 us
    ppermute x4, starting transfers between devices: 12.9 us -> 9.23 us  [the longest x2 5.05 us: y_halos(): lax.ppermute(inner, 'gy', [(i, i ^ 1) for i in range(GY)])]
    unnamed x48 -> x36, local copies, waits for them, and re-layouts: 4.9 us -> 2.58 us
    pallas_call x14, Pallas kernels: 33.8 us -> 32.2 us  [call(): pl.pallas_call(body, in_specs=ins, out_specs=[spec for spec, _ in outs],...]
  transfers between devices with their start and end apart: 14 -> 14, of which waited for: 7 -> 6; matrix products, arithmetic and copies ran while one was open for 0% -> 0% of each run, Pallas kernels for 14% -> 14%
where the time goes in v4:
time: 122 us; the launch traced here: 121 us
  starting transfers between devices  44 us (36%)
  Pallas kernels  32.2 us (26%)
  blocking collectives  26.3 us (22%)
  waiting for transfers between devices  15 us (12%)
  local copies, waits for them, and re-layouts  2.58 us (2%)
    pallas_call x14, Pallas kernels, call(): pl.pallas_call(body, in_specs=ins, out_specs=[spec for spec, _ in outs],...  32.2 us
    all_to_all x6, starting transfers between devices, exchange(): return lax.all_to_all(blocks, axis, 0, 0, tiled=True)  26.6 us
    all_to_all x2, blocking collectives, exchange(): return lax.all_to_all(blocks, axis, 0, 0, tiled=True)  26.3 us
    ppermute x2, waiting for transfers between devices, y_halos(): lax.ppermute(outer, 'gy', ahead + behind)  8.6 us
    all_to_all x6, waiting for transfers between devices, exchange(): return lax.all_to_all(blocks, axis, 0, 0, tiled=True)  6.4 us
    ppermute x2, starting transfers between devices, z_halos(): zlo = lax.ppermute(back, 'gz', [(i, i + 1) for i in range(GZ - 1)])  5.41 us
    ppermute x2, starting transfers between devices, y_halos(): lax.ppermute(inner, 'gy', [(i, i ^ 1) for i in range(GY)])  5.05 us
    ppermute x2, starting transfers between devices, y_halos(): lax.ppermute(outer, 'gy', ahead + behind)  4.18 us
  transfers between devices with their start and end apart: 14, of which 6 were waited for; matrix products, arithmetic and copies ran while one was open for 0% of the time, Pallas kernels for 14%

profile of v4, /device:TPU:1, one launch (start us, length us, event | category | flops | bytes accessed | tf_op | source)
XLA Modules:
  0.0 121.3 jit_solution(3933922042754593891)
XLA Ops:
  0.6 0.0 copy-start
  0.6 0.0 copy-start.2
  0.7 3.1 %shard_map.111 = (bf16[8,128,128]{2,1,0:T(8,128)(2,1)}, bf16[8,32,512]{2,1,0:T(8,128)(2,1)}, bf16[8,32,512]{2,1,0:T(8,128)(2,1)}, bf16[128,512]{1,0:T(8,128)(2,1)}, bf16[128,512]{1,0:T(8,128)(2,1)}) custom-call(bf16[8,128,512]{2,1,0:T(8,128)(2,1)} %bitcast.9, bf16[64,512]{1,0:T(8,128)(2,1)} %constant.6.clone.tx_hbm), custom_call_target="tpu_custom_call" | custom-call | tf_op jit(solution)/shard_map/pallas_call | solution.py:547
  3.7 5.8 %all-to-all-start = ((bf16[8,128,128]{2,1,0:T(8,128)(2,1)}), bf16[8,128,128]{2,1,0:T(8,128)(2,1)S(1)}, u32[]{:S(2)}, u32[]{:S(2)}) async-start(bf16[8,128,128]{2,1,0:T(8,128)(2,1)} %get-tuple-element.42), calls=%async_computation | async-start | bytes 524288 | tf_op jit(solution)/shard_map/all_to_all | solution.py:558
  9.5 3.2 %collective-permute-start = (bf16[8,32,512]{2,1,0:T(8,128)(2,1)}, bf16[8,32,512]{2,1,0:T(8,128)(2,1)S(1)}, u32[]{:S(2)}, u32[]{:S(2)}) collective-permute-start(bf16[8,32,512]{2,1,0:T(8,128)(2,1)} %get-tuple-element.44), channel_id=1, source_target_pairs={{0,1},{1,2},{2,3},{3,4},{4,5},{5,6},{6,7},{7,8},{8,9},{9,10},{10,1... | collective-permute-start | bytes 786440 | tf_op jit(solution)/shard_map/ppermute | solution.py:573
  12.7 0.0 copy-start.10
  12.8 0.0 copy-start.11
  12.8 1.4 %collective-permute-start.1 = (bf16[8,32,512]{2,1,0:T(8,128)(2,1)}, bf16[8,32,512]{2,1,0:T(8,128)(2,1)S(1)}, u32[]{:S(2)}, u32[]{:S(2)}) collective-permute-start(bf16[8,32,512]{2,1,0:T(8,128)(2,1)} %get-tuple-element.45), channel_id=1, source_target_pairs={{1,0},{2,1},{3,2},{4,3},{5,4},{6,5},{7,6},{8,7},{9,8},{10,9},{11,1... | collective-permute-start | bytes 786440 | tf_op jit(solution)/shard_map/ppermute | solution.py:574
  14.2 1.8 %all-to-all-done.recv_ref = bf16[8,128,128]{2,1,0:T(8,128)(2,1)S(1)} async-done(((bf16[8,128,128]{2,1,0:T(8,128)(2,1)}), bf16[8,128,128]{2,1,0:T(8,128)(2,1)S(1)}, u32[]{:S(2)}, u32[]{:S(2)}) %all-to-all-start) | async-done | bytes 262176 | tf_op jit(solution)/shard_map/all_to_all | solution.py:558
  16.0 0.0 copy-done
  16.0 0.3 shard_map.112
  16.3 14.1 %all_to_all.40.recv_ref = bf16[16,16,128]{2,1,0:T(8,128)(2,1)S(1)} all-to-all(bf16[16,16,128]{2,1,0:T(8,128)(2,1)S(1)} %shard_map.112), channel_id=1, replica_groups=mesh['gy'=8,'gz'=16] {'gz'}, dimensions={0} | all-to-all | bytes 131072 | tf_op jit(solution)/shard_map/all_to_all | solution.py:558
  30.4 0.0 copy-done.2
  30.4 2.1 %shard_map.113 = (bf16[16,64,128]{2,1,0:T(8,128)(2,1)}, f32[128,128]{1,0:T(8,128)S(1)}) custom-call(bf16[16,16,128]{2,1,0:T(8,128)(2,1)S(1)} %all_to_all.40.recv_ref, bf16[64,8192]{1,0:T(8,128)(2,1)S(1)} %bitcast.7, bf16[1408,512]{1,0:T(8,128)(2,1)S(1)} %copy-done), custom_call_target="tpu_custom_call" | custom-call | tf_op jit(solution)/shard_map/pallas_call | solution.py:547
  32.5 0.6 copy-done.12
  33.1 3.5 %all-to-all-start.2 = ((bf16[16,64,128]{2,1,0:T(8,128)(2,1)}), bf16[16,64,128]{2,1,0:T(8,128)(2,1)S(1)}, u32[]{:S(2)}, u32[]{:S(2)}) async-start(bf16[16,64,128]{2,1,0:T(8,128)(2,1)} %get-tuple-element.43), calls=%async_computation.2 | async-start | bytes 524288 | tf_op jit(solution)/shard_map/all_to_all | solution.py:558
  36.7 0.0 collective-permute-done.zlo_ref
  36.7 0.0 copy-start.3
  36.7 0.0 collective-permute-done.1.zhi_ref
  36.7 0.0 copy-start.4
  36.7 0.0 copy-done.10
  36.7 0.0 copy-done.11
  36.7 0.1 shard_map.114
  36.8 2.5 %collective-permute-start.2 = (bf16[192,512]{1,0:T(8,128)(2,1)S(1)}, bf16[192,512]{1,0:T(8,128)(2,1)S(1)}, u32[]{:S(2)}, u32[]{:S(2)}) collective-permute-start(bf16[192,512]{1,0:T(8,128)(2,1)S(1)} %get-tuple-element.49), channel_id=1, source_target_pairs={{0,16},{16,0},{32,48},{48,32},{64,80},{80,64},{96,112},{112,96},{1... | collective-permute-start | bytes 589832 | tf_op jit(solution)/shard_map/ppermute | solution.py:586
  39.3 2.1 %collective-permute-start.3 = (bf16[192,512]{1,0:T(8,128)(2,1)S(1)}, bf16[192,512]{1,0:T(8,128)(2,1)}, u32[]{:S(2)}, u32[]{:S(2)}) collective-permute-start(bf16[192,512]{1,0:T(8,128)(2,1)S(1)} %get-tuple-element.50), channel_id=1, source_target_pairs={{16,32},{48,64},{80,96},{32,16},{64,48},{96,80},{17,33},{49,65},{8... | collective-permute-start | bytes 589832 | tf_op jit(solution)/shard_map/ppermute | solution.py:587
  41.4 0.0 collective-permute-done.2.inner_ref
  41.4 0.0 copy-start.14
  41.5 5.2 %collective-permute-done.3.outer_ref = bf16[192,512]{1,0:T(8,128)(2,1)} collective-permute-done((bf16[192,512]{1,0:T(8,128)(2,1)S(1)}, bf16[192,512]{1,0:T(8,128)(2,1)}, u32[]{:S(2)}, u32[]{:S(2)}) %collective-permute-start.3) | collective-permute-done | bytes 196640 | tf_op jit(solution)/shard_map/ppermute | solution.py:587
  46.6 0.0 all-to-all-done.2.recv_ref
  46.6 1.0 shard_map.115
  47.6 4.5 %all-to-all-start.3 = ((bf16[8,64,128]{2,1,0:T(8,128)(2,1)}), bf16[8,64,128]{2,1,0:T(8,128)(2,1)S(1)}, u32[]{:S(2)}, u32[]{:S(2)}) async-start(bf16[8,64,128]{2,1,0:T(8,128)(2,1)} %shard_map.115), calls=%async_computation.3 | async-start | bytes 262144 | tf_op jit(solution)/shard_map/all_to_all | solution.py:558
  52.0 0.0 copy-done.3
  52.0 0.0 copy-done.4
  52.0 5.1 %shard_map.116.local_ref = bf16[8,128,512]{2,1,0:T(8,128)(2,1)} custom-call(bf16[8,128,512]{2,1,0:T(8,128)(2,1)} %bitcast.10, bf16[8,32,512]{2,1,0:T(8,128)(2,1)} %copy-done.3, bf16[8,32,512]{2,1,0:T(8,128)(2,1)} %copy-done.4, bf16[192,512]{1,0:T(8,128)(2,1)} %copy-done.14, bf16[192,512]{1,0:T(8,128)(2,1)} %collective-permute-done.3.outer_ref, ...), custom_call_target="tpu_custom_call" | custom-call | tf_op jit(solution)/shard_map/pallas_call | solution.py:547
  57.1 0.2 all-to-all-done.3.recv_ref
  57.3 0.7 copy-done.15
  58.0 7.4 %shard_map.117 = (bf16[8,128,512]{2,1,0:T(8,128)(2,1)}, bf16[8,32,512]{2,1,0:T(8,128)(2,1)}, bf16[8,32,512]{2,1,0:T(8,128)(2,1)}, bf16[128,512]{1,0:T(8,128)(2,1...) custom-call(bf16[8,64,128]{2,1,0:T(8,128)(2,1)} %copy-done.15, bf16[8,128,512]{2,1,0:T(8,128)(2,1)} %shard_map.116.local_ref, ...), custom_call_target="tpu_custom_call" | custom-call | tf_op jit(solution)/shard_map/pallas_call | solution.py:547
  65.4 4.7 %all-to-all-start.4 = ((bf16[8,128,128]{2,1,0:T(8,128)(2,1)}), bf16[8,128,128]{2,1,0:T(8,128)(2,1)S(1)}, u32[]{:S(2)}, u32[]{:S(2)}) async-start(bf16[8,128,128]{2,1,0:T(8,128)(2,1)} %get-tuple-element.57), calls=%async_computation.4 | async-start | bytes 524288 | tf_op jit(solution)/shard_map/all_to_all | solution.py:558
  70.1 2.2 %collective-permute-start.4 = (bf16[8,32,512]{2,1,0:T(8,128)(2,1)}, bf16[8,32,512]{2,1,0:T(8,128)(2,1)S(1)}, u32[]{:S(2)}, u32[]{:S(2)}) collective-permute-start(bf16[8,32,512]{2,1,0:T(8,128)(2,1)} %get-tuple-element.62), channel_id=1, source_target_pairs={{0,1},{1,2},{2,3},{3,4},{4,5},{5,6},{6,7},{7,8},{8,9},{9,10},{10,1... | collective-permute-start | bytes 786440 | tf_op jit(solution)/shard_map/ppermute | solution.py:573
  72.3 1.3 %collective-permute-start.5 = (bf16[8,32,512]{2,1,0:T(8,128)(2,1)}, bf16[8,32,512]{2,1,0:T(8,128)(2,1)S(1)}, u32[]{:S(2)}, u32[]{:S(2)}) collective-permute-start(bf16[8,32,512]{2,1,0:T(8,128)(2,1)} %get-tuple-element.63), channel_id=1, source_target_pairs={{1,0},{2,1},{3,2},{4,3},{5,4},{6,5},{7,6},{8,7},{9,8},{10,9},{11,1... | collective-permute-start | bytes 786440 | tf_op jit(solution)/shard_map/ppermute | solution.py:574
  73.6 3.0 %all-to-all-done.4.recv_ref = bf16[8,128,128]{2,1,0:T(8,128)(2,1)S(1)} async-done(((bf16[8,128,128]{2,1,0:T(8,128)(2,1)}), bf16[8,128,128]{2,1,0:T(8,128)(2,1)S(1)}, u32[]{:S(2)}, u32[]{:S(2)}) %all-to-all-start.4) | async-done | bytes 262176 | tf_op jit(solution)/shard_map/all_to_all | solution.py:558
  76.6 0.3 shard_map.118
  76.9 12.2 %all_to_all.41.recv_ref = bf16[16,24,128]{2,1,0:T(8,128)(2,1)S(1)} all-to-all(bf16[16,24,128]{2,1,0:T(8,128)(2,1)S(1)} %shard_map.118), channel_id=1, replica_groups=mesh['gy'=8,'gz'=16] {'gz'}, dimensions={0} | all-to-all | bytes 196608 | tf_op jit(solution)/shard_map/all_to_all | solution.py:558
  89.1 2.5 %shard_map.119 = (bf16[16,64,128]{2,1,0:T(8,128)(2,1)}, f32[128,128]{1,0:T(8,128)S(1)}) custom-call(bf16[16,24,128]{2,1,0:T(8,128)(2,1)S(1)} %all_to_all.41.recv_ref, bf16[64,8192]{1,0:T(8,128)(2,1)S(1)} %bitcast.8, bf16[1408,512]{1,0:T(8,128)(2,1)S(1)} %copy-done), custom_call_target="tpu_custom_call" | custom-call | tf_op jit(solution)/shard_map/pallas_call | solution.py:547
  91.6 3.5 %all-to-all-start.6 = ((bf16[16,64,128]{2,1,0:T(8,128)(2,1)}), bf16[16,64,128]{2,1,0:T(8,128)(2,1)S(1)}, u32[]{:S(2)}, u32[]{:S(2)}) async-start(bf16[16,64,128]{2,1,0:T(8,128)(2,1)} %get-tuple-element.58), calls=%async_computation.6 | async-start | bytes 524288 | tf_op jit(solution)/shard_map/all_to_all | solution.py:558
  95.2 0.0 collective-permute-done.4.zlo_ref
  95.2 0.0 collective-permute-done.5.zhi_ref
  95.2 0.1 shard_map.121
  95.3 2.5 %collective-permute-start.6 = (bf16[192,512]{1,0:T(8,128)(2,1)S(1)}, bf16[192,512]{1,0:T(8,128)(2,1)S(1)}, u32[]{:S(2)}, u32[]{:S(2)}) collective-permute-start(bf16[192,512]{1,0:T(8,128)(2,1)S(1)} %get-tuple-element.67), channel_id=1, source_target_pairs={{0,16},{16,0},{32,48},{48,32},{64,80},{80,64},{96,112},{112,96},{1... | collective-permute-start | bytes 589832 | tf_op jit(solution)/shard_map/ppermute | solution.py:586
  97.8 2.1 %collective-permute-start.7 = (bf16[192,512]{1,0:T(8,128)(2,1)S(1)}, bf16[192,512]{1,0:T(8,128)(2,1)S(1)}, u32[]{:S(2)}, u32[]{:S(2)}) collective-permute-start(bf16[192,512]{1,0:T(8,128)(2,1)S(1)} %get-tuple-element.68), channel_id=1, source_target_pairs={{16,32},{48,64},{80,96},{32,16},{64,48},{96,80},{17,33},{49,65},{8... | collective-permute-start | bytes 589832 | tf_op jit(solution)/shard_map/ppermute | solution.py:587
  99.9 0.0 copy-done.13
  99.9 1.7 %shard_map.120 = f32[64,8192]{1,0:T(8,128)} custom-call(f32[128,128]{1,0:T(8,128)S(1)} %copy-done.13, f32[128,128]{1,0:T(8,128)S(1)} %get-tuple-element.61.back_ref), custom_call_target="tpu_custom_call" | custom-call | tf_op jit(solution)/shard_map/pallas_call | solution.py:547
  101.6 0.0 collective-permute-done.6.inner_ref
  101.6 0.0 copy-start.16
  101.6 3.4 %collective-permute-done.7.outer_ref = bf16[192,512]{1,0:T(8,128)(2,1)S(1)} collective-permute-done((bf16[192,512]{1,0:T(8,128)(2,1)S(1)}, bf16[192,512]{1,0:T(8,128)(2,1)S(1)}, u32[]{:S(2)}, u32[]{:S(2)}) %collective-permute-start.7) | collective-permute-done | bytes 196640 | tf_op jit(solution)/shard_map/ppermute | solution.py:587
  105.1 0.0 all-to-all-done.6.recv_ref
  105.1 1.0 shard_map.122
  106.1 0.0 copy-done.5
  106.1 4.6 %all-to-all-start.7 = ((bf16[8,128,128]{2,1,0:T(8,128)(2,1)}), bf16[8,128,128]{2,1,0:T(8,128)(2,1)S(1)}, u32[]{:S(2)}, u32[]{:S(2)}) async-start(bf16[8,128,128]{2,1,0:T(8,128)(2,1)} %shard_map.122), calls=%async_computation.7 | async-start | bytes 524288 | tf_op jit(solution)/shard_map/all_to_all | solution.py:558
  110.7 0.0 copy-done.17
  110.7 5.1 %shard_map.123.conv_ref = bf16[8,128,512]{2,1,0:T(8,128)(2,1)} custom-call(bf16[8,128,512]{2,1,0:T(8,128)(2,1)} %get-tuple-element.71.own_ref, bf16[8,32,512]{2,1,0:T(8,128)(2,1)} %copy-done.5, bf16[8,32,512]{2,1,0:T(8,128)(2,1)} %copy-done.6, bf16[192,512]{1,0:T(8,128)(2,1)} %copy-done.16, bf16[192,512]{1,0:T(8,128)(2,1)} %copy-done.17, ...), custom_call_target="tpu_custom_call" | custom-call | tf_op jit(solution)/shard_map/pallas_call | solution.py:547
  115.8 1.4 %all-to-all-done.7.recv_ref = bf16[8,128,128]{2,1,0:T(8,128)(2,1)S(1)} async-done(((bf16[8,128,128]{2,1,0:T(8,128)(2,1)}), bf16[8,128,128]{2,1,0:T(8,128)(2,1)S(1)}, u32[]{:S(2)}, u32[]{:S(2)}) %all-to-all-start.7) | async-done | bytes 262176 | tf_op jit(solution)/shard_map/all_to_all | solution.py:558
  117.2 1.2 %copy-done.1 = bf16[8,128,512]{2,1,0:T(8,128)(2,1)S(1)} copy-done((bf16[8,128,512]{2,1,0:T(8,128)(2,1)S(1)}, bf16[8,128,512]{2,1,0:T(8,128)(2,1)}, u32[]{:S(2)}) %copy-start.1) | copy-done | bytes 1048600
  118.4 2.7 %shard_map.124 = (bf16[8,128,512]{2,1,0:T(8,128)(2,1)}, f32[3,3,32,96]{3,2,1,0:T(8,128)}, f32[1,32]{1,0:T(1,128)}) custom-call(bf16[8,128,128]{2,1,0:T(8,128)(2,1)S(1)} %all-to-all-done.7.recv_ref, bf16[8,128,512]{2,1,0:T(8,128)(2,1)S(1)} %copy-done.1, bf16[192,512]{1,0:T(8,128)(2,1)S(1)} %copy-done.7), custom_call_target="tpu_custom_call" | custom-call | tf_op jit(solution)/shard_map/pallas_call | solution.py:547
  (16 shorter events, 0.0 us)
Async XLA Ops:
  0.6 15.4 %copy-start = (bf16[1408,512]{1,0:T(8,128)(2,1)S(1)}, bf16[1408,512]{1,0:T(8,128)(2,1)}, u32[]{:S(2)}) copy-start(bf16[1408,512]{1,0:T(8,128)(2,1)} %constant.8.clone.table_ref) | copy-start | bytes 4325380
  0.6 29.8 %copy-start.2 = (bf16[2,32,8192]{2,1,0:T(8,128)(2,1)S(1)}, bf16[2,32,8192]{2,1,0:T(8,128)(2,1)}, u32[]{:S(2)}) copy-start(bf16[2,32,8192]{2,1,0:T(8,128)(2,1)} %param.10) | copy-start | bytes 3145732
  3.7 12.3 %all-to-all-start = ((bf16[8,128,128]{2,1,0:T(8,128)(2,1)}), bf16[8,128,128]{2,1,0:T(8,128)(2,1)S(1)}, u32[]{:S(2)}, u32[]{:S(2)}) async-start(bf16[8,128,128]{2,1,0:T(8,128)(2,1)} %get-tuple-element.42), calls=%async_computation | async-start | bytes 524288 | tf_op jit(solution)/shard_map/all_to_all | solution.py:558
  9.5 27.1 %collective-permute-start = (bf16[8,32,512]{2,1,0:T(8,128)(2,1)}, bf16[8,32,512]{2,1,0:T(8,128)(2,1)S(1)}, u32[]{:S(2)}, u32[]{:S(2)}) collective-permute-start(bf16[8,32,512]{2,1,0:T(8,128)(2,1)} %get-tuple-element.44), channel_id=1, source_target_pairs={{0,1},{1,2},{2,3},{3,4},{4,5},{5,6},{6,7},{7,8},{8,9},{9,10},{10,1... | collective-permute-start | bytes 786440 | tf_op jit(solution)/shard_map/ppermute | solution.py:573
  12.7 24.0 %copy-start.10 = (bf16[128,512]{1,0:T(8,128)(2,1)S(1)}, bf16[128,512]{1,0:T(8,128)(2,1)}, u32[]{:S(2)}) copy-start(bf16[128,512]{1,0:T(8,128)(2,1)} %get-tuple-element.47.own_first_ref) | copy-start | bytes 393220
  12.8 24.0 %copy-start.11 = (bf16[128,512]{1,0:T(8,128)(2,1)S(1)}, bf16[128,512]{1,0:T(8,128)(2,1)}, u32[]{:S(2)}) copy-start(bf16[128,512]{1,0:T(8,128)(2,1)} %get-tuple-element.48.own_last_ref) | copy-start | bytes 393220
  12.8 23.9 %collective-permute-start.1 = (bf16[8,32,512]{2,1,0:T(8,128)(2,1)}, bf16[8,32,512]{2,1,0:T(8,128)(2,1)S(1)}, u32[]{:S(2)}, u32[]{:S(2)}) collective-permute-start(bf16[8,32,512]{2,1,0:T(8,128)(2,1)} %get-tuple-element.45), channel_id=1, source_target_pairs={{1,0},{2,1},{3,2},{4,3},{5,4},{6,5},{7,6},{8,7},{9,8},{10,9},{11,1... | collective-permute-start | bytes 786440 | tf_op jit(solution)/shard_map/ppermute | solution.py:574
  32.5 0.6 copy-start.12
  33.1 13.5 %all-to-all-start.2 = ((bf16[16,64,128]{2,1,0:T(8,128)(2,1)}), bf16[16,64,128]{2,1,0:T(8,128)(2,1)S(1)}, u32[]{:S(2)}, u32[]{:S(2)}) async-start(bf16[16,64,128]{2,1,0:T(8,128)(2,1)} %get-tuple-element.43), calls=%async_computation.2 | async-start | bytes 524288 | tf_op jit(solution)/shard_map/all_to_all | solution.py:558
  36.7 15.3 %copy-start.3 = (bf16[8,32,512]{2,1,0:T(8,128)(2,1)}, bf16[8,32,512]{2,1,0:T(8,128)(2,1)S(1)}, u32[]{:S(2)}) copy-start(bf16[8,32,512]{2,1,0:T(8,128)(2,1)S(1)} %collective-permute-done.zlo_ref) | copy-start | bytes 786436
  36.7 15.3 %copy-start.4 = (bf16[8,32,512]{2,1,0:T(8,128)(2,1)}, bf16[8,32,512]{2,1,0:T(8,128)(2,1)S(1)}, u32[]{:S(2)}) copy-start(bf16[8,32,512]{2,1,0:T(8,128)(2,1)S(1)} %collective-permute-done.1.zhi_ref) | copy-start | bytes 786436
  36.8 4.7 %collective-permute-start.2 = (bf16[192,512]{1,0:T(8,128)(2,1)S(1)}, bf16[192,512]{1,0:T(8,128)(2,1)S(1)}, u32[]{:S(2)}, u32[]{:S(2)}) collective-permute-start(bf16[192,512]{1,0:T(8,128)(2,1)S(1)} %get-tuple-element.49), channel_id=1, source_target_pairs={{0,16},{16,0},{32,48},{48,32},{64,80},{80,64},{96,112},{112,96},{1... | collective-permute-start | bytes 589832 | tf_op jit(solution)/shard_map/ppermute | solution.py:586
  39.3 7.3 %collective-permute-start.3 = (bf16[192,512]{1,0:T(8,128)(2,1)S(1)}, bf16[192,512]{1,0:T(8,128)(2,1)}, u32[]{:S(2)}, u32[]{:S(2)}) collective-permute-start(bf16[192,512]{1,0:T(8,128)(2,1)S(1)} %get-tuple-element.50), channel_id=1, source_target_pairs={{16,32},{48,64},{80,96},{32,16},{64,48},{96,80},{17,33},{49,65},{8... | collective-permute-start | bytes 589832 | tf_op jit(solution)/shard_map/ppermute | solution.py:587
  41.4 10.6 %copy-start.14 = (bf16[192,512]{1,0:T(8,128)(2,1)}, bf16[192,512]{1,0:T(8,128)(2,1)S(1)}, u32[]{:S(2)}) copy-start(bf16[192,512]{1,0:T(8,128)(2,1)S(1)} %collective-permute-done.2.inner_ref) | copy-start | bytes 589828
  47.6 9.7 %all-to-all-start.3 = ((bf16[8,64,128]{2,1,0:T(8,128)(2,1)}), bf16[8,64,128]{2,1,0:T(8,128)(2,1)S(1)}, u32[]{:S(2)}, u32[]{:S(2)}) async-start(bf16[8,64,128]{2,1,0:T(8,128)(2,1)} %shard_map.115), calls=%async_computation.3 | async-start | bytes 262144 | tf_op jit(solution)/shard_map/all_to_all | solution.py:558
  57.3 0.7 copy-start.15
  65.4 11.2 %all-to-all-start.4 = ((bf16[8,128,128]{2,1,0:T(8,128)(2,1)}), bf16[8,128,128]{2,1,0:T(8,128)(2,1)S(1)}, u32[]{:S(2)}, u32[]{:S(2)}) async-start(bf16[8,128,128]{2,1,0:T(8,128)(2,1)} %get-tuple-element.57), calls=%async_computation.4 | async-start | bytes 524288 | tf_op jit(solution)/shard_map/all_to_all | solution.py:558
  70.1 25.1 %collective-permute-start.4 = (bf16[8,32,512]{2,1,0:T(8,128)(2,1)}, bf16[8,32,512]{2,1,0:T(8,128)(2,1)S(1)}, u32[]{:S(2)}, u32[]{:S(2)}) collective-permute-start(bf16[8,32,512]{2,1,0:T(8,128)(2,1)} %get-tuple-element.62), channel_id=1, source_target_pairs={{0,1},{1,2},{2,3},{3,4},{4,5},{5,6},{6,7},{7,8},{8,9},{9,10},{10,1... | collective-permute-start | bytes 786440 | tf_op jit(solution)/shard_map/ppermute | solution.py:573
  72.3 22.9 %collective-permute-start.5 = (bf16[8,32,512]{2,1,0:T(8,128)(2,1)}, bf16[8,32,512]{2,1,0:T(8,128)(2,1)S(1)}, u32[]{:S(2)}, u32[]{:S(2)}) collective-permute-start(bf16[8,32,512]{2,1,0:T(8,128)(2,1)} %get-tuple-element.63), channel_id=1, source_target_pairs={{1,0},{2,1},{3,2},{4,3},{5,4},{6,5},{7,6},{8,7},{9,8},{10,9},{11,1... | collective-permute-start | bytes 786440 | tf_op jit(solution)/shard_map/ppermute | solution.py:574
  76.8 18.4 %copy-start.8 = (bf16[128,512]{1,0:T(8,128)(2,1)S(1)}, bf16[128,512]{1,0:T(8,128)(2,1)}, u32[]{:S(2)}) copy-start(bf16[128,512]{1,0:T(8,128)(2,1)} %get-tuple-element.65.own_first_ref) | copy-start | bytes 393220
  76.9 18.4 %copy-start.9 = (bf16[128,512]{1,0:T(8,128)(2,1)S(1)}, bf16[128,512]{1,0:T(8,128)(2,1)}, u32[]{:S(2)}) copy-start(bf16[128,512]{1,0:T(8,128)(2,1)} %get-tuple-element.66.own_last_ref) | copy-start | bytes 393220
  76.9 23.0 %copy-start.13 = (f32[128,128]{1,0:T(8,128)S(1)}, f32[128,128]{1,0:T(8,128)}, u32[]{:S(2)}) copy-start(f32[128,128]{1,0:T(8,128)} %copy-done.12) | copy-start | bytes 196612
  91.6 13.4 %all-to-all-start.6 = ((bf16[16,64,128]{2,1,0:T(8,128)(2,1)}), bf16[16,64,128]{2,1,0:T(8,128)(2,1)S(1)}, u32[]{:S(2)}, u32[]{:S(2)}) async-start(bf16[16,64,128]{2,1,0:T(8,128)(2,1)} %get-tuple-element.58), calls=%async_computation.6 | async-start | bytes 524288 | tf_op jit(solution)/shard_map/all_to_all | solution.py:558
  95.2 10.9 %copy-start.5 = (bf16[8,32,512]{2,1,0:T(8,128)(2,1)}, bf16[8,32,512]{2,1,0:T(8,128)(2,1)S(1)}, u32[]{:S(2)}) copy-start(bf16[8,32,512]{2,1,0:T(8,128)(2,1)S(1)} %collective-permute-done.4.zlo_ref) | copy-start | bytes 786436
  95.2 10.9 %copy-start.6 = (bf16[8,32,512]{2,1,0:T(8,128)(2,1)}, bf16[8,32,512]{2,1,0:T(8,128)(2,1)S(1)}, u32[]{:S(2)}) copy-start(bf16[8,32,512]{2,1,0:T(8,128)(2,1)S(1)} %collective-permute-done.5.zhi_ref) | copy-start | bytes 786436
  95.3 6.3 %collective-permute-start.6 = (bf16[192,512]{1,0:T(8,128)(2,1)S(1)}, bf16[192,512]{1,0:T(8,128)(2,1)S(1)}, u32[]{:S(2)}, u32[]{:S(2)}) collective-permute-start(bf16[192,512]{1,0:T(8,128)(2,1)S(1)} %get-tuple-element.67), channel_id=1, source_target_pairs={{0,16},{16,0},{32,48},{48,32},{64,80},{80,64},{96,112},{112,96},{1... | collective-permute-start | bytes 589832 | tf_op jit(solution)/shard_map/ppermute | solution.py:586
  97.8 7.3 %collective-permute-start.7 = (bf16[192,512]{1,0:T(8,128)(2,1)S(1)}, bf16[192,512]{1,0:T(8,128)(2,1)S(1)}, u32[]{:S(2)}, u32[]{:S(2)}) collective-permute-start(bf16[192,512]{1,0:T(8,128)(2,1)S(1)} %get-tuple-element.68), channel_id=1, source_target_pairs={{16,32},{48,64},{80,96},{32,16},{64,48},{96,80},{17,33},{49,65},{8... | collective-permute-start | bytes 589832 | tf_op jit(solution)/shard_map/ppermute | solution.py:587
  101.6 9.1 %copy-start.16 = (bf16[192,512]{1,0:T(8,128)(2,1)}, bf16[192,512]{1,0:T(8,128)(2,1)S(1)}, u32[]{:S(2)}) copy-start(bf16[192,512]{1,0:T(8,128)(2,1)S(1)} %collective-permute-done.6.inner_ref) | copy-start | bytes 589828
  105.1 5.6 %copy-start.17 = (bf16[192,512]{1,0:T(8,128)(2,1)}, bf16[192,512]{1,0:T(8,128)(2,1)S(1)}, u32[]{:S(2)}) copy-start(bf16[192,512]{1,0:T(8,128)(2,1)S(1)} %collective-permute-done.7.outer_ref) | copy-start | bytes 589828
  106.1 11.2 %copy-start.7 = (bf16[192,512]{1,0:T(8,128)(2,1)S(1)}, bf16[192,512]{1,0:T(8,128)(2,1)}, u32[]{:S(2)}) copy-start(bf16[192,512]{1,0:T(8,128)(2,1)} %constant.7.clone.txi_hbm) | copy-start | bytes 589828
  106.1 11.1 %all-to-all-start.7 = ((bf16[8,128,128]{2,1,0:T(8,128)(2,1)}), bf16[8,128,128]{2,1,0:T(8,128)(2,1)S(1)}, u32[]{:S(2)}, u32[]{:S(2)}) async-start(bf16[8,128,128]{2,1,0:T(8,128)(2,1)} %shard_map.122), calls=%async_computation.7 | async-start | bytes 524288 | tf_op jit(solution)/shard_map/all_to_all | solution.py:558
  117.2 1.2 %copy-start.1 = (bf16[8,128,512]{2,1,0:T(8,128)(2,1)S(1)}, bf16[8,128,512]{2,1,0:T(8,128)(2,1)}, u32[]{:S(2)}) copy-start(bf16[8,128,512]{2,1,0:T(8,128)(2,1)} %shard_map.123.conv_ref) | copy-start | bytes 3145732

commit v5 on v4

--- a/solution.py
+++ b/solution.py
@@ -582,10 +582,9 @@
 def y_halos(inner, outer):
     ahead = [(i, i + 1) for i in range(1, GY - 1, 2)]
     behind = [(i, i - 1) for i in range(2, GY, 2)]
-    return (
-        lax.ppermute(inner, "gy", [(i, i ^ 1) for i in range(GY)]),
-        lax.ppermute(outer, "gy", ahead + behind),
-    )
+    outer = lax.ppermute(outer, "gy", ahead + behind)
+    inner = lax.ppermute(inner, "gy", [(i, i ^ 1) for i in range(GY)])
+    return inner, outer
 
 
 def conv(flip, own, halo, kernel, bias):
@@ -644,7 +643,8 @@
     )
     halo = (zlo, zhi, *y_halos(*y_edges(after(first, send), last, zlo, zhi)))
     recv = exchange(send, "gz")
-    recv, *halo = lax.optimization_barrier((recv, *halo))
+    recv, inner = lax.optimization_barrier((recv, halo[2]))
+    halo = (zlo, zhi, inner, halo[3])
     (send,) = call(spread_kernel, [AUTO] * 2, [lines_out(LINE_ROWS)], [], SMALL, recv, table)
     local = conv(False, after(own, send), halo, kernel_weight, bias)
     recv = exchange(send, "gy")

time: 122 us -> 121 us (level)
  starting transfers between devices: 44 us -> 48.3 us
  waiting for transfers between devices: 15 us -> 10.9 us
  blocking collectives: 26.3 us -> 23.6 us
    ppermute x4, waiting for transfers between devices: 8.6 us -> 2.46 us  [the longest x2 2.45 us: y_halos(): outer = lax.ppermute(outer, 'gy', ahead + behind)]
    all_to_all x6, starting transfers between devices: 26.6 us -> 30.1 us  [exchange(): return lax.all_to_all(blocks, axis, 0, 0, tiled=True)]
    all_to_all x2, blocking collectives: 26.3 us -> 23.6 us  [exchange(): return lax.all_to_all(blocks, axis, 0, 0, tiled=True)]
    all_to_all x6, waiting for transfers between devices: 6.4 us -> 8.43 us  [exchange(): return lax.all_to_all(blocks, axis, 0, 0, tiled=True)]
  transfers between devices with their start and end apart: 14 -> 14, of which waited for: 6 -> 6; matrix products, arithmetic and copies ran while one was open for 0% -> 0% of each run, Pallas kernels for 14% -> 16%
where the time goes in v5:
time: 121 us; the launch traced here: 119 us
  starting transfers between devices  48.3 us (40%)
  Pallas kernels  33 us (27%)
  blocking collectives  23.6 us (20%)
  waiting for transfers between devices  10.9 us (9%)
  local copies, waits for them, and re-layouts  2.58 us (2%)
    pallas_call x14, Pallas kernels, call(): pl.pallas_call(body, in_specs=ins, out_specs=[spec for spec, _ in outs],...  33 us
    all_to_all x6, starting transfers between devices, exchange(): return lax.all_to_all(blocks, axis, 0, 0, tiled=True)  30.1 us
    all_to_all x2, blocking collectives, exchange(): return lax.all_to_all(blocks, axis, 0, 0, tiled=True)  23.6 us
    all_to_all x6, waiting for transfers between devices, exchange(): return lax.all_to_all(blocks, axis, 0, 0, tiled=True)  8.43 us
    ppermute x2, starting transfers between devices, z_halos(): zlo = lax.ppermute(back, 'gz', [(i, i + 1) for i in range(GZ - 1)])  5.4 us
    ppermute x2, starting transfers between devices, y_halos(): outer = lax.ppermute(outer, 'gy', ahead + behind)  5.15 us
    ppermute x2, starting transfers between devices, y_halos(): inner = lax.ppermute(inner, 'gy', [(i, i ^ 1) for i in range(GY)])  4.95 us
    ppermute x2, starting transfers between devices, z_halos(): zhi = lax.ppermute(front, 'gz', [(i + 1, i) for i in range(GZ - 1)])  2.72 us
  transfers between devices with their start and end apart: 14, of which 6 were waited for; matrix products, arithmetic and copies ran while one was open for 0% of the time, Pallas kernels for 16%

profile of v5, /device:TPU:1, one launch (start us, length us, event | category | flops | bytes accessed | tf_op | source)
XLA Modules:
  0.0 119.5 jit_solution(10284225342958562116)
XLA Ops:
  0.6 0.0 copy-start
  0.6 0.0 copy-start.2
  0.7 3.1 %shard_map.111 = (bf16[8,128,128]{2,1,0:T(8,128)(2,1)}, bf16[8,32,512]{2,1,0:T(8,128)(2,1)}, bf16[8,32,512]{2,1,0:T(8,128)(2,1)}, bf16[128,512]{1,0:T(8,128)(2,1)}, bf16[128,512]{1,0:T(8,128)(2,1)}) custom-call(bf16[8,128,512]{2,1,0:T(8,128)(2,1)} %bitcast.9, bf16[64,512]{1,0:T(8,128)(2,1)} %constant.6.clone.tx_hbm), custom_call_target="tpu_custom_call" | custom-call | tf_op jit(solution)/shard_map/pallas_call | solution.py:547
  3.7 5.8 %all-to-all-start = ((bf16[8,128,128]{2,1,0:T(8,128)(2,1)}), bf16[8,128,128]{2,1,0:T(8,128)(2,1)S(1)}, u32[]{:S(2)}, u32[]{:S(2)}) async-start(bf16[8,128,128]{2,1,0:T(8,128)(2,1)} %get-tuple-element.39), calls=%async_computation | async-start | bytes 524288 | tf_op jit(solution)/shard_map/all_to_all | solution.py:558
  9.5 3.2 %collective-permute-start = (bf16[8,32,512]{2,1,0:T(8,128)(2,1)}, bf16[8,32,512]{2,1,0:T(8,128)(2,1)S(1)}, u32[]{:S(2)}, u32[]{:S(2)}) collective-permute-start(bf16[8,32,512]{2,1,0:T(8,128)(2,1)} %get-tuple-element.44), channel_id=1, source_target_pairs={{0,1},{1,2},{2,3},{3,4},{4,5},{5,6},{6,7},{7,8},{8,9},{9,10},{10,1... | collective-permute-start | bytes 786440 | tf_op jit(solution)/shard_map/ppermute | solution.py:573
  12.7 0.0 copy-start.10
  12.8 0.0 copy-start.11
  12.8 1.4 %collective-permute-start.1 = (bf16[8,32,512]{2,1,0:T(8,128)(2,1)}, bf16[8,32,512]{2,1,0:T(8,128)(2,1)S(1)}, u32[]{:S(2)}, u32[]{:S(2)}) collective-permute-start(bf16[8,32,512]{2,1,0:T(8,128)(2,1)} %get-tuple-element.45), channel_id=1, source_target_pairs={{1,0},{2,1},{3,2},{4,3},{5,4},{6,5},{7,6},{8,7},{9,8},{10,9},{11,1... | collective-permute-start | bytes 786440 | tf_op jit(solution)/shard_map/ppermute | solution.py:574
  14.2 1.8 %all-to-all-done.recv_ref = bf16[8,128,128]{2,1,0:T(8,128)(2,1)S(1)} async-done(((bf16[8,128,128]{2,1,0:T(8,128)(2,1)}), bf16[8,128,128]{2,1,0:T(8,128)(2,1)S(1)}, u32[]{:S(2)}, u32[]{:S(2)}) %all-to-all-start) | async-done | bytes 262176 | tf_op jit(solution)/shard_map/all_to_all | solution.py:558
  16.0 0.0 copy-done
  16.0 0.3 shard_map.112
  16.3 14.1 %all_to_all.40.recv_ref = bf16[16,16,128]{2,1,0:T(8,128)(2,1)S(1)} all-to-all(bf16[16,16,128]{2,1,0:T(8,128)(2,1)S(1)} %shard_map.112), channel_id=1, replica_groups=mesh['gy'=8,'gz'=16] {'gz'}, dimensions={0} | all-to-all | bytes 131072 | tf_op jit(solution)/shard_map/all_to_all | solution.py:558
  30.4 0.0 copy-done.2
  30.4 2.1 %shard_map.113 = (bf16[16,64,128]{2,1,0:T(8,128)(2,1)}, f32[128,128]{1,0:T(8,128)S(1)}) custom-call(bf16[16,16,128]{2,1,0:T(8,128)(2,1)S(1)} %all_to_all.40.recv_ref, bf16[64,8192]{1,0:T(8,128)(2,1)S(1)} %bitcast.7, bf16[1408,512]{1,0:T(8,128)(2,1)S(1)} %copy-done), custom_call_target="tpu_custom_call" | custom-call | tf_op jit(solution)/shard_map/pallas_call | solution.py:547
  32.5 0.6 copy-done.12
  33.1 3.5 %all-to-all-start.2 = ((bf16[16,64,128]{2,1,0:T(8,128)(2,1)}), bf16[16,64,128]{2,1,0:T(8,128)(2,1)S(1)}, u32[]{:S(2)}, u32[]{:S(2)}) async-start(bf16[16,64,128]{2,1,0:T(8,128)(2,1)} %get-tuple-element.40), calls=%async_computation.2 | async-start | bytes 524288 | tf_op jit(solution)/shard_map/all_to_all | solution.py:558
  36.7 0.0 collective-permute-done.zlo_ref
  36.7 0.0 copy-start.3
  36.7 0.0 collective-permute-done.1.zhi_ref
  36.7 0.0 copy-start.4
  36.7 0.0 copy-done.10
  36.7 0.0 copy-done.11
  36.7 0.8 shard_map.114
  37.5 2.5 %collective-permute-start.2 = (bf16[192,512]{1,0:T(8,128)(2,1)S(1)}, bf16[192,512]{1,0:T(8,128)(2,1)S(1)}, u32[]{:S(2)}, u32[]{:S(2)}) collective-permute-start(bf16[192,512]{1,0:T(8,128)(2,1)S(1)} %get-tuple-element.46), channel_id=1, source_target_pairs={{0,16},{16,0},{32,48},{48,32},{64,80},{80,64},{96,112},{112,96},{1... | collective-permute-start | bytes 589832 | tf_op jit(solution)/shard_map/ppermute | solution.py:586
  40.0 2.1 %collective-permute-start.3 = (bf16[192,512]{1,0:T(8,128)(2,1)}, bf16[192,512]{1,0:T(8,128)(2,1)}, u32[]{:S(2)}, u32[]{:S(2)}) collective-permute-start(bf16[192,512]{1,0:T(8,128)(2,1)} %get-tuple-element.50), channel_id=1, source_target_pairs={{16,32},{48,64},{80,96},{32,16},{64,48},{96,80},{17,33},{49,65},{8... | collective-permute-start | bytes 589832 | tf_op jit(solution)/shard_map/ppermute | solution.py:585
  42.1 0.0 collective-permute-done.2.inner_ref
  42.1 0.0 copy-start.14
  42.1 2.1 %all-to-all-done.2.recv_ref = bf16[16,64,128]{2,1,0:T(8,128)(2,1)S(1)} async-done(((bf16[16,64,128]{2,1,0:T(8,128)(2,1)}), bf16[16,64,128]{2,1,0:T(8,128)(2,1)S(1)}, u32[]{:S(2)}, u32[]{:S(2)}) %all-to-all-start.2) | async-done | bytes 262176 | tf_op jit(solution)/shard_map/all_to_all | solution.py:558
  44.2 1.0 shard_map.115
  45.1 6.9 %all-to-all-start.3 = ((bf16[8,64,128]{2,1,0:T(8,128)(2,1)}), bf16[8,64,128]{2,1,0:T(8,128)(2,1)S(1)}, u32[]{:S(2)}, u32[]{:S(2)}) async-start(bf16[8,64,128]{2,1,0:T(8,128)(2,1)} %shard_map.115), calls=%async_computation.3 | async-start | bytes 262144 | tf_op jit(solution)/shard_map/all_to_all | solution.py:558
  52.0 0.0 collective-permute-done.3.outer_ref
  52.0 0.0 copy-done.3
  52.0 0.0 copy-done.4
  52.0 0.0 copy-done.14
  52.0 5.1 %shard_map.116.local_ref = bf16[8,128,512]{2,1,0:T(8,128)(2,1)} custom-call(bf16[8,128,512]{2,1,0:T(8,128)(2,1)} %bitcast.10, bf16[8,32,512]{2,1,0:T(8,128)(2,1)} %copy-done.3, bf16[8,32,512]{2,1,0:T(8,128)(2,1)} %copy-done.4, bf16[192,512]{1,0:T(8,128)(2,1)} %copy-done.14, bf16[192,512]{1,0:T(8,128)(2,1)} %collective-permute-done.3.outer_ref, ...), custom_call_target="tpu_custom_call" | custom-call | tf_op jit(solution)/shard_map/pallas_call | solution.py:547
  57.2 0.2 all-to-all-done.3.recv_ref
  57.3 0.7 copy-done.15
  58.0 7.4 %shard_map.117 = (bf16[8,128,512]{2,1,0:T(8,128)(2,1)}, bf16[8,32,512]{2,1,0:T(8,128)(2,1)}, bf16[8,32,512]{2,1,0:T(8,128)(2,1)}, bf16[128,512]{1,0:T(8,128)(2,1...) custom-call(bf16[8,64,128]{2,1,0:T(8,128)(2,1)} %copy-done.15, bf16[8,128,512]{2,1,0:T(8,128)(2,1)} %shard_map.116.local_ref, ...), custom_call_target="tpu_custom_call" | custom-call | tf_op jit(solution)/shard_map/pallas_call | solution.py:547
  65.4 4.7 %all-to-all-start.4 = ((bf16[8,128,128]{2,1,0:T(8,128)(2,1)}), bf16[8,128,128]{2,1,0:T(8,128)(2,1)S(1)}, u32[]{:S(2)}, u32[]{:S(2)}) async-start(bf16[8,128,128]{2,1,0:T(8,128)(2,1)} %get-tuple-element.51), calls=%async_computation.4 | async-start | bytes 524288 | tf_op jit(solution)/shard_map/all_to_all | solution.py:558
  70.1 2.2 %collective-permute-start.4 = (bf16[8,32,512]{2,1,0:T(8,128)(2,1)}, bf16[8,32,512]{2,1,0:T(8,128)(2,1)S(1)}, u32[]{:S(2)}, u32[]{:S(2)}) collective-permute-start(bf16[8,32,512]{2,1,0:T(8,128)(2,1)} %get-tuple-element.56), channel_id=1, source_target_pairs={{0,1},{1,2},{2,3},{3,4},{4,5},{5,6},{6,7},{7,8},{8,9},{9,10},{10,1... | collective-permute-start | bytes 786440 | tf_op jit(solution)/shard_map/ppermute | solution.py:573
  72.3 1.3 %collective-permute-start.5 = (bf16[8,32,512]{2,1,0:T(8,128)(2,1)}, bf16[8,32,512]{2,1,0:T(8,128)(2,1)S(1)}, u32[]{:S(2)}, u32[]{:S(2)}) collective-permute-start(bf16[8,32,512]{2,1,0:T(8,128)(2,1)} %get-tuple-element.57), channel_id=1, source_target_pairs={{1,0},{2,1},{3,2},{4,3},{5,4},{6,5},{7,6},{8,7},{9,8},{10,9},{11,1... | collective-permute-start | bytes 786440 | tf_op jit(solution)/shard_map/ppermute | solution.py:574
  73.6 3.0 %all-to-all-done.4.recv_ref = bf16[8,128,128]{2,1,0:T(8,128)(2,1)S(1)} async-done(((bf16[8,128,128]{2,1,0:T(8,128)(2,1)}), bf16[8,128,128]{2,1,0:T(8,128)(2,1)S(1)}, u32[]{:S(2)}, u32[]{:S(2)}) %all-to-all-start.4) | async-done | bytes 262176 | tf_op jit(solution)/shard_map/all_to_all | solution.py:558
  76.6 0.3 shard_map.118
  76.9 0.0 copy-start.8
  76.9 0.0 copy-start.9
  76.9 9.5 %all_to_all.41.recv_ref = bf16[16,24,128]{2,1,0:T(8,128)(2,1)S(1)} all-to-all(bf16[16,24,128]{2,1,0:T(8,128)(2,1)S(1)} %shard_map.118), channel_id=1, replica_groups=mesh['gy'=8,'gz'=16] {'gz'}, dimensions={0} | all-to-all | bytes 196608 | tf_op jit(solution)/shard_map/all_to_all | solution.py:558
  86.4 2.5 %shard_map.119 = (bf16[16,64,128]{2,1,0:T(8,128)(2,1)}, f32[128,128]{1,0:T(8,128)S(1)}) custom-call(bf16[16,24,128]{2,1,0:T(8,128)(2,1)S(1)} %all_to_all.41.recv_ref, bf16[64,8192]{1,0:T(8,128)(2,1)S(1)} %bitcast.8, bf16[1408,512]{1,0:T(8,128)(2,1)S(1)} %copy-done), custom_call_target="tpu_custom_call" | custom-call | tf_op jit(solution)/shard_map/pallas_call | solution.py:547
  88.9 3.5 %all-to-all-start.6 = ((bf16[16,64,128]{2,1,0:T(8,128)(2,1)}), bf16[16,64,128]{2,1,0:T(8,128)(2,1)S(1)}, u32[]{:S(2)}, u32[]{:S(2)}) async-start(bf16[16,64,128]{2,1,0:T(8,128)(2,1)} %get-tuple-element.52), calls=%async_computation.6 | async-start | bytes 524288 | tf_op jit(solution)/shard_map/all_to_all | solution.py:558
  92.4 0.0 collective-permute-done.4.zlo_ref
  92.4 0.0 collective-permute-done.5.zhi_ref
  92.5 0.1 shard_map.121
  92.5 2.5 %collective-permute-start.6 = (bf16[192,512]{1,0:T(8,128)(2,1)S(1)}, bf16[192,512]{1,0:T(8,128)(2,1)S(1)}, u32[]{:S(2)}, u32[]{:S(2)}) collective-permute-start(bf16[192,512]{1,0:T(8,128)(2,1)S(1)} %get-tuple-element.61), channel_id=1, source_target_pairs={{0,16},{16,0},{32,48},{48,32},{64,80},{80,64},{96,112},{112,96},{1... | collective-permute-start | bytes 589832 | tf_op jit(solution)/shard_map/ppermute | solution.py:586
  95.0 3.1 %collective-permute-start.7 = (bf16[192,512]{1,0:T(8,128)(2,1)S(1)}, bf16[192,512]{1,0:T(8,128)(2,1)S(1)}, u32[]{:S(2)}, u32[]{:S(2)}) collective-permute-start(bf16[192,512]{1,0:T(8,128)(2,1)S(1)} %get-tuple-element.62), channel_id=1, source_target_pairs={{16,32},{48,64},{80,96},{32,16},{64,48},{96,80},{17,33},{49,65},{8... | collective-permute-start | bytes 589832 | tf_op jit(solution)/shard_map/ppermute | solution.py:585
  98.1 0.0 copy-done.13
  98.1 1.7 %shard_map.120 = f32[64,8192]{1,0:T(8,128)} custom-call(f32[128,128]{1,0:T(8,128)S(1)} %copy-done.13, f32[128,128]{1,0:T(8,128)S(1)} %get-tuple-element.55.back_ref), custom_call_target="tpu_custom_call" | custom-call | tf_op jit(solution)/shard_map/pallas_call | solution.py:547
  99.8 0.0 collective-permute-done.6.inner_ref
  99.8 2.5 %collective-permute-done.7.outer_ref = bf16[192,512]{1,0:T(8,128)(2,1)S(1)} collective-permute-done((bf16[192,512]{1,0:T(8,128)(2,1)S(1)}, bf16[192,512]{1,0:T(8,128)(2,1)S(1)}, u32[]{:S(2)}, u32[]{:S(2)}) %collective-permute-start.7) | collective-permute-done | bytes 196640 | tf_op jit(solution)/shard_map/ppermute | solution.py:585
  102.3 0.0 all-to-all-done.6.recv_ref
  102.3 1.0 shard_map.122
  103.3 5.6 %all-to-all-start.7 = ((bf16[8,128,128]{2,1,0:T(8,128)(2,1)}), bf16[8,128,128]{2,1,0:T(8,128)(2,1)S(1)}, u32[]{:S(2)}, u32[]{:S(2)}) async-start(bf16[8,128,128]{2,1,0:T(8,128)(2,1)} %shard_map.122), calls=%async_computation.7 | async-start | bytes 524288 | tf_op jit(solution)/shard_map/all_to_all | solution.py:558
  108.9 5.1 %shard_map.123.conv_ref = bf16[8,128,512]{2,1,0:T(8,128)(2,1)} custom-call(bf16[8,128,512]{2,1,0:T(8,128)(2,1)} %get-tuple-element.65.own_ref, bf16[8,32,512]{2,1,0:T(8,128)(2,1)} %copy-done.5, bf16[8,32,512]{2,1,0:T(8,128)(2,1)} %copy-done.6, bf16[192,512]{1,0:T(8,128)(2,1)} %copy-done.16, bf16[192,512]{1,0:T(8,128)(2,1)} %copy-done.17, ...), custom_call_target="tpu_custom_call" | custom-call | tf_op jit(solution)/shard_map/pallas_call | solution.py:547
  114.1 1.4 %all-to-all-done.7.recv_ref = bf16[8,128,128]{2,1,0:T(8,128)(2,1)S(1)} async-done(((bf16[8,128,128]{2,1,0:T(8,128)(2,1)}), bf16[8,128,128]{2,1,0:T(8,128)(2,1)S(1)}, u32[]{:S(2)}, u32[]{:S(2)}) %all-to-all-start.7) | async-done | bytes 262176 | tf_op jit(solution)/shard_map/all_to_all | solution.py:558
  115.4 1.2 %copy-done.1 = bf16[8,128,512]{2,1,0:T(8,128)(2,1)S(1)} copy-done((bf16[8,128,512]{2,1,0:T(8,128)(2,1)S(1)}, bf16[8,128,512]{2,1,0:T(8,128)(2,1)}, u32[]{:S(2)}) %copy-start.1) | copy-done | bytes 1048600
  116.7 2.7 %shard_map.124 = (bf16[8,128,512]{2,1,0:T(8,128)(2,1)}, f32[3,3,32,96]{3,2,1,0:T(8,128)}, f32[1,32]{1,0:T(1,128)}) custom-call(bf16[8,128,128]{2,1,0:T(8,128)(2,1)S(1)} %all-to-all-done.7.recv_ref, bf16[8,128,512]{2,1,0:T(8,128)(2,1)S(1)} %copy-done.1, bf16[192,512]{1,0:T(8,128)(2,1)S(1)} %copy-done.7), custom_call_target="tpu_custom_call" | custom-call | tf_op jit(solution)/shard_map/pallas_call | solution.py:547
  (16 shorter events, 0.0 us)
Async XLA Ops:
  0.6 15.4 %copy-start = (bf16[1408,512]{1,0:T(8,128)(2,1)S(1)}, bf16[1408,512]{1,0:T(8,128)(2,1)}, u32[]{:S(2)}) copy-start(bf16[1408,512]{1,0:T(8,128)(2,1)} %constant.8.clone.table_ref) | copy-start | bytes 4325380
  0.6 29.8 %copy-start.2 = (bf16[2,32,8192]{2,1,0:T(8,128)(2,1)S(1)}, bf16[2,32,8192]{2,1,0:T(8,128)(2,1)}, u32[]{:S(2)}) copy-start(bf16[2,32,8192]{2,1,0:T(8,128)(2,1)} %param.10) | copy-start | bytes 3145732
  3.7 12.3 %all-to-all-start = ((bf16[8,128,128]{2,1,0:T(8,128)(2,1)}), bf16[8,128,128]{2,1,0:T(8,128)(2,1)S(1)}, u32[]{:S(2)}, u32[]{:S(2)}) async-start(bf16[8,128,128]{2,1,0:T(8,128)(2,1)} %get-tuple-element.39), calls=%async_computation | async-start | bytes 524288 | tf_op jit(solution)/shard_map/all_to_all | solution.py:558
  9.5 27.1 %collective-permute-start = (bf16[8,32,512]{2,1,0:T(8,128)(2,1)}, bf16[8,32,512]{2,1,0:T(8,128)(2,1)S(1)}, u32[]{:S(2)}, u32[]{:S(2)}) collective-permute-start(bf16[8,32,512]{2,1,0:T(8,128)(2,1)} %get-tuple-element.44), channel_id=1, source_target_pairs={{0,1},{1,2},{2,3},{3,4},{4,5},{5,6},{6,7},{7,8},{8,9},{9,10},{10,1... | collective-permute-start | bytes 786440 | tf_op jit(solution)/shard_map/ppermute | solution.py:573
  12.7 24.0 %copy-start.10 = (bf16[128,512]{1,0:T(8,128)(2,1)S(1)}, bf16[128,512]{1,0:T(8,128)(2,1)}, u32[]{:S(2)}) copy-start(bf16[128,512]{1,0:T(8,128)(2,1)} %get-tuple-element.42.own_first_ref) | copy-start | bytes 393220
  12.8 24.0 %copy-start.11 = (bf16[128,512]{1,0:T(8,128)(2,1)S(1)}, bf16[128,512]{1,0:T(8,128)(2,1)}, u32[]{:S(2)}) copy-start(bf16[128,512]{1,0:T(8,128)(2,1)} %get-tuple-element.43.own_last_ref) | copy-start | bytes 393220
  12.8 23.9 %collective-permute-start.1 = (bf16[8,32,512]{2,1,0:T(8,128)(2,1)}, bf16[8,32,512]{2,1,0:T(8,128)(2,1)S(1)}, u32[]{:S(2)}, u32[]{:S(2)}) collective-permute-start(bf16[8,32,512]{2,1,0:T(8,128)(2,1)} %get-tuple-element.45), channel_id=1, source_target_pairs={{1,0},{2,1},{3,2},{4,3},{5,4},{6,5},{7,6},{8,7},{9,8},{10,9},{11,1... | collective-permute-start | bytes 786440 | tf_op jit(solution)/shard_map/ppermute | solution.py:574
  32.5 0.6 copy-start.12
  33.1 11.0 %all-to-all-start.2 = ((bf16[16,64,128]{2,1,0:T(8,128)(2,1)}), bf16[16,64,128]{2,1,0:T(8,128)(2,1)S(1)}, u32[]{:S(2)}, u32[]{:S(2)}) async-start(bf16[16,64,128]{2,1,0:T(8,128)(2,1)} %get-tuple-element.40), calls=%async_computation.2 | async-start | bytes 524288 | tf_op jit(solution)/shard_map/all_to_all | solution.py:558
  36.7 15.3 %copy-start.3 = (bf16[8,32,512]{2,1,0:T(8,128)(2,1)}, bf16[8,32,512]{2,1,0:T(8,128)(2,1)S(1)}, u32[]{:S(2)}) copy-start(bf16[8,32,512]{2,1,0:T(8,128)(2,1)S(1)} %collective-permute-done.zlo_ref) | copy-start | bytes 786436
  36.7 15.3 %copy-start.4 = (bf16[8,32,512]{2,1,0:T(8,128)(2,1)}, bf16[8,32,512]{2,1,0:T(8,128)(2,1)S(1)}, u32[]{:S(2)}) copy-start(bf16[8,32,512]{2,1,0:T(8,128)(2,1)S(1)} %collective-permute-done.1.zhi_ref) | copy-start | bytes 786436
  37.5 4.5 %collective-permute-start.2 = (bf16[192,512]{1,0:T(8,128)(2,1)S(1)}, bf16[192,512]{1,0:T(8,128)(2,1)S(1)}, u32[]{:S(2)}, u32[]{:S(2)}) collective-permute-start(bf16[192,512]{1,0:T(8,128)(2,1)S(1)} %get-tuple-element.46), channel_id=1, source_target_pairs={{0,16},{16,0},{32,48},{48,32},{64,80},{80,64},{96,112},{112,96},{1... | collective-permute-start | bytes 589832 | tf_op jit(solution)/shard_map/ppermute | solution.py:586
  40.0 12.0 %collective-permute-start.3 = (bf16[192,512]{1,0:T(8,128)(2,1)}, bf16[192,512]{1,0:T(8,128)(2,1)}, u32[]{:S(2)}, u32[]{:S(2)}) collective-permute-start(bf16[192,512]{1,0:T(8,128)(2,1)} %get-tuple-element.50), channel_id=1, source_target_pairs={{16,32},{48,64},{80,96},{32,16},{64,48},{96,80},{17,33},{49,65},{8... | collective-permute-start | bytes 589832 | tf_op jit(solution)/shard_map/ppermute | solution.py:585
  42.1 9.9 %copy-start.14 = (bf16[192,512]{1,0:T(8,128)(2,1)}, bf16[192,512]{1,0:T(8,128)(2,1)S(1)}, u32[]{:S(2)}) copy-start(bf16[192,512]{1,0:T(8,128)(2,1)S(1)} %collective-permute-done.2.inner_ref) | copy-start | bytes 589828
  45.1 12.2 %all-to-all-start.3 = ((bf16[8,64,128]{2,1,0:T(8,128)(2,1)}), bf16[8,64,128]{2,1,0:T(8,128)(2,1)S(1)}, u32[]{:S(2)}, u32[]{:S(2)}) async-start(bf16[8,64,128]{2,1,0:T(8,128)(2,1)} %shard_map.115), calls=%async_computation.3 | async-start | bytes 262144 | tf_op jit(solution)/shard_map/all_to_all | solution.py:558
  57.3 0.7 copy-start.15
  65.4 11.2 %all-to-all-start.4 = ((bf16[8,128,128]{2,1,0:T(8,128)(2,1)}), bf16[8,128,128]{2,1,0:T(8,128)(2,1)S(1)}, u32[]{:S(2)}, u32[]{:S(2)}) async-start(bf16[8,128,128]{2,1,0:T(8,128)(2,1)} %get-tuple-element.51), calls=%async_computation.4 | async-start | bytes 524288 | tf_op jit(solution)/shard_map/all_to_all | solution.py:558
  70.1 22.4 %collective-permute-start.4 = (bf16[8,32,512]{2,1,0:T(8,128)(2,1)}, bf16[8,32,512]{2,1,0:T(8,128)(2,1)S(1)}, u32[]{:S(2)}, u32[]{:S(2)}) collective-permute-start(bf16[8,32,512]{2,1,0:T(8,128)(2,1)} %get-tuple-element.56), channel_id=1, source_target_pairs={{0,1},{1,2},{2,3},{3,4},{4,5},{5,6},{6,7},{7,8},{8,9},{9,10},{10,1... | collective-permute-start | bytes 786440 | tf_op jit(solution)/shard_map/ppermute | solution.py:573
  72.3 20.2 %collective-permute-start.5 = (bf16[8,32,512]{2,1,0:T(8,128)(2,1)}, bf16[8,32,512]{2,1,0:T(8,128)(2,1)S(1)}, u32[]{:S(2)}, u32[]{:S(2)}) collective-permute-start(bf16[8,32,512]{2,1,0:T(8,128)(2,1)} %get-tuple-element.57), channel_id=1, source_target_pairs={{1,0},{2,1},{3,2},{4,3},{5,4},{6,5},{7,6},{8,7},{9,8},{10,9},{11,1... | collective-permute-start | bytes 786440 | tf_op jit(solution)/shard_map/ppermute | solution.py:574
  76.9 15.6 %copy-start.8 = (bf16[128,512]{1,0:T(8,128)(2,1)S(1)}, bf16[128,512]{1,0:T(8,128)(2,1)}, u32[]{:S(2)}) copy-start(bf16[128,512]{1,0:T(8,128)(2,1)} %get-tuple-element.59.own_first_ref) | copy-start | bytes 393220
  76.9 15.6 %copy-start.9 = (bf16[128,512]{1,0:T(8,128)(2,1)S(1)}, bf16[128,512]{1,0:T(8,128)(2,1)}, u32[]{:S(2)}) copy-start(bf16[128,512]{1,0:T(8,128)(2,1)} %get-tuple-element.60.own_last_ref) | copy-start | bytes 393220
  76.9 21.2 %copy-start.13 = (f32[128,128]{1,0:T(8,128)S(1)}, f32[128,128]{1,0:T(8,128)}, u32[]{:S(2)}) copy-start(f32[128,128]{1,0:T(8,128)} %copy-done.12) | copy-start | bytes 196612
  88.9 13.4 %all-to-all-start.6 = ((bf16[16,64,128]{2,1,0:T(8,128)(2,1)}), bf16[16,64,128]{2,1,0:T(8,128)(2,1)S(1)}, u32[]{:S(2)}, u32[]{:S(2)}) async-start(bf16[16,64,128]{2,1,0:T(8,128)(2,1)} %get-tuple-element.52), calls=%async_computation.6 | async-start | bytes 524288 | tf_op jit(solution)/shard_map/all_to_all | solution.py:558
  92.4 10.9 %copy-start.5 = (bf16[8,32,512]{2,1,0:T(8,128)(2,1)}, bf16[8,32,512]{2,1,0:T(8,128)(2,1)S(1)}, u32[]{:S(2)}) copy-start(bf16[8,32,512]{2,1,0:T(8,128)(2,1)S(1)} %collective-permute-done.4.zlo_ref) | copy-start | bytes 786436
  92.5 10.8 %copy-start.6 = (bf16[8,32,512]{2,1,0:T(8,128)(2,1)}, bf16[8,32,512]{2,1,0:T(8,128)(2,1)S(1)}, u32[]{:S(2)}) copy-start(bf16[8,32,512]{2,1,0:T(8,128)(2,1)S(1)} %collective-permute-done.5.zhi_ref) | copy-start | bytes 786436
  92.5 7.3 %collective-permute-start.6 = (bf16[192,512]{1,0:T(8,128)(2,1)S(1)}, bf16[192,512]{1,0:T(8,128)(2,1)S(1)}, u32[]{:S(2)}, u32[]{:S(2)}) collective-permute-start(bf16[192,512]{1,0:T(8,128)(2,1)S(1)} %get-tuple-element.61), channel_id=1, source_target_pairs={{0,16},{16,0},{32,48},{48,32},{64,80},{80,64},{96,112},{112,96},{1... | collective-permute-start | bytes 589832 | tf_op jit(solution)/shard_map/ppermute | solution.py:586
  95.0 7.3 %collective-permute-start.7 = (bf16[192,512]{1,0:T(8,128)(2,1)S(1)}, bf16[192,512]{1,0:T(8,128)(2,1)S(1)}, u32[]{:S(2)}, u32[]{:S(2)}) collective-permute-start(bf16[192,512]{1,0:T(8,128)(2,1)S(1)} %get-tuple-element.62), channel_id=1, source_target_pairs={{16,32},{48,64},{80,96},{32,16},{64,48},{96,80},{17,33},{49,65},{8... | collective-permute-start | bytes 589832 | tf_op jit(solution)/shard_map/ppermute | solution.py:585
  99.8 9.1 %copy-start.16 = (bf16[192,512]{1,0:T(8,128)(2,1)}, bf16[192,512]{1,0:T(8,128)(2,1)S(1)}, u32[]{:S(2)}) copy-start(bf16[192,512]{1,0:T(8,128)(2,1)S(1)} %collective-permute-done.6.inner_ref) | copy-start | bytes 589828
  102.3 6.6 %copy-start.17 = (bf16[192,512]{1,0:T(8,128)(2,1)}, bf16[192,512]{1,0:T(8,128)(2,1)S(1)}, u32[]{:S(2)}) copy-start(bf16[192,512]{1,0:T(8,128)(2,1)S(1)} %collective-permute-done.7.outer_ref) | copy-start | bytes 589828
  103.3 12.1 %copy-start.7 = (bf16[192,512]{1,0:T(8,128)(2,1)S(1)}, bf16[192,512]{1,0:T(8,128)(2,1)}, u32[]{:S(2)}) copy-start(bf16[192,512]{1,0:T(8,128)(2,1)} %constant.7.clone.txi_hbm) | copy-start | bytes 589828
  103.3 12.1 %all-to-all-start.7 = ((bf16[8,128,128]{2,1,0:T(8,128)(2,1)}), bf16[8,128,128]{2,1,0:T(8,128)(2,1)S(1)}, u32[]{:S(2)}, u32[]{:S(2)}) async-start(bf16[8,128,128]{2,1,0:T(8,128)(2,1)} %shard_map.122), calls=%async_computation.7 | async-start | bytes 524288 | tf_op jit(solution)/shard_map/all_to_all | solution.py:558
  115.4 1.2 %copy-start.1 = (bf16[8,128,512]{2,1,0:T(8,128)(2,1)S(1)}, bf16[8,128,512]{2,1,0:T(8,128)(2,1)}, u32[]{:S(2)}) copy-start(bf16[8,128,512]{2,1,0:T(8,128)(2,1)} %shard_map.123.conv_ref) | copy-start | bytes 3145732

commit v6 on v5

--- a/solution.py
+++ b/solution.py
@@ -416,26 +416,27 @@
     finish(fetched[5:])
     bias = jnp.zeros((128, 1), F32)
     for start in range(0, YL, 4):
-        left, right = [], []
+        left, right = ([], []), ([], [])
         for y in range(start, start + 4):
             slope = slopes[y]
             wide = slope.astype(F32)
             bias = bias + jnp.sum(wide, axis=1, keepdims=True)
-            left.append(
-                jnp.concatenate([shift_left(wide).astype(BF16), slope, shift_right(wide).astype(BF16)], 0)
-            )
-            right.append(pad[y : y + 3].reshape(576, NX))
-        part = dot_nt(jnp.concatenate(left, 1), jnp.concatenate(right, 1))
-        sums_ref[...] = part if start == 0 else sums_ref[...] + part
+            three = (shift_left(wide).astype(BF16), slope, shift_right(wide).astype(BF16))
+            for half in range(2):
+                left[half].append(jnp.concatenate([v[half * 64 : half * 64 + 64] for v in three], 0))
+                right[half].append(pad[y : y + 3, half * 64 : half * 64 + 128].reshape(384, NX))
+        for half in range(2):
+            part = dot_nt(jnp.concatenate(left[half], 1), jnp.concatenate(right[half], 1))
+            sums_ref[half] = part if start == 0 else sums_ref[half] + part
     bias32 = bias[0:32] + bias[32:64] + bias[64:96] + bias[96:128]
     pieces = []
     for dx in range(3):
         for dy in range(3):
             total = jnp.zeros((C, 96), F32)
             for z in range(ZL):
-                row = (dx * ZL + z) * C
-                col = dy * 192 + z * C
-                total = total + sums_ref[row : row + C, col : col + 96]
+                row = (dx * 2 + z % 2) * C
+                col = dy * 128 + z % 2 * C
+                total = total + sums_ref[z // 2, row : row + C, col : col + 96]
             pieces += [total[:, dz * C : dz * C + C] for dz in range(3)]
     pieces.append(jnp.broadcast_to(bias32, (C, C)))
     for g in range(GY):
@@ -655,7 +656,7 @@
         [
             vmem((GY, LINE_ROWS, 128), BF16), vmem((YL, 128, NX), BF16), vmem((YL, 128, NX), BF16), PAD,
             vmem((192, NX), BF16), vmem((64, NX), BF16), vmem((512, 128), F32), vmem((YL, 128, NX), BF16),
-            vmem((384, 576), F32), sems(10), sems(5),
+            vmem((2, 192, 384), F32), sems(10), sems(5),
         ],
         LARGE,
         recv, local, cot, own, *halo, txi, tx,

time: 121 us -> 120 us (level)
  no operation moved by 1% of the time
where the time goes in v6:
time: 120 us; the launch traced here: 119 us
  starting transfers between devices  48.3 us (40%)
  Pallas kernels  32.4 us (27%)
  blocking collectives  23.6 us (20%)
  waiting for transfers between devices  10.9 us (9%)
  local copies, waits for them, and re-layouts  2.58 us (2%)
    pallas_call x14, Pallas kernels, call(): pl.pallas_call(body, in_specs=ins, out_specs=[spec for spec, _ in outs],...  32.4 us
    all_to_all x6, starting transfers between devices, exchange(): return lax.all_to_all(blocks, axis, 0, 0, tiled=True)  30.1 us
    all_to_all x2, blocking collectives, exchange(): return lax.all_to_all(blocks, axis, 0, 0, tiled=True)  23.6 us
    all_to_all x6, waiting for transfers between devices, exchange(): return lax.all_to_all(blocks, axis, 0, 0, tiled=True)  8.43 us
    ppermute x2, starting transfers between devices, z_halos(): zlo = lax.ppermute(back, 'gz', [(i, i + 1) for i in range(GZ - 1)])  5.4 us
    ppermute x2, starting transfers between devices, y_halos(): outer = lax.ppermute(outer, 'gy', ahead + behind)  5.15 us
    ppermute x2, starting transfers between devices, y_halos(): inner = lax.ppermute(inner, 'gy', [(i, i ^ 1) for i in range(GY)])  4.95 us
    ppermute x2, starting transfers between devices, z_halos(): zhi = lax.ppermute(front, 'gz', [(i + 1, i) for i in range(GZ - 1)])  2.72 us
  transfers between devices with their start and end apart: 14, of which 6 were waited for; matrix products, arithmetic and copies ran while one was open for 0% of the time, Pallas kernels for 16%

profile of v6, /device:TPU:1, one launch (start us, length us, event | category | flops | bytes accessed | tf_op | source)
XLA Modules:
  0.0 118.9 jit_solution(15015221154091824398)
XLA Ops:
  0.6 0.0 copy-start
  0.6 0.0 copy-start.2
  0.7 3.1 %shard_map.111 = (bf16[8,128,128]{2,1,0:T(8,128)(2,1)}, bf16[8,32,512]{2,1,0:T(8,128)(2,1)}, bf16[8,32,512]{2,1,0:T(8,128)(2,1)}, bf16[128,512]{1,0:T(8,128)(2,1)}, bf16[128,512]{1,0:T(8,128)(2,1)}) custom-call(bf16[8,128,512]{2,1,0:T(8,128)(2,1)} %bitcast.9, bf16[64,512]{1,0:T(8,128)(2,1)} %constant.6.clone.tx_hbm), custom_call_target="tpu_custom_call" | custom-call | tf_op jit(solution)/shard_map/pallas_call | solution.py:548
  3.7 5.8 %all-to-all-start = ((bf16[8,128,128]{2,1,0:T(8,128)(2,1)}), bf16[8,128,128]{2,1,0:T(8,128)(2,1)S(1)}, u32[]{:S(2)}, u32[]{:S(2)}) async-start(bf16[8,128,128]{2,1,0:T(8,128)(2,1)} %get-tuple-element.39), calls=%async_computation | async-start | bytes 524288 | tf_op jit(solution)/shard_map/all_to_all | solution.py:559
  9.5 3.2 %collective-permute-start = (bf16[8,32,512]{2,1,0:T(8,128)(2,1)}, bf16[8,32,512]{2,1,0:T(8,128)(2,1)S(1)}, u32[]{:S(2)}, u32[]{:S(2)}) collective-permute-start(bf16[8,32,512]{2,1,0:T(8,128)(2,1)} %get-tuple-element.44), channel_id=1, source_target_pairs={{0,1},{1,2},{2,3},{3,4},{4,5},{5,6},{6,7},{7,8},{8,9},{9,10},{10,1... | collective-permute-start | bytes 786440 | tf_op jit(solution)/shard_map/ppermute | solution.py:574
  12.7 0.0 copy-start.10
  12.8 0.0 copy-start.11
  12.8 1.4 %collective-permute-start.1 = (bf16[8,32,512]{2,1,0:T(8,128)(2,1)}, bf16[8,32,512]{2,1,0:T(8,128)(2,1)S(1)}, u32[]{:S(2)}, u32[]{:S(2)}) collective-permute-start(bf16[8,32,512]{2,1,0:T(8,128)(2,1)} %get-tuple-element.45), channel_id=1, source_target_pairs={{1,0},{2,1},{3,2},{4,3},{5,4},{6,5},{7,6},{8,7},{9,8},{10,9},{11,1... | collective-permute-start | bytes 786440 | tf_op jit(solution)/shard_map/ppermute | solution.py:575
  14.2 1.8 %all-to-all-done.recv_ref = bf16[8,128,128]{2,1,0:T(8,128)(2,1)S(1)} async-done(((bf16[8,128,128]{2,1,0:T(8,128)(2,1)}), bf16[8,128,128]{2,1,0:T(8,128)(2,1)S(1)}, u32[]{:S(2)}, u32[]{:S(2)}) %all-to-all-start) | async-done | bytes 262176 | tf_op jit(solution)/shard_map/all_to_all | solution.py:559
  16.0 0.0 copy-done
  16.0 0.3 shard_map.112
  16.3 14.1 %all_to_all.40.recv_ref = bf16[16,16,128]{2,1,0:T(8,128)(2,1)S(1)} all-to-all(bf16[16,16,128]{2,1,0:T(8,128)(2,1)S(1)} %shard_map.112), channel_id=1, replica_groups=mesh['gy'=8,'gz'=16] {'gz'}, dimensions={0} | all-to-all | bytes 131072 | tf_op jit(solution)/shard_map/all_to_all | solution.py:559
  30.4 0.0 copy-done.2
  30.4 2.1 %shard_map.113 = (bf16[16,64,128]{2,1,0:T(8,128)(2,1)}, f32[128,128]{1,0:T(8,128)S(1)}) custom-call(bf16[16,16,128]{2,1,0:T(8,128)(2,1)S(1)} %all_to_all.40.recv_ref, bf16[64,8192]{1,0:T(8,128)(2,1)S(1)} %bitcast.7, bf16[1408,512]{1,0:T(8,128)(2,1)S(1)} %copy-done), custom_call_target="tpu_custom_call" | custom-call | tf_op jit(solution)/shard_map/pallas_call | solution.py:548
  32.5 0.6 copy-done.12
  33.1 3.5 %all-to-all-start.2 = ((bf16[16,64,128]{2,1,0:T(8,128)(2,1)}), bf16[16,64,128]{2,1,0:T(8,128)(2,1)S(1)}, u32[]{:S(2)}, u32[]{:S(2)}) async-start(bf16[16,64,128]{2,1,0:T(8,128)(2,1)} %get-tuple-element.40), calls=%async_computation.2 | async-start | bytes 524288 | tf_op jit(solution)/shard_map/all_to_all | solution.py:559
  36.7 0.0 collective-permute-done.zlo_ref
  36.7 0.0 copy-start.3
  36.7 0.0 collective-permute-done.1.zhi_ref
  36.7 0.0 copy-start.4
  36.7 0.0 copy-done.10
  36.7 0.0 copy-done.11
  36.7 0.8 shard_map.114
  37.5 2.5 %collective-permute-start.2 = (bf16[192,512]{1,0:T(8,128)(2,1)S(1)}, bf16[192,512]{1,0:T(8,128)(2,1)S(1)}, u32[]{:S(2)}, u32[]{:S(2)}) collective-permute-start(bf16[192,512]{1,0:T(8,128)(2,1)S(1)} %get-tuple-element.46), channel_id=1, source_target_pairs={{0,16},{16,0},{32,48},{48,32},{64,80},{80,64},{96,112},{112,96},{1... | collective-permute-start | bytes 589832 | tf_op jit(solution)/shard_map/ppermute | solution.py:587
  40.0 2.1 %collective-permute-start.3 = (bf16[192,512]{1,0:T(8,128)(2,1)}, bf16[192,512]{1,0:T(8,128)(2,1)}, u32[]{:S(2)}, u32[]{:S(2)}) collective-permute-start(bf16[192,512]{1,0:T(8,128)(2,1)} %get-tuple-element.50), channel_id=1, source_target_pairs={{16,32},{48,64},{80,96},{32,16},{64,48},{96,80},{17,33},{49,65},{8... | collective-permute-start | bytes 589832 | tf_op jit(solution)/shard_map/ppermute | solution.py:586
  42.1 0.0 collective-permute-done.2.inner_ref
  42.1 0.0 copy-start.14
  42.1 2.1 %all-to-all-done.2.recv_ref = bf16[16,64,128]{2,1,0:T(8,128)(2,1)S(1)} async-done(((bf16[16,64,128]{2,1,0:T(8,128)(2,1)}), bf16[16,64,128]{2,1,0:T(8,128)(2,1)S(1)}, u32[]{:S(2)}, u32[]{:S(2)}) %all-to-all-start.2) | async-done | bytes 262176 | tf_op jit(solution)/shard_map/all_to_all | solution.py:559
  44.2 1.0 shard_map.115
  45.1 6.9 %all-to-all-start.3 = ((bf16[8,64,128]{2,1,0:T(8,128)(2,1)}), bf16[8,64,128]{2,1,0:T(8,128)(2,1)S(1)}, u32[]{:S(2)}, u32[]{:S(2)}) async-start(bf16[8,64,128]{2,1,0:T(8,128)(2,1)} %shard_map.115), calls=%async_computation.3 | async-start | bytes 262144 | tf_op jit(solution)/shard_map/all_to_all | solution.py:559
  52.0 0.0 collective-permute-done.3.outer_ref
  52.0 5.1 %shard_map.116.local_ref = bf16[8,128,512]{2,1,0:T(8,128)(2,1)} custom-call(bf16[8,128,512]{2,1,0:T(8,128)(2,1)} %bitcast.10, bf16[8,32,512]{2,1,0:T(8,128)(2,1)} %copy-done.3, bf16[8,32,512]{2,1,0:T(8,128)(2,1)} %copy-done.4, bf16[192,512]{1,0:T(8,128)(2,1)} %copy-done.14, bf16[192,512]{1,0:T(8,128)(2,1)} %collective-permute-done.3.outer_ref, ...), custom_call_target="tpu_custom_call" | custom-call | tf_op jit(solution)/shard_map/pallas_call | solution.py:548
  57.2 0.2 all-to-all-done.3.recv_ref
  57.3 0.7 copy-done.15
  58.0 6.8 %shard_map.117 = (bf16[8,128,512]{2,1,0:T(8,128)(2,1)}, bf16[8,32,512]{2,1,0:T(8,128)(2,1)}, bf16[8,32,512]{2,1,0:T(8,128)(2,1)}, bf16[128,512]{1,0:T(8,128)(2,1...) custom-call(bf16[8,64,128]{2,1,0:T(8,128)(2,1)} %copy-done.15, bf16[8,128,512]{2,1,0:T(8,128)(2,1)} %shard_map.116.local_ref, ...), custom_call_target="tpu_custom_call" | custom-call | tf_op jit(solution)/shard_map/pallas_call | solution.py:548
  64.8 4.7 %all-to-all-start.4 = ((bf16[8,128,128]{2,1,0:T(8,128)(2,1)}), bf16[8,128,128]{2,1,0:T(8,128)(2,1)S(1)}, u32[]{:S(2)}, u32[]{:S(2)}) async-start(bf16[8,128,128]{2,1,0:T(8,128)(2,1)} %get-tuple-element.51), calls=%async_computation.4 | async-start | bytes 524288 | tf_op jit(solution)/shard_map/all_to_all | solution.py:559
  69.5 2.2 %collective-permute-start.4 = (bf16[8,32,512]{2,1,0:T(8,128)(2,1)}, bf16[8,32,512]{2,1,0:T(8,128)(2,1)S(1)}, u32[]{:S(2)}, u32[]{:S(2)}) collective-permute-start(bf16[8,32,512]{2,1,0:T(8,128)(2,1)} %get-tuple-element.56), channel_id=1, source_target_pairs={{0,1},{1,2},{2,3},{3,4},{4,5},{5,6},{6,7},{7,8},{8,9},{9,10},{10,1... | collective-permute-start | bytes 786440 | tf_op jit(solution)/shard_map/ppermute | solution.py:574
  71.7 1.3 %collective-permute-start.5 = (bf16[8,32,512]{2,1,0:T(8,128)(2,1)}, bf16[8,32,512]{2,1,0:T(8,128)(2,1)S(1)}, u32[]{:S(2)}, u32[]{:S(2)}) collective-permute-start(bf16[8,32,512]{2,1,0:T(8,128)(2,1)} %get-tuple-element.57), channel_id=1, source_target_pairs={{1,0},{2,1},{3,2},{4,3},{5,4},{6,5},{7,6},{8,7},{9,8},{10,9},{11,1... | collective-permute-start | bytes 786440 | tf_op jit(solution)/shard_map/ppermute | solution.py:575
  73.0 3.0 %all-to-all-done.4.recv_ref = bf16[8,128,128]{2,1,0:T(8,128)(2,1)S(1)} async-done(((bf16[8,128,128]{2,1,0:T(8,128)(2,1)}), bf16[8,128,128]{2,1,0:T(8,128)(2,1)S(1)}, u32[]{:S(2)}, u32[]{:S(2)}) %all-to-all-start.4) | async-done | bytes 262176 | tf_op jit(solution)/shard_map/all_to_all | solution.py:559
  76.0 0.3 shard_map.118
  76.3 9.5 %all_to_all.41.recv_ref = bf16[16,24,128]{2,1,0:T(8,128)(2,1)S(1)} all-to-all(bf16[16,24,128]{2,1,0:T(8,128)(2,1)S(1)} %shard_map.118), channel_id=1, replica_groups=mesh['gy'=8,'gz'=16] {'gz'}, dimensions={0} | all-to-all | bytes 196608 | tf_op jit(solution)/shard_map/all_to_all | solution.py:559
  85.8 2.5 %shard_map.119 = (bf16[16,64,128]{2,1,0:T(8,128)(2,1)}, f32[128,128]{1,0:T(8,128)S(1)}) custom-call(bf16[16,24,128]{2,1,0:T(8,128)(2,1)S(1)} %all_to_all.41.recv_ref, bf16[64,8192]{1,0:T(8,128)(2,1)S(1)} %bitcast.8, bf16[1408,512]{1,0:T(8,128)(2,1)S(1)} %copy-done), custom_call_target="tpu_custom_call" | custom-call | tf_op jit(solution)/shard_map/pallas_call | solution.py:548
  88.3 3.5 %all-to-all-start.6 = ((bf16[16,64,128]{2,1,0:T(8,128)(2,1)}), bf16[16,64,128]{2,1,0:T(8,128)(2,1)S(1)}, u32[]{:S(2)}, u32[]{:S(2)}) async-start(bf16[16,64,128]{2,1,0:T(8,128)(2,1)} %get-tuple-element.52), calls=%async_computation.6 | async-start | bytes 524288 | tf_op jit(solution)/shard_map/all_to_all | solution.py:559
  91.9 0.0 collective-permute-done.4.zlo_ref
  91.9 0.0 collective-permute-done.5.zhi_ref
  91.9 0.0 copy-start.6
  91.9 0.0 copy-done.8
  91.9 0.0 copy-done.9
  91.9 0.1 shard_map.121
  92.0 2.5 %collective-permute-start.6 = (bf16[192,512]{1,0:T(8,128)(2,1)S(1)}, bf16[192,512]{1,0:T(8,128)(2,1)S(1)}, u32[]{:S(2)}, u32[]{:S(2)}) collective-permute-start(bf16[192,512]{1,0:T(8,128)(2,1)S(1)} %get-tuple-element.61), channel_id=1, source_target_pairs={{0,16},{16,0},{32,48},{48,32},{64,80},{80,64},{96,112},{112,96},{1... | collective-permute-start | bytes 589832 | tf_op jit(solution)/shard_map/ppermute | solution.py:587
  94.5 3.1 %collective-permute-start.7 = (bf16[192,512]{1,0:T(8,128)(2,1)S(1)}, bf16[192,512]{1,0:T(8,128)(2,1)S(1)}, u32[]{:S(2)}, u32[]{:S(2)}) collective-permute-start(bf16[192,512]{1,0:T(8,128)(2,1)S(1)} %get-tuple-element.62), channel_id=1, source_target_pairs={{16,32},{48,64},{80,96},{32,16},{64,48},{96,80},{17,33},{49,65},{8... | collective-permute-start | bytes 589832 | tf_op jit(solution)/shard_map/ppermute | solution.py:586
  97.6 1.7 %shard_map.120 = f32[64,8192]{1,0:T(8,128)} custom-call(f32[128,128]{1,0:T(8,128)S(1)} %copy-done.13, f32[128,128]{1,0:T(8,128)S(1)} %get-tuple-element.55.back_ref), custom_call_target="tpu_custom_call" | custom-call | tf_op jit(solution)/shard_map/pallas_call | solution.py:548
  99.2 0.0 collective-permute-done.6.inner_ref
  99.3 0.0 copy-start.16
  99.3 2.5 %collective-permute-done.7.outer_ref = bf16[192,512]{1,0:T(8,128)(2,1)S(1)} collective-permute-done((bf16[192,512]{1,0:T(8,128)(2,1)S(1)}, bf16[192,512]{1,0:T(8,128)(2,1)S(1)}, u32[]{:S(2)}, u32[]{:S(2)}) %collective-permute-start.7) | collective-permute-done | bytes 196640 | tf_op jit(solution)/shard_map/ppermute | solution.py:586
  101.7 0.0 all-to-all-done.6.recv_ref
  101.7 1.0 shard_map.122
  102.7 5.6 %all-to-all-start.7 = ((bf16[8,128,128]{2,1,0:T(8,128)(2,1)}), bf16[8,128,128]{2,1,0:T(8,128)(2,1)S(1)}, u32[]{:S(2)}, u32[]{:S(2)}) async-start(bf16[8,128,128]{2,1,0:T(8,128)(2,1)} %shard_map.122), calls=%async_computation.7 | async-start | bytes 524288 | tf_op jit(solution)/shard_map/all_to_all | solution.py:559
  108.4 0.0 copy-done.17
  108.4 5.1 %shard_map.123.conv_ref = bf16[8,128,512]{2,1,0:T(8,128)(2,1)} custom-call(bf16[8,128,512]{2,1,0:T(8,128)(2,1)} %get-tuple-element.65.own_ref, bf16[8,32,512]{2,1,0:T(8,128)(2,1)} %copy-done.5, bf16[8,32,512]{2,1,0:T(8,128)(2,1)} %copy-done.6, bf16[192,512]{1,0:T(8,128)(2,1)} %copy-done.16, bf16[192,512]{1,0:T(8,128)(2,1)} %copy-done.17, ...), custom_call_target="tpu_custom_call" | custom-call | tf_op jit(solution)/shard_map/pallas_call | solution.py:548
  113.5 1.4 %all-to-all-done.7.recv_ref = bf16[8,128,128]{2,1,0:T(8,128)(2,1)S(1)} async-done(((bf16[8,128,128]{2,1,0:T(8,128)(2,1)}), bf16[8,128,128]{2,1,0:T(8,128)(2,1)S(1)}, u32[]{:S(2)}, u32[]{:S(2)}) %all-to-all-start.7) | async-done | bytes 262176 | tf_op jit(solution)/shard_map/all_to_all | solution.py:559
  114.9 0.0 copy-done.7
  114.9 1.2 %copy-done.1 = bf16[8,128,512]{2,1,0:T(8,128)(2,1)S(1)} copy-done((bf16[8,128,512]{2,1,0:T(8,128)(2,1)S(1)}, bf16[8,128,512]{2,1,0:T(8,128)(2,1)}, u32[]{:S(2)}) %copy-start.1) | copy-done | bytes 1048600
  116.1 2.7 %shard_map.124 = (bf16[8,128,512]{2,1,0:T(8,128)(2,1)}, f32[3,3,32,96]{3,2,1,0:T(8,128)}, f32[1,32]{1,0:T(1,128)}) custom-call(bf16[8,128,128]{2,1,0:T(8,128)(2,1)S(1)} %all-to-all-done.7.recv_ref, bf16[8,128,512]{2,1,0:T(8,128)(2,1)S(1)} %copy-done.1, bf16[192,512]{1,0:T(8,128)(2,1)S(1)} %copy-done.7), custom_call_target="tpu_custom_call" | custom-call | tf_op jit(solution)/shard_map/pallas_call | solution.py:548
  (16 shorter events, 0.0 us)
Async XLA Ops:
  0.6 15.4 %copy-start = (bf16[1408,512]{1,0:T(8,128)(2,1)S(1)}, bf16[1408,512]{1,0:T(8,128)(2,1)}, u32[]{:S(2)}) copy-start(bf16[1408,512]{1,0:T(8,128)(2,1)} %constant.8.clone.table_ref) | copy-start | bytes 4325380
  0.6 29.8 %copy-start.2 = (bf16[2,32,8192]{2,1,0:T(8,128)(2,1)S(1)}, bf16[2,32,8192]{2,1,0:T(8,128)(2,1)}, u32[]{:S(2)}) copy-start(bf16[2,32,8192]{2,1,0:T(8,128)(2,1)} %param.10) | copy-start | bytes 3145732
  3.7 12.3 %all-to-all-start = ((bf16[8,128,128]{2,1,0:T(8,128)(2,1)}), bf16[8,128,128]{2,1,0:T(8,128)(2,1)S(1)}, u32[]{:S(2)}, u32[]{:S(2)}) async-start(bf16[8,128,128]{2,1,0:T(8,128)(2,1)} %get-tuple-element.39), calls=%async_computation | async-start | bytes 524288 | tf_op jit(solution)/shard_map/all_to_all | solution.py:559
  9.5 27.1 %collective-permute-start = (bf16[8,32,512]{2,1,0:T(8,128)(2,1)}, bf16[8,32,512]{2,1,0:T(8,128)(2,1)S(1)}, u32[]{:S(2)}, u32[]{:S(2)}) collective-permute-start(bf16[8,32,512]{2,1,0:T(8,128)(2,1)} %get-tuple-element.44), channel_id=1, source_target_pairs={{0,1},{1,2},{2,3},{3,4},{4,5},{5,6},{6,7},{7,8},{8,9},{9,10},{10,1... | collective-permute-start | bytes 786440 | tf_op jit(solution)/shard_map/ppermute | solution.py:574
  12.7 24.0 %copy-start.10 = (bf16[128,512]{1,0:T(8,128)(2,1)S(1)}, bf16[128,512]{1,0:T(8,128)(2,1)}, u32[]{:S(2)}) copy-start(bf16[128,512]{1,0:T(8,128)(2,1)} %get-tuple-element.42.own_first_ref) | copy-start | bytes 393220
  12.8 24.0 %copy-start.11 = (bf16[128,512]{1,0:T(8,128)(2,1)S(1)}, bf16[128,512]{1,0:T(8,128)(2,1)}, u32[]{:S(2)}) copy-start(bf16[128,512]{1,0:T(8,128)(2,1)} %get-tuple-element.43.own_last_ref) | copy-start | bytes 393220
  12.8 23.9 %collective-permute-start.1 = (bf16[8,32,512]{2,1,0:T(8,128)(2,1)}, bf16[8,32,512]{2,1,0:T(8,128)(2,1)S(1)}, u32[]{:S(2)}, u32[]{:S(2)}) collective-permute-start(bf16[8,32,512]{2,1,0:T(8,128)(2,1)} %get-tuple-element.45), channel_id=1, source_target_pairs={{1,0},{2,1},{3,2},{4,3},{5,4},{6,5},{7,6},{8,7},{9,8},{10,9},{11,1... | collective-permute-start | bytes 786440 | tf_op jit(solution)/shard_map/ppermute | solution.py:575
  32.5 0.6 copy-start.12
  33.1 11.0 %all-to-all-start.2 = ((bf16[16,64,128]{2,1,0:T(8,128)(2,1)}), bf16[16,64,128]{2,1,0:T(8,128)(2,1)S(1)}, u32[]{:S(2)}, u32[]{:S(2)}) async-start(bf16[16,64,128]{2,1,0:T(8,128)(2,1)} %get-tuple-element.40), calls=%async_computation.2 | async-start | bytes 524288 | tf_op jit(solution)/shard_map/all_to_all | solution.py:559
  36.7 15.3 %copy-start.3 = (bf16[8,32,512]{2,1,0:T(8,128)(2,1)}, bf16[8,32,512]{2,1,0:T(8,128)(2,1)S(1)}, u32[]{:S(2)}) copy-start(bf16[8,32,512]{2,1,0:T(8,128)(2,1)S(1)} %collective-permute-done.zlo_ref) | copy-start | bytes 786436
  36.7 15.3 %copy-start.4 = (bf16[8,32,512]{2,1,0:T(8,128)(2,1)}, bf16[8,32,512]{2,1,0:T(8,128)(2,1)S(1)}, u32[]{:S(2)}) copy-start(bf16[8,32,512]{2,1,0:T(8,128)(2,1)S(1)} %collective-permute-done.1.zhi_ref) | copy-start | bytes 786436
  37.5 4.5 %collective-permute-start.2 = (bf16[192,512]{1,0:T(8,128)(2,1)S(1)}, bf16[192,512]{1,0:T(8,128)(2,1)S(1)}, u32[]{:S(2)}, u32[]{:S(2)}) collective-permute-start(bf16[192,512]{1,0:T(8,128)(2,1)S(1)} %get-tuple-element.46), channel_id=1, source_target_pairs={{0,16},{16,0},{32,48},{48,32},{64,80},{80,64},{96,112},{112,96},{1... | collective-permute-start | bytes 589832 | tf_op jit(solution)/shard_map/ppermute | solution.py:587
  40.0 12.0 %collective-permute-start.3 = (bf16[192,512]{1,0:T(8,128)(2,1)}, bf16[192,512]{1,0:T(8,128)(2,1)}, u32[]{:S(2)}, u32[]{:S(2)}) collective-permute-start(bf16[192,512]{1,0:T(8,128)(2,1)} %get-tuple-element.50), channel_id=1, source_target_pairs={{16,32},{48,64},{80,96},{32,16},{64,48},{96,80},{17,33},{49,65},{8... | collective-permute-start | bytes 589832 | tf_op jit(solution)/shard_map/ppermute | solution.py:586
  42.1 9.9 %copy-start.14 = (bf16[192,512]{1,0:T(8,128)(2,1)}, bf16[192,512]{1,0:T(8,128)(2,1)S(1)}, u32[]{:S(2)}) copy-start(bf16[192,512]{1,0:T(8,128)(2,1)S(1)} %collective-permute-done.2.inner_ref) | copy-start | bytes 589828
  45.1 12.2 %all-to-all-start.3 = ((bf16[8,64,128]{2,1,0:T(8,128)(2,1)}), bf16[8,64,128]{2,1,0:T(8,128)(2,1)S(1)}, u32[]{:S(2)}, u32[]{:S(2)}) async-start(bf16[8,64,128]{2,1,0:T(8,128)(2,1)} %shard_map.115), calls=%async_computation.3 | async-start | bytes 262144 | tf_op jit(solution)/shard_map/all_to_all | solution.py:559
  57.3 0.7 copy-start.15
  64.8 11.2 %all-to-all-start.4 = ((bf16[8,128,128]{2,1,0:T(8,128)(2,1)}), bf16[8,128,128]{2,1,0:T(8,128)(2,1)S(1)}, u32[]{:S(2)}, u32[]{:S(2)}) async-start(bf16[8,128,128]{2,1,0:T(8,128)(2,1)} %get-tuple-element.51), calls=%async_computation.4 | async-start | bytes 524288 | tf_op jit(solution)/shard_map/all_to_all | solution.py:559
  69.5 22.4 %collective-permute-start.4 = (bf16[8,32,512]{2,1,0:T(8,128)(2,1)}, bf16[8,32,512]{2,1,0:T(8,128)(2,1)S(1)}, u32[]{:S(2)}, u32[]{:S(2)}) collective-permute-start(bf16[8,32,512]{2,1,0:T(8,128)(2,1)} %get-tuple-element.56), channel_id=1, source_target_pairs={{0,1},{1,2},{2,3},{3,4},{4,5},{5,6},{6,7},{7,8},{8,9},{9,10},{10,1... | collective-permute-start | bytes 786440 | tf_op jit(solution)/shard_map/ppermute | solution.py:574
  71.7 20.2 %collective-permute-start.5 = (bf16[8,32,512]{2,1,0:T(8,128)(2,1)}, bf16[8,32,512]{2,1,0:T(8,128)(2,1)S(1)}, u32[]{:S(2)}, u32[]{:S(2)}) collective-permute-start(bf16[8,32,512]{2,1,0:T(8,128)(2,1)} %get-tuple-element.57), channel_id=1, source_target_pairs={{1,0},{2,1},{3,2},{4,3},{5,4},{6,5},{7,6},{8,7},{9,8},{10,9},{11,1... | collective-permute-start | bytes 786440 | tf_op jit(solution)/shard_map/ppermute | solution.py:575
  76.3 15.6 %copy-start.8 = (bf16[128,512]{1,0:T(8,128)(2,1)S(1)}, bf16[128,512]{1,0:T(8,128)(2,1)}, u32[]{:S(2)}) copy-start(bf16[128,512]{1,0:T(8,128)(2,1)} %get-tuple-element.59.own_first_ref) | copy-start | bytes 393220
  76.3 15.6 %copy-start.9 = (bf16[128,512]{1,0:T(8,128)(2,1)S(1)}, bf16[128,512]{1,0:T(8,128)(2,1)}, u32[]{:S(2)}) copy-start(bf16[128,512]{1,0:T(8,128)(2,1)} %get-tuple-element.60.own_last_ref) | copy-start | bytes 393220
  76.3 21.2 %copy-start.13 = (f32[128,128]{1,0:T(8,128)S(1)}, f32[128,128]{1,0:T(8,128)}, u32[]{:S(2)}) copy-start(f32[128,128]{1,0:T(8,128)} %copy-done.12) | copy-start | bytes 196612
  88.3 13.4 %all-to-all-start.6 = ((bf16[16,64,128]{2,1,0:T(8,128)(2,1)}), bf16[16,64,128]{2,1,0:T(8,128)(2,1)S(1)}, u32[]{:S(2)}, u32[]{:S(2)}) async-start(bf16[16,64,128]{2,1,0:T(8,128)(2,1)} %get-tuple-element.52), calls=%async_computation.6 | async-start | bytes 524288 | tf_op jit(solution)/shard_map/all_to_all | solution.py:559
  91.9 10.9 %copy-start.5 = (bf16[8,32,512]{2,1,0:T(8,128)(2,1)}, bf16[8,32,512]{2,1,0:T(8,128)(2,1)S(1)}, u32[]{:S(2)}) copy-start(bf16[8,32,512]{2,1,0:T(8,128)(2,1)S(1)} %collective-permute-done.4.zlo_ref) | copy-start | bytes 786436
  91.9 10.8 %copy-start.6 = (bf16[8,32,512]{2,1,0:T(8,128)(2,1)}, bf16[8,32,512]{2,1,0:T(8,128)(2,1)S(1)}, u32[]{:S(2)}) copy-start(bf16[8,32,512]{2,1,0:T(8,128)(2,1)S(1)} %collective-permute-done.5.zhi_ref) | copy-start | bytes 786436
  92.0 7.3 %collective-permute-start.6 = (bf16[192,512]{1,0:T(8,128)(2,1)S(1)}, bf16[192,512]{1,0:T(8,128)(2,1)S(1)}, u32[]{:S(2)}, u32[]{:S(2)}) collective-permute-start(bf16[192,512]{1,0:T(8,128)(2,1)S(1)} %get-tuple-element.61), channel_id=1, source_target_pairs={{0,16},{16,0},{32,48},{48,32},{64,80},{80,64},{96,112},{112,96},{1... | collective-permute-start | bytes 589832 | tf_op jit(solution)/shard_map/ppermute | solution.py:587
  94.5 7.3 %collective-permute-start.7 = (bf16[192,512]{1,0:T(8,128)(2,1)S(1)}, bf16[192,512]{1,0:T(8,128)(2,1)S(1)}, u32[]{:S(2)}, u32[]{:S(2)}) collective-permute-start(bf16[192,512]{1,0:T(8,128)(2,1)S(1)} %get-tuple-element.62), channel_id=1, source_target_pairs={{16,32},{48,64},{80,96},{32,16},{64,48},{96,80},{17,33},{49,65},{8... | collective-permute-start | bytes 589832 | tf_op jit(solution)/shard_map/ppermute | solution.py:586
  99.3 9.1 %copy-start.16 = (bf16[192,512]{1,0:T(8,128)(2,1)}, bf16[192,512]{1,0:T(8,128)(2,1)S(1)}, u32[]{:S(2)}) copy-start(bf16[192,512]{1,0:T(8,128)(2,1)S(1)} %collective-permute-done.6.inner_ref) | copy-start | bytes 589828
  101.7 6.6 %copy-start.17 = (bf16[192,512]{1,0:T(8,128)(2,1)}, bf16[192,512]{1,0:T(8,128)(2,1)S(1)}, u32[]{:S(2)}) copy-start(bf16[192,512]{1,0:T(8,128)(2,1)S(1)} %collective-permute-done.7.outer_ref) | copy-start | bytes 589828
  102.7 12.1 %copy-start.7 = (bf16[192,512]{1,0:T(8,128)(2,1)S(1)}, bf16[192,512]{1,0:T(8,128)(2,1)}, u32[]{:S(2)}) copy-start(bf16[192,512]{1,0:T(8,128)(2,1)} %constant.7.clone.txi_hbm) | copy-start | bytes 589828
  102.7 12.1 %all-to-all-start.7 = ((bf16[8,128,128]{2,1,0:T(8,128)(2,1)}), bf16[8,128,128]{2,1,0:T(8,128)(2,1)S(1)}, u32[]{:S(2)}, u32[]{:S(2)}) async-start(bf16[8,128,128]{2,1,0:T(8,128)(2,1)} %shard_map.122), calls=%async_computation.7 | async-start | bytes 524288 | tf_op jit(solution)/shard_map/all_to_all | solution.py:559
  114.9 1.2 %copy-start.1 = (bf16[8,128,512]{2,1,0:T(8,128)(2,1)S(1)}, bf16[8,128,512]{2,1,0:T(8,128)(2,1)}, u32[]{:S(2)}) copy-start(bf16[8,128,512]{2,1,0:T(8,128)(2,1)} %shard_map.123.conv_ref) | copy-start | bytes 3145732
